TPU v7x, 32 devices: a whole 2x2x4 slice. The times are simulated.
32 devices in a mesh: groups: 2 (over x), row: 16 (over z, y, core).
Axes of the slice: x: 2, y: 2, z: 4, core: 2. Of those that a mesh axis runs over, the one named last changes fastest.
Arguments:
- pair: bfloat16 [4, 128, 64, 128], P('groups', 'row'), parts along dimension 0, may hold values from -6 to 6
- cotangent: bfloat16 [4, 128, 64, 128], P('groups', 'row'), parts along dimension 0, may hold values from -6 to 6
- token_mask: int32 [256], P('groups'), parts along dimension 0, may hold values 0 or 1
- coverage: int32 [4, 1, 1], P('groups'), parts along dimension 0, may hold values 0 or 1
- w_proj: bfloat16 [4, 64, 64], replicated, may hold values from -0.75 to 0.75
- w_out: bfloat16 [2, 64, 64], replicated, may hold values from -0.75 to 0.75
- layer_norm_gains: float32 [2, 64], replicated, may hold values from 0.1 to 1.9
- ln_bias: float32 [64], replicated, may hold values from -3 to 3
Outputs:
- pair_grad: bfloat16 [4, 128, 64, 128], P('groups', 'row'), parts along dimension 0
- grad_proj: float32 [8, 64, 64], P('groups'), parts along dimension 0
- grad_out: float32 [4, 64, 64], P('groups'), parts along dimension 0
- norm_gain_gradients: float32 [6, 64], P('groups'), parts along dimension 0
There are 2 independent parts, one for each index of `groups`. A program takes and returns all parts, laid end to end along the dimension named above; an argument that names none is the same for every part. Nothing has to cross between parts.
All inputs are finite; a program needn't handle non-finite values.
Results may differ from a plain program's by a relative error of at most 0.014.
Values may be sent and summed in bfloat16 or wider, within the bound.
No kernel may reach another device: no remote copies, remote signals or barrier semaphores. Data moves between devices by JAX's collectives and lax.ppermute only.
A program may use at most 128 MiB of HBM per device.

v0:
```python
import jax
import jax.numpy as jnp
from jax import lax
from jax.sharding import PartitionSpec as P

EPS = 1e-05


def apply_layer_norm(values, reduce_dimension):
    mean = jnp.mean(values, axis=reduce_dimension, keepdims=True)
    centred = values - mean
    rstd = lax.rsqrt(jnp.mean(centred * centred, axis=reduce_dimension, keepdims=True) + EPS)
    return (centred * rstd, rstd)


def layer_norm_backward(grad, normed_values, rstd, reduce_dimension):
    mean_grad = jnp.mean(grad, axis=reduce_dimension, keepdims=True)
    mean_proj = jnp.mean(grad * normed_values, axis=reduce_dimension, keepdims=True)
    return rstd * (grad - mean_grad - normed_values * mean_proj)


def tile_mask(token_mask, coverage, row_first, count, tile):
    maskf = token_mask.astype(jnp.float32)
    row_ids = row_first + jnp.arange(count, dtype=jnp.int32)
    tiles = coverage.shape[1]
    onehot = (row_ids[:, None] // tile == jnp.arange(tiles, dtype=jnp.int32)[None, :]).astype(
        jnp.float32
    )
    row_cov = jnp.einsum("rb,tbc->trc", onehot, coverage.astype(jnp.float32))
    columns = jnp.repeat(row_cov, tile, axis=2)
    row_mask = lax.dynamic_slice_in_dim(maskf, row_first, count)
    return columns * row_mask[None, :, None] * maskf[None, None, :]


def gating_back(grad, gate_pre, value_pre, mask):
    sig = jax.nn.sigmoid(gate_pre)
    d_gate = (grad * value_pre * mask * sig * (1.0 - sig)).astype(jnp.bfloat16)
    d_value = (grad * sig * mask).astype(jnp.bfloat16)
    return [d_gate, d_value]


def per_device(pair, cotangent, token_mask, coverage, w_proj, w_out, layer_norm_gains, ln_bias):
    templ, rows, chans, width = pair.shape
    tile = width // coverage.shape[1]
    first = lax.axis_index("row") * rows
    flat = (templ * chans, rows, width)
    shape_cm = (templ, chans, rows, width)
    normed_values, rstd = apply_layer_norm(pair.astype(jnp.float32), 2)
    zn = (normed_values * layer_norm_gains[0][:, None] + ln_bias[:, None]).astype(jnp.bfloat16)
    mask_cm = tile_mask(token_mask, coverage, first, rows, tile)[:, None, :, :]

    def project(index):
        return jnp.einsum("co,trck->tork", w_proj[index], zn, preferred_element_type=jnp.float32)

    def gated(gate_pre, value_pre):
        return (jax.nn.sigmoid(gate_pre) * value_pre * mask_cm).astype(jnp.bfloat16)

    pre = [project(p) for p in range(4)]
    left = gated(pre[0], pre[1])
    right = gated(pre[2], pre[3])
    left_cols, right_cols = (
        lax.all_to_all(left.reshape(flat), "row", split_axis=0, concat_axis=1, tiled=True),
        lax.all_to_all(right.reshape(flat), "row", split_axis=0, concat_axis=1, tiled=True),
    )
    mixed_cols = jnp.einsum(
        "sik,sjk->sij", left_cols, right_cols, preferred_element_type=jnp.float32
    )
    mixed_product = (
        lax.all_to_all(
            mixed_cols.astype(jnp.bfloat16), "row", split_axis=1, concat_axis=0, tiled=True
        )
        .astype(mixed_cols.dtype)
        .reshape(shape_cm)
    )
    centred_scaled_input, input_inverse_deviation = apply_layer_norm(mixed_product, 1)
    normed_update = (centred_scaled_input * layer_norm_gains[1][:, None, None]).astype(jnp.bfloat16)
    update = jnp.einsum(
        "co,tcrj->troj", w_out[1], normed_update, preferred_element_type=jnp.float32
    )
    gate = jax.nn.sigmoid(
        jnp.einsum("co,trcj->troj", w_out[0], zn, preferred_element_type=jnp.float32)
    )
    cot = cotangent.astype(jnp.float32)
    d_gate = (cot * update * gate * (1.0 - gate)).astype(jnp.bfloat16)
    d_update = (cot * gate).astype(jnp.bfloat16)
    normed_update_gradient = jnp.einsum(
        "co,troj->tcrj", w_out[1], d_update, preferred_element_type=jnp.float32
    )
    mixed_gradient = layer_norm_backward(
        normed_update_gradient * layer_norm_gains[1][:, None, None],
        centred_scaled_input,
        input_inverse_deviation,
        1,
    ).astype(jnp.bfloat16)
    dmix_cols = lax.all_to_all(
        mixed_gradient.reshape(flat), "row", split_axis=0, concat_axis=1, tiled=True
    )
    left_grad_cols = jnp.einsum(
        "sij,sjk->sik", dmix_cols, right_cols, preferred_element_type=jnp.float32
    )
    right_grad_cols = jnp.einsum(
        "sij,sik->sjk", dmix_cols, left_cols, preferred_element_type=jnp.float32
    )
    left_back, right_back = (
        lax.all_to_all(
            left_grad_cols.astype(jnp.bfloat16), "row", split_axis=1, concat_axis=0, tiled=True
        ).astype(left_grad_cols.dtype),
        lax.all_to_all(
            right_grad_cols.astype(jnp.bfloat16), "row", split_axis=1, concat_axis=0, tiled=True
        ).astype(right_grad_cols.dtype),
    )
    d_left = left_back.reshape(shape_cm)
    d_right = right_back.reshape(shape_cm)
    grads = gating_back(d_left, pre[0], pre[1], mask_cm) + gating_back(
        d_right, pre[2], pre[3], mask_cm
    )
    local_proj = jnp.stack(
        [
            jnp.einsum("trck,tork->co", zn, grads[p], preferred_element_type=jnp.float32)
            for p in range(4)
        ]
    )
    local_out = jnp.stack(
        [
            jnp.einsum("trcj,troj->co", zn, d_gate, preferred_element_type=jnp.float32),
            jnp.einsum(
                "tcrj,troj->co", normed_update, d_update, preferred_element_type=jnp.float32
            ),
        ]
    )
    normed_input_gradient = jnp.einsum(
        "co,troj->trcj", w_out[0], d_gate, preferred_element_type=jnp.float32
    )
    for p in range(4):
        normed_input_gradient = normed_input_gradient + jnp.einsum(
            "co,tork->trck", w_proj[p], grads[p], preferred_element_type=jnp.float32
        )
    local_norms = jnp.stack(
        [
            jnp.sum(normed_input_gradient * normed_values, axis=(0, 1, 3)),
            jnp.sum(normed_input_gradient, axis=(0, 1, 3)),
            jnp.sum(normed_update_gradient * centred_scaled_input, axis=(0, 2, 3)),
        ]
    )
    pair_grad = layer_norm_backward(
        normed_input_gradient * layer_norm_gains[0][:, None], normed_values, rstd, 2
    ).astype(jnp.bfloat16)
    total_proj, total_out, total_norms = lax.psum((local_proj, local_out, local_norms), "row")
    scale = 1.0 / width
    return (pair_grad, total_proj * scale, total_out * scale, total_norms * scale)


def solution(mesh):
    return jax.shard_map(
        per_device,
        mesh=mesh,
        in_specs=(
            P("groups", "row", None, None),
            P("groups", "row", None, None),
            P("groups"),
            P("groups", None, None),
            P(),
            P(),
            P(),
            P(),
        ),
        out_specs=(
            P("groups", "row", None, None),
            P("groups", None, None),
            P("groups", None, None),
            P("groups", None),
        ),
        check_vma=False,
    )
```

profile of v0, /device:TPU:0, one launch (start us, length us, event | category | flops | bytes accessed | tf_op | source)
XLA Modules:
  0.0 206.3 jit_solution(5049841562773925767)
XLA Ops:
  8.4 1.0 convert_reduce_fusion
  13.4 1.1 multiply_convert_fusion.8
  14.5 0.9 copy.172
  15.4 7.4 %all-to-all-start = ((bf16[128,8,128]{2,1,0:T(8,128)(2,1)}), bf16[128,8,128]{2,1,0:T(8,128)(2,1)S(1)}, u32[]{:S(2)}, u32[]{:S(2)}) async-start(bf16[128,8,128]{2,1,0:T(8,128)(2,1)} %bitcast.11), calls=%async_computation | async-start | bytes 524288 | tf_op jit(solution)/shard_map/all_to_all | solution.py:62
  23.0 9.9 %all-to-all-done = bf16[128,8,128]{2,1,0:T(8,128)(2,1)S(1)} async-done(((bf16[128,8,128]{2,1,0:T(8,128)(2,1)}), bf16[128,8,128]{2,1,0:T(8,128)(2,1)S(1)}, u32[]{:S(2)}, u32[]{:S(2)}) %all-to-all-start) | async-done | bytes 262176 | tf_op jit(solution)/shard_map/all_to_all | solution.py:62
  32.8 12.8 %all_to_all.81 = bf16[128,8,128]{2,1,0:T(8,128)(2,1)S(1)} all-to-all(bf16[128,8,128]{2,1,0:T(8,128)(2,1)S(1)} %bitcast.248), channel_id=1, replica_groups=mesh['groups'=2,'row'=16] {'row'}, dimensions={0} | all-to-all | bytes 524288 | tf_op jit(solution)/shard_map/all_to_all | solution.py:63
  46.0 0.9 copy.178
  46.8 3.7 %all-to-all-start.2 = ((bf16[8,128,128]{2,0,1:T(8,128)(2,1)}), bf16[8,128,128]{2,0,1:T(8,128)(2,1)S(1)}, u32[]{:S(2)}, u32[]{:S(2)}) async-start(bf16[8,128,128]{2,0,1:T(8,128)(2,1)} %copy.178), calls=%async_computation.2 | async-start | bytes 524288 | tf_op jit(solution)/shard_map/all_to_all | solution.py:69
  50.7 0.7 mul.263
  51.4 1.1 fusion.30
  52.5 8.0 %all-to-all-done.2 = bf16[8,128,128]{2,0,1:T(8,128)(2,1)S(1)} async-done(((bf16[8,128,128]{2,0,1:T(8,128)(2,1)}), bf16[8,128,128]{2,0,1:T(8,128)(2,1)S(1)}, u32[]{:S(2)}, u32[]{:S(2)}) %all-to-all-start.2) | async-done | bytes 262176 | tf_op jit(solution)/shard_map/all_to_all | solution.py:69
  61.5 1.7 multiply_reduce_fusion
  63.4 0.9 copy.189
  64.3 3.7 %all-to-all-start.3 = ((bf16[128,8,128]{2,1,0:T(8,128)(2,1)}), bf16[128,8,128]{2,1,0:T(8,128)(2,1)S(1)}, u32[]{:S(2)}, u32[]{:S(2)}) async-start(bf16[128,8,128]{2,1,0:T(8,128)(2,1)} %bitcast.48), calls=%async_computation.3 | async-start | bytes 524288 | tf_op jit(solution)/shard_map/all_to_all | solution.py:95
  68.0 0.9 multiply_convert_fusion.6
  69.0 0.9 copy-done.5
  69.9 1.0 fusion.15
  70.9 7.0 %all-to-all-done.3 = bf16[128,8,128]{2,1,0:T(8,128)(2,1)S(1)} async-done(((bf16[128,8,128]{2,1,0:T(8,128)(2,1)}), bf16[128,8,128]{2,1,0:T(8,128)(2,1)S(1)}, u32[]{:S(2)}, u32[]{:S(2)}) %all-to-all-start.3) | async-done | bytes 262176 | tf_op jit(solution)/shard_map/all_to_all | solution.py:95
  78.2 0.9 copy.191
  79.0 3.7 %all-to-all-start.4 = ((bf16[8,128,128]{2,0,1:T(8,128)(2,1)}), bf16[8,128,128]{2,0,1:T(8,128)(2,1)S(1)}, u32[]{:S(2)}, u32[]{:S(2)}) async-start(bf16[8,128,128]{2,0,1:T(8,128)(2,1)} %copy.191), calls=%async_computation.4 | async-start | bytes 524288 | tf_op jit(solution)/shard_map/all_to_all | solution.py:105
  82.7 0.8 convolution_bitcast_fusion.5
  83.8 0.8 convolution_bitcast_fusion.4
  84.9 0.9 copy.199
  85.7 7.0 %all-to-all-done.4 = bf16[8,128,128]{2,0,1:T(8,128)(2,1)S(1)} async-done(((bf16[8,128,128]{2,0,1:T(8,128)(2,1)}), bf16[8,128,128]{2,0,1:T(8,128)(2,1)S(1)}, u32[]{:S(2)}, u32[]{:S(2)}) %all-to-all-start.4) | async-done | bytes 262176 | tf_op jit(solution)/shard_map/all_to_all | solution.py:105
  92.7 4.2 %all-to-all-start.5 = ((bf16[8,128,128]{2,0,1:T(8,128)(2,1)}), bf16[8,128,128]{2,0,1:T(8,128)(2,1)}, u32[]{:S(2)}, u32[]{:S(2)}) async-start(bf16[8,128,128]{2,0,1:T(8,128)(2,1)} %copy.199), calls=%async_computation.5 | async-start | bytes 524288 | tf_op jit(solution)/shard_map/all_to_all | solution.py:108
  98.0 9.0 %all-to-all-done.5 = bf16[8,128,128]{2,0,1:T(8,128)(2,1)} async-done(((bf16[8,128,128]{2,0,1:T(8,128)(2,1)}), bf16[8,128,128]{2,0,1:T(8,128)(2,1)}, u32[]{:S(2)}, u32[]{:S(2)}) %all-to-all-start.5) | async-done | bytes 262176 | tf_op jit(solution)/shard_map/all_to_all | solution.py:108
  107.0 1.0 convert_bitcast_fusion
  108.0 1.0 copy-done.1
  113.3 59.7 %all-reduce = (f32[2,64,64]{2,1,0:T(8,128)S(1)}, f32[3,64]{1,0:T(4,128)S(1)}) all-reduce(f32[2,64,64]{2,1,0:T(8,128)S(1)} %pad_maximum_fusion.1, f32[3,64]{1,0:T(4,128)S(1)} %pad_maximum_fusion.2), channel_id=1, replica_groups=mesh['groups'=2,'row'=16] {'row'}, use_global_device_ids=true, to_apply=%region_11.12 | all-reduce | flops 8384 | bytes 67072 | tf_op jit(solution)/shard_map/psum | solution.py:148
  173.7 0.9 fusion.27
  175.1 22.7 %all-reduce.3.cloned.1.call-done = f32[4,64,64]{2,1,0:T(8,128)} async-done(((f32[4,64,64]{2,1,0:T(8,128)}), f32[4,64,64]{2,1,0:T(8,128)}) %all-reduce.3.cloned.1.call-update) | async-done | bytes 65552 | tf_op jit(solution)/shard_map/psum | solution.py:148
  197.9 1.6 broadcast_multiply_fusion
  (111 shorter events, 14.2 us)
Async XLA Ops:
  7.2 0.7 copy-start.24
  7.2 2.2 %copy-start = (bf16[2,8,64,128]{3,2,1,0:T(8,128)(2,1)S(1)}, bf16[2,8,64,128]{3,2,1,0:T(8,128)(2,1)}, u32[]{:S(2)}) copy-start(bf16[2,8,64,128]{3,2,1,0:T(8,128)(2,1)} %param.8) | copy-start | bytes 786436
  8.4 1.2 copy-start.20
  9.5 0.7 copy-start.25
  10.2 0.8 copy-start.9
  11.9 0.7 copy-start.26
  13.4 1.1 copy-start.12
  15.4 17.4 %all-to-all-start = ((bf16[128,8,128]{2,1,0:T(8,128)(2,1)}), bf16[128,8,128]{2,1,0:T(8,128)(2,1)S(1)}, u32[]{:S(2)}, u32[]{:S(2)}) async-start(bf16[128,8,128]{2,1,0:T(8,128)(2,1)} %bitcast.11), calls=%async_computation | async-start | bytes 524288 | tf_op jit(solution)/shard_map/all_to_all | solution.py:62
  46.8 4.5 %copy-start.4 = (bf16[2,8,64,128]{3,2,1,0:T(8,128)(2,1)S(1)}, bf16[2,8,64,128]{3,2,1,0:T(8,128)(2,1)}, u32[]{:S(2)}) copy-start(bf16[2,8,64,128]{3,2,1,0:T(8,128)(2,1)} %param.9) | copy-start | bytes 786436
  46.8 13.7 %all-to-all-start.2 = ((bf16[8,128,128]{2,0,1:T(8,128)(2,1)}), bf16[8,128,128]{2,0,1:T(8,128)(2,1)S(1)}, u32[]{:S(2)}, u32[]{:S(2)}) async-start(bf16[8,128,128]{2,0,1:T(8,128)(2,1)} %copy.178), calls=%async_computation.2 | async-start | bytes 524288 | tf_op jit(solution)/shard_map/all_to_all | solution.py:69
  50.5 0.9 copy-start.14
  52.5 8.3 %copy-start.6 = (bf16[2,8,64,128]{3,2,1,0:T(8,128)(2,1)}, bf16[2,8,64,128]{3,2,1,0:T(8,128)(2,1)S(1)}, u32[]{:S(2)}) copy-start(bf16[2,8,64,128]{3,2,1,0:T(8,128)(2,1)S(1)} %get-tuple-element.25) | copy-start | bytes 786436
  60.7 2.5 %copy-start.10 = (f32[2,8,128]{2,1,0:T(8,128)}, f32[2,8,128]{2,1,0:T(8,128)S(1)}, u32[]{:S(2)}) copy-start(f32[2,8,128]{2,1,0:T(8,128)S(1)} %add_rsqrt_fusion) | copy-start | bytes 24580
  60.8 0.8 copy-start.15
  60.8 0.7 copy-start.22
  64.3 3.7 %copy-start.11 = (f32[2,8,128]{2,1,0:T(8,128)S(1)}, f32[2,8,128]{2,1,0:T(8,128)}, u32[]{:S(2)}) copy-start(f32[2,8,128]{2,1,0:T(8,128)} %copy-done.10) | copy-start | bytes 24580
  64.3 13.7 %all-to-all-start.3 = ((bf16[128,8,128]{2,1,0:T(8,128)(2,1)}), bf16[128,8,128]{2,1,0:T(8,128)(2,1)S(1)}, u32[]{:S(2)}, u32[]{:S(2)}) async-start(bf16[128,8,128]{2,1,0:T(8,128)(2,1)} %bitcast.48), calls=%async_computation.3 | async-start | bytes 524288 | tf_op jit(solution)/shard_map/all_to_all | solution.py:95
  68.0 1.1 copy-start.3
  68.9 1.0 copy-start.5
  68.9 1.0 copy-start.16
  79.0 3.7 %copy-start.2 = (bf16[2,8,64,128]{3,2,1,0:T(8,128)(2,1)S(1)}, bf16[2,8,64,128]{3,2,1,0:T(8,128)(2,1)}, u32[]{:S(2)}) copy-start(bf16[2,8,64,128]{3,2,1,0:T(8,128)(2,1)} %fusion.15) | copy-start | bytes 786436
  79.0 13.7 %all-to-all-start.4 = ((bf16[8,128,128]{2,0,1:T(8,128)(2,1)}), bf16[8,128,128]{2,0,1:T(8,128)(2,1)S(1)}, u32[]{:S(2)}, u32[]{:S(2)}) async-start(bf16[8,128,128]{2,0,1:T(8,128)(2,1)} %copy.191), calls=%async_computation.4 | async-start | bytes 524288 | tf_op jit(solution)/shard_map/all_to_all | solution.py:105
  82.7 1.0 copy-start.7
  82.7 1.0 copy-start.8
  85.7 11.3 %copy-start.18 = (f32[1,64,64]{2,1,0:T(8,128)S(1)}, f32[1,64,64]{2,1,0:T(8,128)}, u32[]{:S(2)}) copy-start(f32[1,64,64]{2,1,0:T(8,128)} %convolution_bitcast_fusion.5) | copy-start | bytes 49156
  85.7 11.3 %copy-start.19 = (f32[1,64,64]{2,1,0:T(8,128)S(1)}, f32[1,64,64]{2,1,0:T(8,128)}, u32[]{:S(2)}) copy-start(f32[1,64,64]{2,1,0:T(8,128)} %convolution_bitcast_fusion.4) | copy-start | bytes 49156
  92.7 14.3 %all-to-all-start.5 = ((bf16[8,128,128]{2,0,1:T(8,128)(2,1)}), bf16[8,128,128]{2,0,1:T(8,128)(2,1)}, u32[]{:S(2)}, u32[]{:S(2)}) async-start(bf16[8,128,128]{2,0,1:T(8,128)(2,1)} %copy.199), calls=%async_computation.5 | async-start | bytes 524288 | tf_op jit(solution)/shard_map/all_to_all | solution.py:108
  96.9 0.8 copy-start.17
  96.9 100.9 %all-reduce.3.cloned.1.call-start = ((), (), s32[]{:S(2)}) async-start(), calls=%async_computation.6 | async-start | bytes 262144 | tf_op jit(solution)/shard_map/psum | solution.py:148
  108.0 1.0 copy-start.1
  108.0 1.0 copy-start.13
  110.8 0.7 copy-start.21
  (2 other events, 1.3 us)
Sparse Core Ops, SparseCore 0:
  112.7 85.1 all-reduce.2
where the time goes:
time: 208 us; the launch traced here: 206 us
  blocking collectives  72.5 us (35%)
  waiting for transfers between devices  63.6 us (31%)
  starting transfers between devices  22.6 us (11%)
  between operations  14.6 us (7%)
  local copies, waits for them, and re-layouts  14 us (7%)
  matrix products  10.2 us (5%)
  other arithmetic  8.72 us (4%)
    psum x1, blocking collectives, per_device(): lax.psum((local_proj, local_out, local_norms), 'row')  59.7 us
    psum x1, waiting for transfers between devices, per_device(): lax.psum((local_proj, local_out, local_norms), 'row')  22.7 us
    all_to_all x1, blocking collectives, per_device(): lax.all_to_all(right.reshape(flat), 'row', split_axis=0, concat_axis=1, t...  12.8 us
    all_to_all x1, waiting for transfers between devices, per_device(): lax.all_to_all(left.reshape(flat), 'row', split_axis=0, concat_axis=1, ti...  9.87 us
    all_to_all x1, waiting for transfers between devices, per_device(): lax.all_to_all(right_grad_cols.astype(jnp.bfloat16), 'row', split_axis=1,...  8.98 us
    all_to_all x1, waiting for transfers between devices, per_device(): lax.all_to_all(mixed_cols.astype(jnp.bfloat16), 'row', split_axis=1, conc...  8.03 us
    unnamed x56, local copies, waits for them, and re-layouts  7.82 us
    all_to_all x1, starting transfers between devices, per_device(): lax.all_to_all(left.reshape(flat), 'row', split_axis=0, concat_axis=1, ti...  7.38 us
  transfers between devices with their start and end apart: 6, of which 6 were waited for; matrix products, arithmetic and copies ran while one was open for 5% of the time, Pallas kernels for 0%

commit v1 on v0

v1 whole, which is shorter than its diff:
```python
import functools

import jax
import jax.numpy as jnp
from jax import lax
from jax.experimental import pallas as pl
from jax.experimental.pallas import tpu as pltpu
from jax.sharding import PartitionSpec as P

EPS = 1e-05
LANES = 128
PACK_ROWS = 256
F32 = jnp.float32
BF16 = jnp.bfloat16


def dot(a, b):
    return jnp.dot(a, b, preferred_element_type=F32)


def dot_nt(a, b):
    return lax.dot_general(a, b, (((1,), (1,)), ((), ())), preferred_element_type=F32)


def dot_tn(a, b):
    return lax.dot_general(a, b, (((0,), (0,)), ((), ())), preferred_element_type=F32)


def transposed(weight):
    return weight.astype(F32).T.astype(BF16)


def column(row):
    n = row.shape[1]
    eye = lax.broadcasted_iota(jnp.int32, (n, n), 0) == lax.broadcasted_iota(jnp.int32, (n, n), 1)
    return jnp.sum(jnp.where(eye, row, 0.0), axis=1, keepdims=True)


def as_row(col):
    n = col.shape[0]
    eye = lax.broadcasted_iota(jnp.int32, (n, n), 0) == lax.broadcasted_iota(jnp.int32, (n, n), 1)
    return jnp.sum(jnp.where(eye, col, 0.0), axis=0, keepdims=True)


def layer_norm(x):
    mean = jnp.mean(x, axis=0, keepdims=True)
    centred = x - mean
    rstd = lax.rsqrt(jnp.mean(centred * centred, axis=0, keepdims=True) + EPS)
    return centred * rstd, rstd


def mask_rows(first_ref, tokens_ref, cover_ref, column_mask, templ, rows):
    width, tiles = tokens_ref.shape[0], cover_ref.shape[1]
    tile = width // tiles
    block = pl.program_id(0) * LANES // tile
    out = []
    for t in range(templ):
        for r in range(rows):
            i = first_ref[0] + r
            scalar = tokens_ref[i] * cover_ref[t, i // tile, block]
            out.append(column_mask * scalar.astype(F32))
    return out


def project_kernel(templ, rows, first_ref, tokens_ref, cover_ref, pair_ref, tok_ref, w_ref, gains_ref, bias_ref, lr_ref, zn_ref, left_scr, right_scr):
    count, chans = templ * rows, pair_ref.shape[1]
    gain, bias = column(gains_ref[0:1, :]), column(bias_ref[...])
    masks = mask_rows(first_ref, tokens_ref, cover_ref, tok_ref[...].astype(F32), templ, rows)
    weights = jnp.concatenate([transposed(w_ref[p]) for p in range(4)], axis=0)
    for pos in range(0, count, 2):
        zn = []
        for q in (pos, pos + 1):
            normed, _ = layer_norm(pair_ref[q].astype(F32))
            zn.append((normed * gain + bias).astype(BF16))
        zn = jnp.concatenate(zn, axis=1)
        zn_ref[0, :, pos * LANES:(pos + 2) * LANES] = zn
        pre = dot(weights, zn)
        for j in range(2):
            part = pre[:, j * LANES:(j + 1) * LANES]
            pre_p = [part[p * chans:(p + 1) * chans] for p in range(4)]
            mask = masks[pos + j]
            where = pl.ds(pos + j, chans, stride=count)
            left_scr[where, :] = jax.nn.sigmoid(pre_p[0]) * pre_p[1] * mask
            right_scr[where, :] = jax.nn.sigmoid(pre_p[2]) * pre_p[3] * mask
    groups, _, per, _, _ = lr_ref.shape
    lr_ref[:, 0] = left_scr[...].astype(BF16).reshape(groups, per, count, LANES)
    lr_ref[:, 1] = right_scr[...].astype(BF16).reshape(groups, per, count, LANES)


def prepare_kernel(templ, rows, first_ref, tokens_ref, cover_ref, pair_ref, cot_ref, zn_ref, tok_ref, w_ref, wo_ref, fac_ref, cg_ref, du_ref, normed_ref, rstd_ref, dout_ref, scr):
    count, chans = templ * rows, pair_ref.shape[1]
    masks = mask_rows(first_ref, tokens_ref, cover_ref, tok_ref[...].astype(F32), templ, rows)
    weights = jnp.concatenate([transposed(w_ref[p]) for p in range(4)] + [transposed(wo_ref[0])], axis=0)
    w_back = wo_ref[1]
    for pos in range(0, count, 2):
        span = slice(pos * LANES, (pos + 2) * LANES)
        pre = dot(weights, zn_ref[0, :, span])
        mask = jnp.concatenate([masks[pos], masks[pos + 1]], axis=1)
        pre_p = [pre[p * chans:(p + 1) * chans] for p in range(5)]
        for p in (0, 2):
            sig = jax.nn.sigmoid(pre_p[p])
            sm = sig * mask
            fac_ref[0, p * chans:(p + 1) * chans, span] = sm * pre_p[p + 1] * (1.0 - sig)
            fac_ref[0, (p + 1) * chans:(p + 2) * chans, span] = sm
        gate = jax.nn.sigmoid(pre_p[4])
        cot = jnp.concatenate([cot_ref[pos], cot_ref[pos + 1]], axis=1).astype(F32)
        d_update = cot * gate
        cg_ref[0, :, span] = d_update * (1.0 - gate)
        d_update = d_update.astype(BF16)
        du_ref[0, :, span] = d_update
        d_outn = dot(w_back, d_update)
        for j in range(2):
            scr[pl.ds(pos + j, chans, stride=count), :] = d_outn[:, j * LANES:(j + 1) * LANES]
            normed, rstd = layer_norm(pair_ref[pos + j].astype(F32))
            lanes = slice((pos + j) * LANES, (pos + j + 1) * LANES)
            normed_ref[0, :, lanes] = normed
            rstd_ref[0, :, lanes] = rstd
    dout_ref[...] = scr[...].reshape(chans, count, LANES)


def mixed_kernel(rows, cols_ref, mixed_ref, left_ref, right_ref):
    n, _, per, count, width = cols_ref.shape
    templ = count // rows
    for c in range(per):
        left_all = cols_ref[:, 0, c].astype(F32)
        right_all = cols_ref[:, 1, c].astype(F32)
        parts = []
        for t in range(templ):
            left = left_all[:, t * rows:(t + 1) * rows].reshape(n * rows, width).astype(BF16)
            right = right_all[:, t * rows:(t + 1) * rows].reshape(n * rows, width).astype(BF16)
            left_ref[c * templ + t] = left
            right_ref[c * templ + t] = right
            parts.append(dot_nt(left, right).reshape(n, rows, width))
        mixed_ref[:, c] = jnp.concatenate(parts, axis=1).astype(BF16)


def triangle_back_kernel(rows, dmix_ref, left_ref, right_ref, out_ref):
    n, per, count, width = dmix_ref.shape
    templ = count // rows
    for c in range(per):
        dmix_all = dmix_ref[:, c].astype(F32)
        left_parts, right_parts = [], []
        for t in range(templ):
            dmix = dmix_all[:, t * rows:(t + 1) * rows].reshape(n * rows, width).astype(BF16)
            left_parts.append(dot(dmix, right_ref[c * templ + t]).reshape(n, rows, width))
            right_parts.append(dot_tn(dmix, left_ref[c * templ + t]).reshape(n, rows, width))
        out_ref[:, 0, c] = jnp.concatenate(left_parts, axis=1).astype(BF16)
        out_ref[:, 1, c] = jnp.concatenate(right_parts, axis=1).astype(BF16)


def tree_sum(parts):
    while len(parts) > 1:
        parts = [a + b for a, b in zip(parts[::2], parts[1::2])] + parts[len(parts) // 2 * 2:]
    return parts[0]


def channel_sum(chans, value):
    accs = [None] * 4
    for c in range(chans):
        v = value(c)
        accs[c % 4] = v if accs[c % 4] is None else accs[c % 4] + v
    return tree_sum([a for a in accs if a is not None])


def mixed_norm_back_kernel(gains_ref, mixed_ref, dout_ref, dmix_ref):
    chans = mixed_ref.shape[0]
    inv = 1.0 / chans
    mean = channel_sum(chans, lambda c: mixed_ref[c].astype(F32)) * inv
    mean_h = channel_sum(chans, lambda c: dout_ref[c] * gains_ref[1, c]) * inv

    def squares(c):
        centred = mixed_ref[c].astype(F32) - mean
        return centred * centred

    rstd = lax.rsqrt(channel_sum(chans, squares) * inv + EPS)

    def products(c):
        return dout_ref[c] * gains_ref[1, c] * ((mixed_ref[c].astype(F32) - mean) * rstd)

    mean_p = channel_sum(chans, products) * inv
    for c in range(chans):
        xhat = (mixed_ref[c].astype(F32) - mean) * rstd
        dmix_ref[c] = (rstd * (dout_ref[c] * gains_ref[1, c] - mean_h - xhat * mean_p)).astype(BF16)


def update_kernel(gains_ref, mixed_ref, dout_ref, zn_ref, cg_ref, du_ref, wo_ref, dgate_ref, grads_ref, scr, norm_scr, outn_scr):
    chans, count, _ = mixed_ref.shape
    inv = 1.0 / chans
    mean = channel_sum(chans, lambda c: mixed_ref[c].astype(F32)) * inv

    def squares(c):
        centred = mixed_ref[c].astype(F32) - mean
        return centred * centred

    rstd = lax.rsqrt(channel_sum(chans, squares) * inv + EPS)
    for c in range(chans):
        xhat = (mixed_ref[c].astype(F32) - mean) * rstd
        scr[c * count:(c + 1) * count, :] = xhat * gains_ref[1, c]
        norm_scr[c:c + 1, :] = jnp.sum(dout_ref[c] * xhat, axis=0, keepdims=True)
    w_update = transposed(wo_ref[1])
    for pos in range(count):
        span = slice(pos * LANES, (pos + 1) * LANES)
        outn_scr[:, span] = scr[pl.ds(pos, chans, stride=count), :].astype(BF16)
    update = dot(w_update, outn_scr[...])
    d_gate = (cg_ref[0] * update).astype(BF16)
    dgate_ref[0] = d_gate
    gate_grad = dot_nt(zn_ref[0], d_gate)
    out_grad = dot_nt(outn_scr[...], du_ref[0])
    norm = as_row(jnp.sum(norm_scr[...], axis=1, keepdims=True))

    @pl.when(pl.program_id(0) == 0)
    def _():
        grads_ref[...] = jnp.zeros_like(grads_ref)

    grads_ref[0:chans, 0:chans] += gate_grad
    grads_ref[0:chans, chans:2 * chans] += out_grad
    grads_ref[chans:chans + 1, 0:chans] += norm


def gating_back_kernel(dlr_ref, fac_ref, zn_ref, dgate_ref, normed_ref, w_ref, wo_ref, pre_grads_ref, dzn_ref, pack_ref, left_scr, right_scr, d_scr):
    groups, _, per, count, _ = dlr_ref.shape
    chans = groups * per
    left_scr[...] = dlr_ref[:, 0].astype(F32).reshape(chans * count, LANES)
    right_scr[...] = dlr_ref[:, 1].astype(F32).reshape(chans * count, LANES)
    d_scr[4 * chans:5 * chans, :] = dgate_ref[0]
    for pos in range(count):
        span = slice(pos * LANES, (pos + 1) * LANES)
        where = pl.ds(pos, chans, stride=count)
        d_left, d_right = left_scr[where, :], right_scr[where, :]
        for p in range(4):
            d = d_left if p < 2 else d_right
            d_scr[p * chans:(p + 1) * chans, span] = (d * fac_ref[0, p * chans:(p + 1) * chans, span]).astype(BF16)
    weights = jnp.concatenate([w_ref[0], w_ref[1], w_ref[2], w_ref[3], wo_ref[0]], axis=1)
    d_zn = dot(weights, d_scr[...])
    dzn_ref[0] = d_zn
    grads = dot_nt(zn_ref[0], d_scr[0:4 * chans, :])
    bias_grad = as_row(jnp.sum(d_zn, axis=1, keepdims=True))
    gain_grad = as_row(jnp.sum(d_zn * normed_ref[0], axis=1, keepdims=True))

    @pl.when(pl.program_id(0) == 0)
    def _():
        pack_ref[...] = jnp.zeros_like(pack_ref)
        pack_ref[2 * chans:3 * chans, :] = pre_grads_ref[0:chans, :]
        pack_ref[3 * chans:3 * chans + 1, :] = pre_grads_ref[chans:chans + 1, :]

    pack_ref[0:chans, :] += grads[:, 0:2 * chans]
    pack_ref[chans:2 * chans, :] += grads[:, 2 * chans:4 * chans]
    pack_ref[3 * chans + 1:3 * chans + 2, 0:chans] += gain_grad
    pack_ref[3 * chans + 2:3 * chans + 3, 0:chans] += bias_grad


def pair_grad_kernel(dzn_ref, normed_ref, rstd_ref, gains_ref, out_ref):
    gain = column(gains_ref[0:1, :])
    for pos in range(out_ref.shape[0]):
        span = slice(pos * LANES, (pos + 1) * LANES)
        h = dzn_ref[0, :, span] * gain
        normed = normed_ref[0, :, span]
        mean_h = jnp.mean(h, axis=0, keepdims=True)
        mean_p = jnp.mean(h * normed, axis=0, keepdims=True)
        out_ref[pos] = (rstd_ref[0, :, span] * (h - mean_h - normed * mean_p)).astype(BF16)


def unpack_kernel(scale, pack_ref, proj_ref, out_ref, norm_ref):
    chans = proj_ref.shape[1]
    for p in range(4):
        proj_ref[p] = pack_ref[(p // 2) * chans:(p // 2 + 1) * chans, (p % 2) * chans:(p % 2 + 1) * chans] * scale
    for p in range(2):
        out_ref[p] = pack_ref[2 * chans:3 * chans, p * chans:(p + 1) * chans] * scale
    for row, place in ((0, 1), (1, 2), (2, 0)):
        norm_ref[row:row + 1, :] = pack_ref[3 * chans + place:3 * chans + place + 1, 0:chans] * scale


def exchange(x):
    return lax.all_to_all(x, "row", split_axis=0, concat_axis=0, tiled=True)


def full(shape):
    return pl.BlockSpec(shape, lambda b: (0,) * len(shape))


SMEM = pl.BlockSpec(memory_space=pltpu.SMEM)


def params():
    return pltpu.CompilerParams(vmem_limit_bytes=40 * 1024 * 1024)


def per_device(n, pair, cotangent, token_mask, coverage, w_proj, w_out, layer_norm_gains, ln_bias):
    templ, rows, chans, width = pair.shape
    count = templ * rows
    blocks = width // LANES
    direct = chans % n == 0
    groups = n if direct else chans
    per = chans // groups
    lanes = count * LANES
    first = (lax.axis_index("row") * rows).astype(jnp.int32).reshape(1)
    pair_rows = pair.reshape(count, chans, width)
    cot_rows = cotangent.reshape(count, chans, width)
    tokens_row = token_mask.reshape(1, width)
    bias_row = ln_bias.reshape(1, chans)

    rows_spec = pl.BlockSpec((count, chans, LANES), lambda b: (0, 0, b))
    tok_spec = pl.BlockSpec((1, LANES), lambda b: (0, b))
    lr_spec = pl.BlockSpec((groups, 2, per, count, LANES), lambda b: (0, 0, 0, 0, b))
    cat_spec = pl.BlockSpec((1, chans, lanes), lambda b: (b, 0, 0))
    fac_spec = pl.BlockSpec((1, 4 * chans, lanes), lambda b: (b, 0, 0))
    one_spec = pl.BlockSpec((1, 1, lanes), lambda b: (b, 0, 0))
    chan_spec = pl.BlockSpec((chans, count, LANES), lambda b: (0, 0, b))
    w_spec, wo_spec, gains_spec = full(w_proj.shape), full(w_out.shape), full(layer_norm_gains.shape)
    scratch = pltpu.VMEM((chans * count, LANES), F32)
    cat = lambda dtype: jax.ShapeDtypeStruct((blocks, chans, lanes), dtype)
    by_chan = lambda dtype: jax.ShapeDtypeStruct((chans, count, width), dtype)

    lr, zn = pl.pallas_call(
        functools.partial(project_kernel, templ, rows),
        grid=(blocks,),
        in_specs=[SMEM, SMEM, SMEM, rows_spec, tok_spec, w_spec, gains_spec, full(bias_row.shape)],
        out_specs=[lr_spec, cat_spec],
        out_shape=[jax.ShapeDtypeStruct((groups, 2, per, count, width), BF16), cat(BF16)],
        scratch_shapes=[scratch, scratch],
        compiler_params=params(),
        name="project",
    )(first, token_mask, coverage, pair_rows, tokens_row, w_proj, layer_norm_gains, bias_row)

    fac, cg, d_update, normed, rstd, d_outn = pl.pallas_call(
        functools.partial(prepare_kernel, templ, rows),
        grid=(blocks,),
        in_specs=[SMEM, SMEM, SMEM, rows_spec, rows_spec, cat_spec, tok_spec, w_spec, wo_spec],
        out_specs=[fac_spec, cat_spec, cat_spec, cat_spec, one_spec, chan_spec],
        out_shape=[
            jax.ShapeDtypeStruct((blocks, 4 * chans, lanes), F32),
            cat(F32),
            cat(BF16),
            cat(F32),
            jax.ShapeDtypeStruct((blocks, 1, lanes), F32),
            by_chan(F32),
        ],
        scratch_shapes=[scratch],
        compiler_params=params(),
        name="prepare",
    )(first, token_mask, coverage, pair_rows, cot_rows, zn, tokens_row, w_proj, w_out)

    if direct:
        cols = exchange(lr)
        mixed, left_cols, right_cols = pl.pallas_call(
            functools.partial(mixed_kernel, rows),
            out_shape=[
                jax.ShapeDtypeStruct((n, per, count, width), BF16),
                jax.ShapeDtypeStruct((per * templ, width, width), BF16),
                jax.ShapeDtypeStruct((per * templ, width, width), BF16),
            ],
            compiler_params=params(),
            name="mixed",
        )(cols)
        mixed_rows = exchange(mixed).reshape(chans, count, width)
    else:
        slices = chans * templ // n
        cols = lr.reshape(chans, 2, templ, rows, width).transpose(0, 2, 1, 3, 4)
        cols = exchange(cols.reshape(n * slices, 2, rows, width)).reshape(n, slices, 2, rows, width)
        left_cols, right_cols = cols.transpose(2, 1, 0, 3, 4).reshape(2, slices, width, width)
        mixed = jnp.einsum("sik,sjk->sij", left_cols, right_cols, preferred_element_type=F32)
        mixed = mixed.astype(BF16).reshape(slices, n, rows, width).transpose(1, 0, 2, 3)
        mixed_rows = exchange(mixed.reshape(n * slices, rows, width)).reshape(chans, count, width)

    d_mixed = pl.pallas_call(
        mixed_norm_back_kernel,
        grid=(blocks,),
        in_specs=[SMEM, chan_spec, chan_spec],
        out_specs=chan_spec,
        out_shape=by_chan(BF16),
        compiler_params=params(),
        name="mixed_norm_back",
    )(layer_norm_gains, mixed_rows, d_outn)

    d_gate, out_grads = pl.pallas_call(
        update_kernel,
        grid=(blocks,),
        in_specs=[SMEM, chan_spec, chan_spec, cat_spec, cat_spec, cat_spec, wo_spec],
        out_specs=[cat_spec, full((chans + 8, 2 * chans))],
        out_shape=[cat(BF16), jax.ShapeDtypeStruct((chans + 8, 2 * chans), F32)],
        scratch_shapes=[scratch, pltpu.VMEM((chans, LANES), F32), pltpu.VMEM((chans, lanes), BF16)],
        compiler_params=params(),
        name="update",
    )(layer_norm_gains, mixed_rows, d_outn, zn, cg, d_update, w_out)

    if direct:
        dmix_cols = exchange(d_mixed.reshape(n, per, count, width))
        d_lr = pl.pallas_call(
            functools.partial(triangle_back_kernel, rows),
            out_shape=jax.ShapeDtypeStruct((n, 2, per, count, width), BF16),
            compiler_params=params(),
            name="triangle_back",
        )(dmix_cols, left_cols, right_cols)
        d_lr = exchange(d_lr)
    else:
        dmix_cols = exchange(d_mixed.reshape(n * slices, rows, width)).reshape(n, slices, rows, width)
        dmix_cols = dmix_cols.transpose(1, 0, 2, 3).reshape(slices, width, width)
        d_left = jnp.einsum("sij,sjk->sik", dmix_cols, right_cols, preferred_element_type=F32)
        d_right = jnp.einsum("sij,sik->sjk", dmix_cols, left_cols, preferred_element_type=F32)
        d_lr = jnp.stack([d_left.astype(BF16), d_right.astype(BF16)]).reshape(2, slices, n, rows, width)
        d_lr = exchange(d_lr.transpose(2, 1, 0, 3, 4).reshape(n * slices, 2, rows, width))
        d_lr = d_lr.reshape(chans, templ, 2, rows, width).transpose(0, 2, 1, 3, 4)
        d_lr = d_lr.reshape(groups, 2, per, count, width)

    d_zn, pack = pl.pallas_call(
        gating_back_kernel,
        grid=(blocks,),
        in_specs=[lr_spec, fac_spec, cat_spec, cat_spec, cat_spec, w_spec, wo_spec, full((chans + 8, 2 * chans))],
        out_specs=[cat_spec, full((PACK_ROWS, 2 * chans))],
        out_shape=[cat(F32), jax.ShapeDtypeStruct((PACK_ROWS, 2 * chans), F32)],
        scratch_shapes=[scratch, scratch, pltpu.VMEM((5 * chans, lanes), BF16)],
        compiler_params=params(),
        name="gating_back",
    )(d_lr, fac, zn, d_gate, normed, w_proj, w_out, out_grads)

    pair_grad = pl.pallas_call(
        pair_grad_kernel,
        grid=(blocks,),
        in_specs=[cat_spec, cat_spec, one_spec, gains_spec],
        out_specs=rows_spec,
        out_shape=jax.ShapeDtypeStruct((count, chans, width), BF16),
        compiler_params=params(),
        name="pair_grad",
    )(d_zn, normed, rstd, layer_norm_gains)

    share = PACK_ROWS // n
    mine = exchange(pack).reshape(n, share, 2 * chans).sum(axis=0)
    total = exchange(jnp.broadcast_to(mine[None], (n, share, 2 * chans)).reshape(PACK_ROWS, 2 * chans))
    grad_proj, grad_out, norm_grads = pl.pallas_call(
        functools.partial(unpack_kernel, 1.0 / width),
        out_shape=[
            jax.ShapeDtypeStruct(w_proj.shape, F32),
            jax.ShapeDtypeStruct(w_out.shape, F32),
            jax.ShapeDtypeStruct((3, chans), F32),
        ],
        name="unpack",
    )(total)
    return pair_grad.reshape(pair.shape), grad_proj, grad_out, norm_grads


def solution(mesh):
    return jax.shard_map(
        functools.partial(per_device, mesh.shape["row"]),
        mesh=mesh,
        in_specs=(
            P("groups", "row", None, None),
            P("groups", "row", None, None),
            P("groups"),
            P("groups", None, None),
            P(),
            P(),
            P(),
            P(),
        ),
        out_specs=(
            P("groups", "row", None, None),
            P("groups", None, None),
            P("groups", None, None),
            P("groups", None),
        ),
        check_vma=False,
    )
```

time: 208 us -> 111 us (0.53)
  waiting for transfers between devices: 63.6 us -> 22.4 us
  blocking collectives: 72.5 us -> 46.2 us
  between operations: 14.6 us -> 0.84 us
  Pallas kernels: 0 us -> 12.5 us
  starting transfers between devices: 22.6 us -> 11.8 us
  matrix products: 10.2 us -> 0 us
  other arithmetic: 8.72 us -> 0.02 us
  local copies, waits for them, and re-layouts: 14 us -> 16.2 us
    psum x1 -> x0, blocking collectives: 59.7 us -> none  [per_device(): lax.psum((local_proj, local_out, local_norms), 'row')]
    all_to_all x1 -> x3, blocking collectives: 12.8 us -> 46.2 us  [exchange(): return lax.all_to_all(x, 'row', split_axis=0, concat_axis=0, tiled=True)]
    psum x1 -> x0, waiting for transfers between devices: 22.7 us -> none  [per_device(): lax.psum((local_proj, local_out, local_norms), 'row')]
    all_to_all x5 -> x3, waiting for transfers between devices: 40.9 us -> 22.4 us  [exchange(): return lax.all_to_all(x, 'row', split_axis=0, concat_axis=0, tiled=True)]
    pallas_call x0 -> x9, Pallas kernels: none -> 12.5 us  [the longest x1 2.59 us: per_device(): pl.pallas_call(functools.partial(prepare_kernel, templ, rows), grid=(bloc...]
    all_to_all x5 -> x3, starting transfers between devices: 22.6 us -> 11.8 us  [exchange(): return lax.all_to_all(x, 'row', split_axis=0, concat_axis=0, tiled=True)]
    dot_general x21 -> x0, matrix products: 10.2 us -> none  [the longest x4 1.96 us: project(): jnp.einsum('co,trck->tork', w_proj[index], zn, preferred_element_type=jnp...]
    unnamed x56 -> x53, local copies, waits for them, and re-layouts: 7.82 us -> 15.5 us
  transfers between devices with their start and end apart: 6 -> 3, of which waited for: 6 -> 3; matrix products, arithmetic and copies ran while one was open for 5% -> 0% of each run, Pallas kernels for 0% -> 5%
where the time goes in v1:
time: 111 us; the launch traced here: 110 us
  blocking collectives  46.2 us (42%)
  waiting for transfers between devices  22.4 us (20%)
  local copies, waits for them, and re-layouts  16.2 us (15%)
  Pallas kernels  12.5 us (11%)
  starting transfers between devices  11.8 us (11%)
    all_to_all x3, blocking collectives, exchange(): return lax.all_to_all(x, 'row', split_axis=0, concat_axis=0, tiled=True)  46.2 us
    all_to_all x3, waiting for transfers between devices, exchange(): return lax.all_to_all(x, 'row', split_axis=0, concat_axis=0, tiled=True)  22.4 us
    unnamed x53, local copies, waits for them, and re-layouts  15.5 us
    all_to_all x3, starting transfers between devices, exchange(): return lax.all_to_all(x, 'row', split_axis=0, concat_axis=0, tiled=True)  11.8 us
    pallas_call x1, Pallas kernels, per_device(): pl.pallas_call(functools.partial(prepare_kernel, templ, rows), grid=(bloc...  2.59 us
    pallas_call x1, Pallas kernels, per_device(): pl.pallas_call(gating_back_kernel, grid=(blocks,), in_specs=[lr_spec, fac...  2.3 us
  transfers between devices with their start and end apart: 3, of which 3 were waited for; matrix products, arithmetic and copies ran while one was open for 0% of the time, Pallas kernels for 5%

profile of v1, /device:TPU:0, one launch (start us, length us, event | category | flops | bytes accessed | tf_op | source)
XLA Modules:
  0.0 110.0 jit_solution(704246300407631545)
XLA Ops:
  0.7 0.7 copy.12.cover_ref
  1.4 0.9 copy-done.4
  2.4 0.8 copy-done.6
  5.2 1.3 %project.1 = (bf16[16,2,4,16,128]{4,3,2,1,0:T(8,128)(2,1)S(1)}, bf16[1,64,2048]{2,1,0:T(8,128)(2,1)S(1)}) custom-call(s32[1]{0:T(128)} %bitcast.first_ref, s32[128]{0:T(128)S(1)} %copy-done.22, s32[2,1,1]{2,1,0:T(1,128)S(1)} %copy.12.cover_ref, bf16[16,64,128]{2,1,0:T(8,128)(2,1)S(1)} %bitcast.12, s32[1,128]{1,0:T(1,128)S(1)} %bitcast.17, ...), custom_call_target="tpu_custom_call" | custom-call | tf_op jit(solution)/shard_map/project/pallas_call | solution.py:314
  6.5 21.6 %all_to_all.37.cols_ref = bf16[16,2,4,16,128]{4,3,2,1,0:T(8,128)(2,1)S(1)} all-to-all(bf16[16,2,4,16,128]{4,3,2,1,0:T(8,128)(2,1)S(1)} %get-tuple-element.22), channel_id=1, replica_groups=mesh['groups'=2,'row'=16] {'row'}, dimensions={0} | all-to-all | bytes 1048576 | tf_op jit(solution)/shard_map/all_to_all | solution.py:274
  28.2 1.0 mixed.1
  29.2 0.7 copy-done.14
  29.9 4.1 %all-to-all-start.1 = ((bf16[16,4,16,128]{3,2,1,0:T(8,128)(2,1)}), bf16[16,4,16,128]{3,2,1,0:T(8,128)(2,1)S(1)}, u32[]{:S(2)}, u32[]{:S(2)}) async-start(bf16[16,4,16,128]{3,2,1,0:T(8,128)(2,1)} %get-tuple-element.23), calls=%async_computation.1 | async-start | bytes 524288 | tf_op jit(solution)/shard_map/all_to_all | solution.py:274
  34.1 0.9 copy-done.11
  35.0 2.6 %prepare.1 = (f32[1,256,2048]{2,1,0:T(8,128)S(1)}, f32[1,64,2048]{2,1,0:T(8,128)S(1)}, bf16[1,64,2048]{2,1,0:T(8,128)(2,1)S(1)}, f32[1,64,2048]{2,1,0:T(8,128)S(...) custom-call(s32[1]{0:T(128)} %bitcast.first_ref, s32[128]{0:T(128)S(1)} %copy-done.23, ...), custom_call_target="tpu_custom_call" | custom-call | tf_op jit(solution)/shard_map/prepare/pallas_call | solution.py:325
  37.6 0.8 copy-done.1
  38.4 0.8 copy-done.8
  39.2 0.7 copy-done.12
  39.9 4.2 %all-to-all-done.1 = bf16[16,4,16,128]{3,2,1,0:T(8,128)(2,1)S(1)} async-done(((bf16[16,4,16,128]{3,2,1,0:T(8,128)(2,1)}), bf16[16,4,16,128]{3,2,1,0:T(8,128)(2,1)S(1)}, u32[]{:S(2)}, u32[]{:S(2)}) %all-to-all-start.1) | async-done | bytes 262176 | tf_op jit(solution)/shard_map/all_to_all | solution.py:274
  44.1 0.9 mixed_norm_back.1
  45.0 12.8 %all_to_all.38.dmix_ref = bf16[16,4,16,128]{3,2,1,0:T(8,128)(2,1)S(1)} all-to-all(bf16[16,4,16,128]{3,2,1,0:T(8,128)(2,1)S(1)} %bitcast.14), channel_id=1, replica_groups=mesh['groups'=2,'row'=16] {'row'}, dimensions={0} | all-to-all | bytes 524288 | tf_op jit(solution)/shard_map/all_to_all | solution.py:274
  57.8 0.9 copy-done.15
  58.8 0.9 copy-done.17
  60.1 0.8 copy-done
  60.9 4.2 %all-to-all-start.3 = ((bf16[16,2,4,16,128]{4,3,2,1,0:T(8,128)(2,1)}), bf16[16,2,4,16,128]{4,3,2,1,0:T(8,128)(2,1)}, u32[]{:S(2)}, u32[]{:S(2)}) async-start(bf16[16,2,4,16,128]{4,3,2,1,0:T(8,128)(2,1)} %copy-done), calls=%async_computation.3 | async-start | bytes 1048576 | tf_op jit(solution)/shard_map/all_to_all | solution.py:274
  65.1 1.0 copy-done.9
  66.2 1.4 %update.1 = (bf16[1,64,2048]{2,1,0:T(8,128)(2,1)S(1)}, f32[72,128]{1,0:T(8,128)S(1)}) custom-call(f32[2,64]{1,0:T(2,128)S(1)} %copy-done.21, bf16[64,16,128]{2,1,0:T(8,128)(2,1)S(1)} %bitcast.11, f32[64,16,128]{2,1,0:T(8,128)S(1)} %get-tuple-element.25.dout_ref, bf16[1,64,2048]{2,1,0:T(8,128)(2,1)S(1)} %get-tuple-element.24.zn_ref, ...), custom_call_target="tpu_custom_call" | custom-call | tf_op jit(solution)/shard_map/update/pallas_call | solution.py:375
  67.6 0.7 copy-done.18
  68.3 11.3 %all-to-all-done.3.dlr_ref = bf16[16,2,4,16,128]{4,3,2,1,0:T(8,128)(2,1)} async-done(((bf16[16,2,4,16,128]{4,3,2,1,0:T(8,128)(2,1)}), bf16[16,2,4,16,128]{4,3,2,1,0:T(8,128)(2,1)}, u32[]{:S(2)}, u32[]{:S(2)}) %all-to-all-start.3) | async-done | bytes 524320 | tf_op jit(solution)/shard_map/all_to_all | solution.py:274
  79.6 1.0 copy-done.2
  80.6 0.9 copy-done.19
  81.6 2.3 %gating_back.1 = (f32[1,64,2048]{2,1,0:T(8,128)S(1)}, f32[256,128]{1,0:T(8,128)S(1)}) custom-call(bf16[16,2,4,16,128]{4,3,2,1,0:T(8,128)(2,1)} %all-to-all-done.3.dlr_ref, f32[1,256,2048]{2,1,0:T(8,128)S(1)} %get-tuple-element.28.fac_ref, bf16[1,64,2048]{2,1,0:T(8,128)(2,1)S(1)} %get-tuple-element.24.zn_ref, bf16[1,64,2048]{2,1,0:T(8,128)(2,1)S(1)} %copy-done.19, ...), custom_call_target="tpu_custom_call" | custom-call | tf_op jit(solution)/shard_map/gating_back/pallas_call | solution.py:405
  83.9 11.8 %all_to_all.39 = f32[16,16,128]{2,1,0:T(8,128)S(1)} all-to-all(f32[16,16,128]{2,1,0:T(8,128)S(1)} %bitcast.16), channel_id=1, replica_groups=mesh['groups'=2,'row'=16] {'row'}, dimensions={0} | all-to-all | bytes 262144 | tf_op jit(solution)/shard_map/all_to_all | solution.py:274
  96.3 3.5 %all-to-all-start.5 = ((f32[16,16,128]{2,1,0:T(8,128)}), f32[16,16,128]{2,1,0:T(8,128)S(1)}, u32[]{:S(2)}, u32[]{:S(2)}) async-start(f32[16,16,128]{2,1,0:T(8,128)} %broadcast_in_dim.2), calls=%async_computation.5 | async-start | bytes 262144 | tf_op jit(solution)/shard_map/all_to_all | solution.py:274
  99.8 1.0 pair_grad.1
  100.8 6.9 %all-to-all-done.5 = f32[16,16,128]{2,1,0:T(8,128)S(1)} async-done(((f32[16,16,128]{2,1,0:T(8,128)}), f32[16,16,128]{2,1,0:T(8,128)S(1)}, u32[]{:S(2)}, u32[]{:S(2)}) %all-to-all-start.5) | async-done | bytes 131104 | tf_op jit(solution)/shard_map/all_to_all | solution.py:274
  108.4 1.7 %unpack.1 = (f32[4,64,64]{2,1,0:T(8,128)}, f32[2,64,64]{2,1,0:T(8,128)}, f32[3,64]{1,0:T(4,128)}) custom-call(f32[256,128]{1,0:T(8,128)} %bitcast.20), custom_call_target="tpu_custom_call" | custom-call | tf_op jit(solution)/shard_map/unpack/pallas_call | solution.py:429
  (41 shorter events, 3.7 us)
Async XLA Ops:
  0.6 33.4 %copy-start.23 = (s32[128]{0:T(128)S(1)}, s32[128]{0:T(128)}, u32[]{:S(2)}) copy-start(s32[128]{0:T(128)} %tokens_ref.3) | copy-start | bytes 1540
  0.6 43.4 %copy-start.21 = (f32[2,64]{1,0:T(2,128)S(1)}, f32[2,64]{1,0:T(2,128)}, u32[]{:S(2)}) copy-start(f32[2,64]{1,0:T(2,128)} %gains_ref.7) | copy-start | bytes 1540
  1.4 0.9 copy-start.4
  2.4 0.8 copy-start.6
  3.2 0.7 copy-start.20
  3.9 0.7 copy-start.22
  4.5 0.7 copy-start.24
  5.2 28.8 %copy-start.5 = (bf16[2,8,64,128]{3,2,1,0:T(8,128)(2,1)S(1)}, bf16[2,8,64,128]{3,2,1,0:T(8,128)(2,1)}, u32[]{:S(2)}) copy-start(bf16[2,8,64,128]{3,2,1,0:T(8,128)(2,1)} %param.8) | copy-start | bytes 786436
  5.2 28.9 %copy-start.7 = (bf16[4,64,64]{2,1,0:T(8,128)(2,1)S(1)}, bf16[4,64,64]{2,1,0:T(8,128)(2,1)}, u32[]{:S(2)}) copy-start(bf16[4,64,64]{2,1,0:T(8,128)(2,1)} %w_ref.5) | copy-start | bytes 98308
  5.2 28.9 %copy-start.10 = (bf16[2,64,64]{2,1,0:T(8,128)(2,1)S(1)}, bf16[2,64,64]{2,1,0:T(8,128)(2,1)}, u32[]{:S(2)}) copy-start(bf16[2,64,64]{2,1,0:T(8,128)(2,1)} %wo_ref.5) | copy-start | bytes 49156
  29.2 0.7 copy-start.14
  29.9 4.1 %copy-start.16 = (bf16[8,128,128]{2,1,0:T(8,128)(2,1)}, bf16[8,128,128]{2,1,0:T(8,128)(2,1)S(1)}, u32[]{:S(2)}) copy-start(bf16[8,128,128]{2,1,0:T(8,128)(2,1)S(1)} %get-tuple-element.27.right_ref) | copy-start | bytes 786436
  29.9 14.2 %all-to-all-start.1 = ((bf16[16,4,16,128]{3,2,1,0:T(8,128)(2,1)}), bf16[16,4,16,128]{3,2,1,0:T(8,128)(2,1)S(1)}, u32[]{:S(2)}, u32[]{:S(2)}) async-start(bf16[16,4,16,128]{3,2,1,0:T(8,128)(2,1)} %get-tuple-element.23), calls=%async_computation.1 | async-start | bytes 524288 | tf_op jit(solution)/shard_map/all_to_all | solution.py:274
  34.1 1.0 copy-start.11
  37.6 0.8 copy-start.1
  38.4 0.8 copy-start.8
  39.2 0.7 copy-start.12
  44.1 21.0 %copy-start.13 = (bf16[1,64,2048]{2,1,0:T(8,128)(2,1)S(1)}, bf16[1,64,2048]{2,1,0:T(8,128)(2,1)}, u32[]{:S(2)}) copy-start(bf16[1,64,2048]{2,1,0:T(8,128)(2,1)} %copy-done.12) | copy-start | bytes 786436
  57.8 1.0 copy-start.15
  58.8 0.9 copy-start.17
  60.1 0.8 copy-start
  60.9 18.7 %all-to-all-start.3 = ((bf16[16,2,4,16,128]{4,3,2,1,0:T(8,128)(2,1)}), bf16[16,2,4,16,128]{4,3,2,1,0:T(8,128)(2,1)}, u32[]{:S(2)}, u32[]{:S(2)}) async-start(bf16[16,2,4,16,128]{4,3,2,1,0:T(8,128)(2,1)} %copy-done), calls=%async_computation.3 | async-start | bytes 1048576 | tf_op jit(solution)/shard_map/all_to_all | solution.py:274
  65.1 1.0 copy-start.9
  67.6 0.7 copy-start.18
  79.6 1.0 copy-start.2
  80.6 0.9 copy-start.19
  81.6 18.3 %copy-start.3 = (f32[1,64,2048]{2,1,0:T(8,128)S(1)}, f32[1,64,2048]{2,1,0:T(8,128)}, u32[]{:S(2)}) copy-start(f32[1,64,2048]{2,1,0:T(8,128)} %copy-done.1) | copy-start | bytes 1572868
  96.3 11.4 %all-to-all-start.5 = ((f32[16,16,128]{2,1,0:T(8,128)}), f32[16,16,128]{2,1,0:T(8,128)S(1)}, u32[]{:S(2)}, u32[]{:S(2)}) async-start(f32[16,16,128]{2,1,0:T(8,128)} %broadcast_in_dim.2), calls=%async_computation.5 | async-start | bytes 262144 | tf_op jit(solution)/shard_map/all_to_all | solution.py:274
  107.7 0.6 copy-start.25

commit v2 on v1

v2 whole, which is shorter than its diff:
```python
import functools

import jax
import jax.numpy as jnp
from jax import lax
from jax.experimental import pallas as pl
from jax.experimental.pallas import tpu as pltpu
from jax.sharding import PartitionSpec as P

EPS = 1e-05
LANES = 128
F32 = jnp.float32
BF16 = jnp.bfloat16


def dot(a, b):
    return jnp.dot(a, b, preferred_element_type=F32)


def dot_nt(a, b):
    return lax.dot_general(a, b, (((1,), (1,)), ((), ())), preferred_element_type=F32)


def dot_tn(a, b):
    return lax.dot_general(a, b, (((0,), (0,)), ((), ())), preferred_element_type=F32)


def transposed(weight):
    return weight.astype(F32).T.astype(BF16)


def column(row):
    n = row.shape[1]
    eye = lax.broadcasted_iota(jnp.int32, (n, n), 0) == lax.broadcasted_iota(jnp.int32, (n, n), 1)
    return jnp.sum(jnp.where(eye, row, 0.0), axis=1, keepdims=True)


def as_row(col):
    n = col.shape[0]
    eye = lax.broadcasted_iota(jnp.int32, (n, n), 0) == lax.broadcasted_iota(jnp.int32, (n, n), 1)
    return jnp.sum(jnp.where(eye, col, 0.0), axis=0, keepdims=True)


def layer_norm(x):
    mean = jnp.mean(x, axis=0, keepdims=True)
    centred = x - mean
    rstd = lax.rsqrt(jnp.mean(centred * centred, axis=0, keepdims=True) + EPS)
    return centred * rstd, rstd


def mask_rows(me_ref, tokens_ref, cover_ref, tok_ref, block, rows):
    width, (tiles, _, templ) = tokens_ref.shape[1], cover_ref.shape
    tile = width // tiles
    first = me_ref[0] * rows
    here = lax.broadcasted_iota(jnp.int32, (rows, width), 0) + first == lax.broadcasted_iota(jnp.int32, (rows, width), 1)
    row_mask = jnp.sum(jnp.where(here, tokens_ref[...].astype(F32), 0.0), axis=1, keepdims=True)
    column_mask = tok_ref[...].astype(F32)
    cover = cover_ref[first // tile].astype(F32)
    here = lax.broadcasted_iota(jnp.int32, (tiles, templ), 0) == block() * LANES // tile
    cover = jnp.sum(jnp.where(here, cover, 0.0), axis=0, keepdims=True)
    out = []
    for t in range(templ):
        masked = column_mask * cover[:, t:t + 1]
        out += [masked * row_mask[r:r + 1, :] for r in range(rows)]
    return out


def front_kernel(rows, block, me_ref, tokens_ref, cover_ref, pair_ref, cot_ref, tok_ref, w_ref, wo_ref, gains_ref, bias_ref, lr_ref, zn_ref, fac_ref, cg_ref, du_ref, normed_ref, rstd_ref, dout_ref, wcat_ref, left_scr, right_scr, dout_scr):
    count, chans, _ = pair_ref.shape
    wcat_ref[...] = jnp.concatenate([w_ref[0], w_ref[1], w_ref[2], w_ref[3], wo_ref[0]], axis=1)
    gain, bias = column(gains_ref[0:1, :]), column(bias_ref[...])
    masks = mask_rows(me_ref, tokens_ref, cover_ref, tok_ref, block, rows)
    weights = jnp.concatenate([transposed(w_ref[p]) for p in range(4)] + [transposed(wo_ref[0])], axis=0)
    w_back = wo_ref[1]
    for pos in range(0, count, 2):
        span = slice(pos * LANES, (pos + 2) * LANES)
        zn = []
        for q in (pos, pos + 1):
            normed, rstd = layer_norm(pair_ref[q].astype(F32))
            lanes = slice(q * LANES, (q + 1) * LANES)
            normed_ref[0, :, lanes] = normed
            rstd_ref[0, :, lanes] = rstd
            zn.append((normed * gain + bias).astype(BF16))
        zn = jnp.concatenate(zn, axis=1)
        zn_ref[0, :, span] = zn
        pre = dot(weights, zn)
        for j in range(2):
            part = pre[:, j * LANES:(j + 1) * LANES]
            pre_p = [part[p * chans:(p + 1) * chans] for p in range(5)]
            mask = masks[pos + j]
            where = pl.ds(pos + j, chans, stride=count)
            lanes = slice((pos + j) * LANES, (pos + j + 1) * LANES)
            for p, scr in ((0, left_scr), (2, right_scr)):
                sig = jax.nn.sigmoid(pre_p[p])
                sig_mask = sig * mask
                both = sig_mask * pre_p[p + 1]
                scr[where, :] = both
                fac_ref[0, p * chans:(p + 1) * chans, lanes] = both * (1.0 - sig)
                fac_ref[0, (p + 1) * chans:(p + 2) * chans, lanes] = sig_mask
            gate = jax.nn.sigmoid(pre_p[4])
            d_update = cot_ref[pos + j].astype(F32) * gate
            cg_ref[0, :, lanes] = d_update * (1.0 - gate)
            du_ref[0, :, lanes] = d_update.astype(BF16)
        d_outn = dot(w_back, du_ref[0, :, span])
        for j in range(2):
            dout_scr[pl.ds(pos + j, chans, stride=count), :] = d_outn[:, j * LANES:(j + 1) * LANES]
    groups, both, _, _ = lr_ref.shape
    per = both // 2
    lr_ref[:, 0:per] = left_scr[...].astype(BF16).reshape(groups, per, count, LANES)
    lr_ref[:, per:both] = right_scr[...].astype(BF16).reshape(groups, per, count, LANES)
    dout_ref[...] = dout_scr[...].reshape(chans, count, LANES)


def mixed_kernel(rows, cols_ref, mixed_ref, left_ref, right_ref):
    n, both, count, width = cols_ref.shape
    per, templ = both // 2, count // rows
    for c in range(per):
        left_all = cols_ref[:, c].astype(F32)
        right_all = cols_ref[:, per + c].astype(F32)
        parts = []
        for t in range(templ):
            left = left_all[:, t * rows:(t + 1) * rows].reshape(n * rows, width).astype(BF16)
            right = right_all[:, t * rows:(t + 1) * rows].reshape(n * rows, width).astype(BF16)
            left_ref[c * templ + t] = left
            right_ref[c * templ + t] = right
            parts.append(dot_nt(left, right).reshape(n, rows, width))
        mixed_ref[:, c] = jnp.concatenate(parts, axis=1).astype(BF16)


def triangle_back_kernel(rows, dmix_ref, left_ref, right_ref, extra_ref, out_ref):
    n, per, count, width = dmix_ref.shape
    templ = count // rows
    for c in range(per):
        dmix_all = dmix_ref[:, c].astype(F32)
        left_parts, right_parts = [], []
        for t in range(templ):
            dmix = dmix_all[:, t * rows:(t + 1) * rows].reshape(n * rows, width).astype(BF16)
            left_parts.append(dot(dmix, right_ref[c * templ + t]).reshape(n, rows, width))
            right_parts.append(dot_tn(dmix, left_ref[c * templ + t]).reshape(n, rows, width))
        out_ref[:, c] = jnp.concatenate(left_parts, axis=1).astype(BF16)
        out_ref[:, per + c] = jnp.concatenate(right_parts, axis=1).astype(BF16)
    out_ref[:, 2 * per] = extra_ref[...]


def split(x):
    high = x.astype(BF16).astype(F32)
    return high, x - high


def tree_sum(parts):
    while len(parts) > 1:
        parts = [a + b for a, b in zip(parts[::2], parts[1::2])] + parts[len(parts) // 2 * 2:]
    return parts[0]


def channel_sum(chans, value):
    accs = [None] * 4
    for c in range(chans):
        v = value(c)
        accs[c % 4] = v if accs[c % 4] is None else accs[c % 4] + v
    return tree_sum([a for a in accs if a is not None])


def middle_kernel(n, block, gains_ref, mixed_ref, dout_ref, zn_ref, cg_ref, du_ref, wo_ref, dmix_ref, dgate_ref, grads_ref, scr, norm_scr, outn_scr):
    chans, count, _ = mixed_ref.shape
    inv = 1.0 / chans
    mean = channel_sum(chans, lambda c: mixed_ref[c].astype(F32)) * inv
    mean_h = channel_sum(chans, lambda c: dout_ref[c] * gains_ref[1, c]) * inv

    def squares(c):
        centred = mixed_ref[c].astype(F32) - mean
        return centred * centred

    rstd = lax.rsqrt(channel_sum(chans, squares) * inv + EPS)

    def products(c):
        gain = gains_ref[1, c]
        xhat = (mixed_ref[c].astype(F32) - mean) * rstd
        outn = xhat * gain
        scr[c * count:(c + 1) * count, :] = outn
        product = dout_ref[c] * xhat
        norm_scr[c:c + 1, :] = jnp.sum(product, axis=0, keepdims=True)
        return product * gain

    mean_p = channel_sum(chans, products) * inv
    for c in range(chans):
        xhat = (mixed_ref[c].astype(F32) - mean) * rstd
        dmix_ref[c] = (rstd * (dout_ref[c] * gains_ref[1, c] - mean_h - xhat * mean_p)).astype(BF16)
    w_update = transposed(wo_ref[1])
    for pos in range(count):
        span = slice(pos * LANES, (pos + 1) * LANES)
        outn_scr[:, span] = scr[pl.ds(pos, chans, stride=count), :].astype(BF16)
    update = dot(w_update, outn_scr[...])
    d_gate = (cg_ref[0] * update).astype(BF16)
    dgate_ref[0] = d_gate
    gate_grad = dot_nt(zn_ref[0], d_gate)
    out_grad = dot_nt(outn_scr[...], du_ref[0])
    norm = as_row(jnp.sum(norm_scr[...], axis=1, keepdims=True))
    if n:
        grads = jnp.concatenate([gate_grad, out_grad], axis=1)
        norm = jnp.concatenate([norm, jnp.zeros_like(norm)], axis=1)
        high, low = split(grads)
        norm_high, norm_low = split(norm)
        share = chans // n
        pad = [jnp.zeros((4 - share, 2 * chans), F32)] if share < 4 else []
        rest = jnp.zeros((6, 2 * chans), F32)
        for d in range(n):
            mine = slice(d * share, (d + 1) * share)
            tile = jnp.concatenate([norm_high, norm_low, high[mine], *pad, low[mine], *pad, rest], axis=0)
            grads_ref[d] = tile.astype(BF16)
        return

    @pl.when(block() == 0)
    def _():
        grads_ref[...] = jnp.zeros_like(grads_ref)

    grads_ref[0:chans, 0:chans] += gate_grad
    grads_ref[0:chans, chans:2 * chans] += out_grad
    grads_ref[chans:chans + 1, 0:chans] += norm


def back_kernel(blocks, block, me_ref, dlr_ref, fac_ref, zn_ref, dgate_ref, normed_ref, rstd_ref, wcat_ref, gains_ref, pair_ref, keep_ref, send_ref, done_ref, left_scr, right_scr, d_scr, pack_scr):
    groups, parts, count, _ = dlr_ref.shape
    per = parts // 2
    chans = groups * per
    left_scr[...] = dlr_ref[:, 0:per].astype(F32).reshape(chans * count, LANES)
    right_scr[...] = dlr_ref[:, per:2 * per].astype(F32).reshape(chans * count, LANES)
    d_scr[4 * chans:5 * chans, :] = dgate_ref[0]
    for pos in range(count):
        span = slice(pos * LANES, (pos + 1) * LANES)
        where = pl.ds(pos, chans, stride=count)
        d_left, d_right = left_scr[where, :], right_scr[where, :]
        for p in range(4):
            d = d_left if p < 2 else d_right
            d_scr[p * chans:(p + 1) * chans, span] = (d * fac_ref[0, p * chans:(p + 1) * chans, span]).astype(BF16)
    d_zn = dot(wcat_ref[...], d_scr[...])
    gain = column(gains_ref[0:1, :])
    for pos in range(count):
        span = slice(pos * LANES, (pos + 1) * LANES)
        h = d_zn[:, span] * gain
        normed = normed_ref[0, :, span]
        mean_h = jnp.mean(h, axis=0, keepdims=True)
        mean_p = jnp.mean(h * normed, axis=0, keepdims=True)
        pair_ref[pos] = (rstd_ref[0, :, span] * (h - mean_h - normed * mean_p)).astype(BF16)
    grads = dot_nt(zn_ref[0], d_scr[0:4 * chans, :])
    bias_grad = as_row(jnp.sum(d_zn, axis=1, keepdims=True))
    gain_grad = as_row(jnp.sum(d_zn * normed_ref[0], axis=1, keepdims=True))

    @pl.when(block() == 0)
    def _():
        pack_scr[...] = jnp.zeros_like(pack_scr)

    pack_scr[0:chans, :] += grads[:, 0:2 * chans]
    pack_scr[chans:2 * chans, :] += grads[:, 2 * chans:4 * chans]
    pack_scr[2 * chans:2 * chans + 1, 0:chans] += gain_grad
    pack_scr[2 * chans + 1:2 * chans + 2, 0:chans] += bias_grad

    @pl.when(block() == blocks - 1)
    def _():
        half = me_ref[0] % 2
        own = pl.multiple_of(half * chans, 8)
        other = pl.multiple_of((1 - half) * chans, 8)
        keep_ref[0:chans, :] = pack_scr[pl.ds(own, chans), :]
        send_ref[0:chans, :] = pack_scr[pl.ds(other, chans), :]
        keep_ref[chans:chans + 8, :] = pack_scr[2 * chans:2 * chans + 8, :]
        send_ref[chans:chans + 8, :] = pack_scr[2 * chans:2 * chans + 8, :]
        if parts > 2 * per:
            done_ref[...] = jnp.sum(dlr_ref[:, 2 * per].astype(F32), axis=0)
        else:
            done_ref[...] = jnp.zeros_like(done_ref)


def combine_kernel(keep_ref, got_ref, done_ref, out_ref):
    rows = keep_ref.shape[0] - 8
    total = keep_ref[...] + got_ref[...]
    norm_high, norm_low = split(total[rows:rows + 2])
    done_high, done_low = split(done_ref[2:6, :] + done_ref[6:10, :])
    tile = jnp.concatenate([norm_high, norm_low, done_high, done_low, jnp.zeros((4, total.shape[1]), F32)], axis=0)
    block = jnp.concatenate([total[0:rows], tile], axis=0).astype(BF16)
    for d in range(out_ref.shape[0]):
        out_ref[d] = block


def unpack_kernel(scale, share, pack_ref, done_ref, proj_ref, out_ref, norm_ref):
    n, chans = pack_ref.shape[0], proj_ref.shape[1]
    for half in range(2):
        total = tree_sum([pack_ref[d, 0:chans, :].astype(F32) for d in range(half, n, 2)]) * scale
        proj_ref[2 * half] = total[:, 0:chans]
        proj_ref[2 * half + 1] = total[:, chans:2 * chans]
    tiles = [pack_ref[d, chans:chans + 16, :].astype(F32) for d in range(n)]
    norms = tree_sum(tiles[::2])
    norms = (norms[0:2] + norms[2:4]) * scale
    norm_ref[0:2, :] = norms[:, 0:chans]
    if share:
        norm_ref[2:3, :] = (done_ref[0:1, 0:chans] + done_ref[1:2, 0:chans]) * scale
        for d in range(n):
            rows = (tiles[d][4:4 + share] + tiles[d][8:8 + share]) * scale
            out_ref[0, d * share:(d + 1) * share] = rows[:, 0:chans]
            out_ref[1, d * share:(d + 1) * share] = rows[:, chans:2 * chans]
    else:
        norm_ref[2:3, :] = done_ref[chans:chans + 1, 0:chans] * scale
        for p in range(2):
            out_ref[p] = done_ref[0:chans, p * chans:(p + 1) * chans] * scale


def exchange(x):
    return lax.all_to_all(x, "row", split_axis=0, concat_axis=0, tiled=True)


def per_device(n, pair, cotangent, token_mask, coverage, w_proj, w_out, layer_norm_gains, ln_bias):
    templ, rows, chans, width = pair.shape
    count = templ * rows
    blocks = width // LANES
    direct = blocks == 1 and chans % n == 0 and chans // n <= 4
    groups = n if direct else chans
    per = chans // groups
    lanes = count * LANES
    me = lax.axis_index("row").astype(jnp.int32).reshape(1)
    tokens_row = token_mask.reshape(1, width)

    params = pltpu.CompilerParams(vmem_limit_bytes=(16 if blocks == 1 else 40) * 1024 * 1024)
    smem = pl.BlockSpec(memory_space=pltpu.SMEM)
    whole = pl.BlockSpec(memory_space=pltpu.VMEM)

    def block_spec(shape, index):
        return whole if blocks == 1 else pl.BlockSpec(shape, index)

    def full(shape):
        return block_spec(shape, lambda b: (0,) * len(shape))

    def array(shape, dtype):
        return pltpu.VMEM(shape, dtype) if blocks == 1 else jax.ShapeDtypeStruct(shape, dtype)

    def from_hbm(x):
        return pltpu.with_memory_space_constraint(x, pltpu.HBM)

    def call(name, kernel, args, in_specs, out_specs, out_shape, scratch_shapes=()):
        block = (lambda: 0) if blocks == 1 else (lambda: pl.program_id(0))
        kernel = functools.partial(kernel, block)
        return pl.pallas_call(
            kernel,
            grid=() if blocks == 1 else (blocks,),
            in_specs=in_specs,
            out_specs=out_specs,
            out_shape=out_shape,
            scratch_shapes=scratch_shapes,
            compiler_params=params,
            name=name,
        )(*args)

    rows_spec = block_spec((count, chans, LANES), lambda b: (0, 0, b))
    tok_spec = block_spec((1, LANES), lambda b: (0, b))
    lr_spec = block_spec((groups, 2 * per, count, LANES), lambda b: (0, 0, 0, b))
    cat_spec = block_spec((1, chans, lanes), lambda b: (b, 0, 0))
    fac_spec = block_spec((1, 4 * chans, lanes), lambda b: (b, 0, 0))
    one_spec = block_spec((1, 1, lanes), lambda b: (b, 0, 0))
    chan_spec = block_spec((chans, count, LANES), lambda b: (0, 0, b))
    w_spec, wo_spec, gains_spec = full(w_proj.shape), full(w_out.shape), full(layer_norm_gains.shape)
    scratch = pltpu.VMEM((chans * count, LANES), F32)
    pair_rows = from_hbm(pair.reshape(count, chans, width))
    cot_rows = from_hbm(cotangent.reshape(count, chans, width))
    w_proj_in, w_out_in, gains_in = from_hbm(w_proj), from_hbm(w_out), from_hbm(layer_norm_gains)
    tokens_in, cover_in = from_hbm(tokens_row), from_hbm(coverage.transpose(1, 2, 0))
    half_rows = chans + 8

    def cat(dtype):
        return array((blocks, chans, lanes), dtype)

    lr, zn, fac, cg, d_update, normed, rstd, d_outn, wcat = call(
        "front",
        functools.partial(front_kernel, rows),
        (me, tokens_in, cover_in, pair_rows, cot_rows, tokens_in, w_proj_in, w_out_in, gains_in, from_hbm(ln_bias.reshape(1, chans))),
        [smem, full((1, width)), full(cover_in.shape), rows_spec, rows_spec, tok_spec, w_spec, wo_spec, gains_spec, full((1, chans))],
        [lr_spec, cat_spec, fac_spec, cat_spec, cat_spec, cat_spec, one_spec, chan_spec, full((chans, 5 * chans))],
        [
            jax.ShapeDtypeStruct((groups, 2 * per, count, width), BF16),
            cat(BF16),
            array((blocks, 4 * chans, lanes), F32),
            cat(F32),
            cat(BF16),
            cat(F32),
            array((blocks, 1, lanes), F32),
            array((chans, count, width), F32),
            array((chans, 5 * chans), BF16),
        ],
        [scratch, scratch, scratch],
    )

    if direct:
        cols = exchange(lr)
        mixed, left_cols, right_cols = pl.pallas_call(
            functools.partial(mixed_kernel, rows),
            out_shape=[
                jax.ShapeDtypeStruct((n, per, count, width), BF16),
                array((per * templ, width, width), BF16),
                array((per * templ, width, width), BF16),
            ],
            compiler_params=params,
            name="mixed",
        )(cols)
        mixed_rows = exchange(mixed).reshape(chans, count, width)
    else:
        slices = chans * templ // n
        cols = lr.reshape(chans, 2, templ, rows, width).transpose(0, 2, 1, 3, 4)
        cols = exchange(cols.reshape(n * slices, 2, rows, width)).reshape(n, slices, 2, rows, width)
        left_cols, right_cols = cols.transpose(2, 1, 0, 3, 4).reshape(2, slices, width, width)
        mixed = jnp.einsum("sik,sjk->sij", left_cols, right_cols, preferred_element_type=F32)
        mixed = mixed.astype(BF16).reshape(slices, n, rows, width).transpose(1, 0, 2, 3)
        mixed_rows = exchange(mixed.reshape(n * slices, rows, width)).reshape(chans, count, width)

    d_mixed, d_gate, out_grads = call(
        "middle",
        functools.partial(middle_kernel, n if direct else 0),
        (layer_norm_gains, mixed_rows, d_outn, zn, cg, d_update, w_out),
        [smem, chan_spec, chan_spec, cat_spec, cat_spec, cat_spec, wo_spec],
        [chan_spec, cat_spec, full((n, 16, 2 * chans) if direct else (chans + 8, 2 * chans))],
        [
            jax.ShapeDtypeStruct((chans, count, width), BF16),
            cat(BF16),
            array((n, 16, 2 * chans), BF16) if direct else array((chans + 8, 2 * chans), F32),
        ],
        [scratch, pltpu.VMEM((chans, LANES), F32), pltpu.VMEM((chans, lanes), BF16)],
    )

    if direct:
        dmix_cols = exchange(d_mixed.reshape(n, per, count, width))
        d_lr = pl.pallas_call(
            functools.partial(triangle_back_kernel, rows),
            out_shape=jax.ShapeDtypeStruct((n, 2 * per + 1, count, width), BF16),
            compiler_params=params,
            name="triangle_back",
        )(dmix_cols, left_cols, right_cols, out_grads)
        d_lr = exchange(d_lr)
        d_lr_spec = whole
    else:
        dmix_cols = exchange(d_mixed.reshape(n * slices, rows, width)).reshape(n, slices, rows, width)
        dmix_cols = dmix_cols.transpose(1, 0, 2, 3).reshape(slices, width, width)
        d_left = jnp.einsum("sij,sjk->sik", dmix_cols, right_cols, preferred_element_type=F32)
        d_right = jnp.einsum("sij,sik->sjk", dmix_cols, left_cols, preferred_element_type=F32)
        d_lr = jnp.stack([d_left.astype(BF16), d_right.astype(BF16)]).reshape(2, slices, n, rows, width)
        d_lr = exchange(d_lr.transpose(2, 1, 0, 3, 4).reshape(n * slices, 2, rows, width))
        d_lr = d_lr.reshape(chans, templ, 2, rows, width).transpose(0, 2, 1, 3, 4)
        d_lr = d_lr.reshape(groups, 2 * per, count, width)
        d_lr_spec = lr_spec

    pair_grad, keep, send, done = call(
        "back",
        functools.partial(back_kernel, blocks),
        (me, d_lr, fac, zn, d_gate, normed, rstd, wcat, layer_norm_gains),
        [smem, d_lr_spec, fac_spec, cat_spec, cat_spec, cat_spec, one_spec, full((chans, 5 * chans)), gains_spec],
        [rows_spec, full((half_rows, 2 * chans)), full((half_rows, 2 * chans)), full((16, 2 * chans))],
        [
            jax.ShapeDtypeStruct((count, chans, width), BF16),
            array((half_rows, 2 * chans), F32),
            jax.ShapeDtypeStruct((half_rows, 2 * chans), F32),
            array((16, 2 * chans), F32),
        ],
        [scratch, scratch, pltpu.VMEM((5 * chans, lanes), BF16), pltpu.VMEM((2 * chans + 8, 2 * chans), F32)],
    )

    got = lax.ppermute(send, "row", [(d, d ^ 1) for d in range(n)])
    sums = pl.pallas_call(
        combine_kernel,
        out_shape=jax.ShapeDtypeStruct((n, chans + 16, 2 * chans), BF16),
        compiler_params=params,
        name="combine",
    )(keep, got, done)
    sums = exchange(sums)
    grad_proj, grad_out, norm_grads = pl.pallas_call(
        functools.partial(unpack_kernel, 1.0 / width, chans // n if direct else 0),
        out_shape=[
            jax.ShapeDtypeStruct(w_proj.shape, F32),
            jax.ShapeDtypeStruct(w_out.shape, F32),
            jax.ShapeDtypeStruct((3, chans), F32),
        ],
        compiler_params=params,
        name="unpack",
    )(sums, done if direct else lax.psum(out_grads, "row"))
    return pair_grad.reshape(pair.shape), grad_proj, grad_out, norm_grads


def solution(mesh):
    return jax.shard_map(
        functools.partial(per_device, mesh.shape["row"]),
        mesh=mesh,
        in_specs=(
            P("groups", "row", None, None),
            P("groups", "row", None, None),
            P("groups"),
            P("groups", None, None),
            P(),
            P(),
            P(),
            P(),
        ),
        out_specs=(
            P("groups", "row", None, None),
            P("groups", None, None),
            P("groups", None, None),
            P("groups", None),
        ),
        check_vma=False,
    )
```

time: 111 us -> 92.8 us (0.84)
  blocking collectives: 46.2 us -> 82.4 us
  waiting for transfers between devices: 22.4 us -> 1.09 us
  local copies, waits for them, and re-layouts: 16.2 us -> 0.01 us
  starting transfers between devices: 11.8 us -> 0.12 us
  Pallas kernels: 12.5 us -> 8.2 us
    all_to_all x3 -> x5, blocking collectives: 46.2 us -> 82.4 us  [exchange(): return lax.all_to_all(x, 'row', split_axis=0, concat_axis=0, tiled=True)]
    all_to_all x3 -> x0, waiting for transfers between devices: 22.4 us -> none  [exchange(): return lax.all_to_all(x, 'row', split_axis=0, concat_axis=0, tiled=True)]
    unnamed x53 -> x4, local copies, waits for them, and re-layouts: 15.5 us -> 0.01 us
    all_to_all x3 -> x0, starting transfers between devices: 11.8 us -> none  [exchange(): return lax.all_to_all(x, 'row', split_axis=0, concat_axis=0, tiled=True)]
    pallas_call x7 -> x5, Pallas kernels: 11.2 us -> 7.56 us  [the longest x3 6.76 us: call(): pl.pallas_call(kernel, grid=() if blocks == 1 else (blocks,), in_specs=in...]
  transfers between devices with their start and end apart: 3 -> 1, of which waited for: 3 -> 1; matrix products, arithmetic and copies ran while one was open for 0% -> 0% of each run, Pallas kernels for 5% -> 0%
where the time goes in v2:
time: 92.8 us; the launch traced here: 92.5 us
  blocking collectives  82.4 us (89%)
  Pallas kernels  8.2 us (9%)
  waiting for transfers between devices  1.09 us (1%)
    all_to_all x5, blocking collectives, exchange(): return lax.all_to_all(x, 'row', split_axis=0, concat_axis=0, tiled=True)  82.4 us
    pallas_call x3, Pallas kernels, call(): pl.pallas_call(kernel, grid=() if blocks == 1 else (blocks,), in_specs=in...  6.76 us
  transfers between devices with their start and end apart: 1, of which 1 were waited for; matrix products, arithmetic and copies ran while one was open for 0% of the time, Pallas kernels for 0%

profile of v2, /device:TPU:0, one launch (start us, length us, event | category | flops | bytes accessed | tf_op | source)
XLA Modules:
  0.0 92.5 jit_solution(11903893973162565441)
XLA Ops:
  0.6 0.0 copy-start.1
  0.6 0.0 copy-start
  0.7 3.5 %front.1 = (bf16[16,8,16,128]{3,2,1,0:T(8,128)(2,1)S(1)}, bf16[1,64,2048]{2,1,0:T(8,128)(2,1)S(1)}, f32[1,256,2048]{2,1,0:T(8,128)S(1)}, f32[1,64,2048]{2,1,0:T(...) custom-call(s32[1]{0:T(128)} %bitcast.me_ref, ...), custom_call_target="tpu_custom_call" | custom-call | tf_op jit(solution)/shard_map/front/pallas_call | solution.py:340
  4.1 21.7 %all_to_all.25.cols_ref = bf16[16,8,16,128]{3,2,1,0:T(8,128)(2,1)S(1)} all-to-all(bf16[16,8,16,128]{3,2,1,0:T(8,128)(2,1)S(1)} %get-tuple-element.26), channel_id=1, replica_groups=mesh['groups'=2,'row'=16] {'row'}, dimensions={0} | all-to-all | bytes 1048576 | tf_op jit(solution)/shard_map/all_to_all | solution.py:307
  25.8 0.3 mixed.1
  26.1 13.9 %all_to_all.26 = bf16[16,4,16,128]{3,2,1,0:T(8,128)(2,1)S(1)} all-to-all(bf16[16,4,16,128]{3,2,1,0:T(8,128)(2,1)S(1)} %get-tuple-element.27), channel_id=1, replica_groups=mesh['groups'=2,'row'=16] {'row'}, dimensions={0} | all-to-all | bytes 524288 | tf_op jit(solution)/shard_map/all_to_all | solution.py:307
  40.1 0.0 copy-done.1
  40.1 0.0 copy-done
  40.1 1.5 %middle.1 = (bf16[64,16,128]{2,1,0:T(8,128)(2,1)S(1)}, bf16[1,64,2048]{2,1,0:T(8,128)(2,1)S(1)}, bf16[16,16,128]{2,1,0:T(8,128)(2,1)S(1)}) custom-call(f32[2,64]{1,0:T(2,128)S(1)} %copy-done.1, bf16[64,16,128]{2,1,0:T(8,128)(2,1)S(1)} %bitcast.9, f32[64,16,128]{2,1,0:T(8,128)S(1)} %get-tuple-element.28.dout_ref, ...), custom_call_target="tpu_custom_call" | custom-call | tf_op jit(solution)/shard_map/middle/pallas_call | solution.py:340
  41.6 12.8 %all_to_all.27.dmix_ref = bf16[16,4,16,128]{3,2,1,0:T(8,128)(2,1)S(1)} all-to-all(bf16[16,4,16,128]{3,2,1,0:T(8,128)(2,1)S(1)} %bitcast.10), channel_id=1, replica_groups=mesh['groups'=2,'row'=16] {'row'}, dimensions={0} | all-to-all | bytes 524288 | tf_op jit(solution)/shard_map/all_to_all | solution.py:307
  54.4 0.3 triangle_back.1
  54.7 20.1 %all_to_all.28.dlr_ref = bf16[16,9,16,128]{3,2,1,0:T(8,128)(2,1)S(1)} all-to-all(bf16[16,9,16,128]{3,2,1,0:T(8,128)(2,1)S(1)} %triangle_back.1), channel_id=1, replica_groups=mesh['groups'=2,'row'=16] {'row'}, dimensions={0} | all-to-all | bytes 1179648 | tf_op jit(solution)/shard_map/all_to_all | solution.py:307
  74.8 1.8 %back.1 = (bf16[16,64,128]{2,1,0:T(8,128)(2,1)}, f32[72,128]{1,0:T(8,128)S(1)}, f32[72,128]{1,0:T(8,128)S(1)}, f32[16,128]{1,0:T(8,128)S(1)}) custom-call(s32[1]{0:T(128)} %bitcast.me_ref, bf16[16,9,16,128]{3,2,1,0:T(8,128)(2,1)S(1)} %all_to_all.28.dlr_ref, f32[1,256,2048]{2,1,0:T(8,128)S(1)} %get-tuple-element.36.fac_ref, ...), custom_call_target="tpu_custom_call" | custom-call | tf_op jit(solution)/shard_map/back/pallas_call | solution.py:340
  76.6 0.1 collective-permute-start
  76.7 1.1 %collective-permute-done.got_ref = f32[72,128]{1,0:T(8,128)S(1)} collective-permute-done((f32[72,128]{1,0:T(8,128)S(1)}, f32[72,128]{1,0:T(8,128)S(1)}, u32[]{:S(2)}, u32[]{:S(2)}) %collective-permute-start) | collective-permute-done | bytes 36896 | tf_op jit(solution)/shard_map/ppermute | solution.py:461
  77.8 13.9 %all_to_all.29.pack_ref = bf16[16,80,128]{2,1,0:T(8,128)(2,1)S(1)} all-to-all(bf16[16,80,128]{2,1,0:T(8,128)(2,1)S(1)} %combine.1), channel_id=1, replica_groups=mesh['groups'=2,'row'=16] {'row'}, dimensions={0} | all-to-all | bytes 655360 | tf_op jit(solution)/shard_map/all_to_all | solution.py:307
  91.7 0.8 unpack.1
  (1 shorter events, 0.0 us)
Async XLA Ops:
  0.6 39.5 %copy-start.1 = (f32[2,64]{1,0:T(2,128)S(1)}, f32[2,64]{1,0:T(2,128)}, u32[]{:S(2)}) copy-start(f32[2,64]{1,0:T(2,128)} %gains_ref.5) | copy-start | bytes 1540
  0.6 39.4 %copy-start = (bf16[2,64,64]{2,1,0:T(8,128)(2,1)S(1)}, bf16[2,64,64]{2,1,0:T(8,128)(2,1)}, u32[]{:S(2)}) copy-start(bf16[2,64,64]{2,1,0:T(8,128)(2,1)} %wo_ref.3) | copy-start | bytes 49156
  76.6 1.2 %collective-permute-start = (f32[72,128]{1,0:T(8,128)S(1)}, f32[72,128]{1,0:T(8,128)S(1)}, u32[]{:S(2)}, u32[]{:S(2)}) collective-permute-start(f32[72,128]{1,0:T(8,128)S(1)} %get-tuple-element.43), channel_id=1, source_target_pairs={{0,1},{1,0},{2,3},{3,2},{4,5},{5,4},{6,7},{7,6},{8,9},{9,8},{10,11... | collective-permute-start | bytes 110600 | tf_op jit(solution)/shard_map/ppermute | solution.py:461

commit v3 on v2

--- a/solution.py
+++ b/solution.py
@@ -127,11 +127,11 @@
         mixed_ref[:, c] = jnp.concatenate(parts, axis=1).astype(BF16)
 
 
-def triangle_back_kernel(rows, dmix_ref, left_ref, right_ref, extra_ref, out_ref):
-    n, per, count, width = dmix_ref.shape
-    templ = count // rows
+def triangle_back_kernel(rows, count, dmix_ref, left_ref, right_ref, out_ref, done_ref):
+    n, length, width = dmix_ref.shape
+    per, templ = length // count, count // rows
     for c in range(per):
-        dmix_all = dmix_ref[:, c].astype(F32)
+        dmix_all = dmix_ref[:, c * count:(c + 1) * count].astype(F32)
         left_parts, right_parts = [], []
         for t in range(templ):
             dmix = dmix_all[:, t * rows:(t + 1) * rows].reshape(n * rows, width).astype(BF16)
@@ -139,7 +139,7 @@
             right_parts.append(dot_tn(dmix, left_ref[c * templ + t]).reshape(n, rows, width))
         out_ref[:, c] = jnp.concatenate(left_parts, axis=1).astype(BF16)
         out_ref[:, per + c] = jnp.concatenate(right_parts, axis=1).astype(BF16)
-    out_ref[:, 2 * per] = extra_ref[...]
+    done_ref[...] = jnp.sum(dmix_ref[:, per * count:].astype(F32), axis=0)
 
 
 def split(x):
@@ -161,7 +161,8 @@
     return tree_sum([a for a in accs if a is not None])
 
 
-def middle_kernel(n, block, gains_ref, mixed_ref, dout_ref, zn_ref, cg_ref, du_ref, wo_ref, dmix_ref, dgate_ref, grads_ref, scr, norm_scr, outn_scr):
+def middle_kernel(n, block, gains_ref, mixed_ref, dout_ref, zn_ref, cg_ref, du_ref, wo_ref, dmix_ref, dgate_ref, *rest_refs):
+    *grads_refs, scr, norm_scr, outn_scr = rest_refs
     chans, count, _ = mixed_ref.shape
     inv = 1.0 / chans
     mean = channel_sum(chans, lambda c: mixed_ref[c].astype(F32)) * inv
@@ -185,7 +186,12 @@
     mean_p = channel_sum(chans, products) * inv
     for c in range(chans):
         xhat = (mixed_ref[c].astype(F32) - mean) * rstd
-        dmix_ref[c] = (rstd * (dout_ref[c] * gains_ref[1, c] - mean_h - xhat * mean_p)).astype(BF16)
+        d_mixed = (rstd * (dout_ref[c] * gains_ref[1, c] - mean_h - xhat * mean_p)).astype(BF16)
+        if n:
+            per = chans // n
+            dmix_ref[c // per, c % per * count:(c % per + 1) * count] = d_mixed
+        else:
+            dmix_ref[c] = d_mixed
     w_update = transposed(wo_ref[1])
     for pos in range(count):
         span = slice(pos * LANES, (pos + 1) * LANES)
@@ -199,16 +205,13 @@
     if n:
         grads = jnp.concatenate([gate_grad, out_grad], axis=1)
         norm = jnp.concatenate([norm, jnp.zeros_like(norm)], axis=1)
-        high, low = split(grads)
-        norm_high, norm_low = split(norm)
         share = chans // n
-        pad = [jnp.zeros((4 - share, 2 * chans), F32)] if share < 4 else []
-        rest = jnp.zeros((6, 2 * chans), F32)
+        rest = jnp.zeros((6 - share, 2 * chans), F32)
         for d in range(n):
-            mine = slice(d * share, (d + 1) * share)
-            tile = jnp.concatenate([norm_high, norm_low, high[mine], *pad, low[mine], *pad, rest], axis=0)
-            grads_ref[d] = tile.astype(BF16)
+            tile = jnp.concatenate([grads[d * share:(d + 1) * share], *split(norm), rest], axis=0)
+            dmix_ref[d, share * count:] = tile.astype(BF16)
         return
+    grads_ref, = grads_refs
 
     @pl.when(block() == 0)
     def _():
@@ -219,7 +222,7 @@
     grads_ref[chans:chans + 1, 0:chans] += norm
 
 
-def back_kernel(blocks, block, me_ref, dlr_ref, fac_ref, zn_ref, dgate_ref, normed_ref, rstd_ref, wcat_ref, gains_ref, pair_ref, keep_ref, send_ref, done_ref, left_scr, right_scr, d_scr, pack_scr):
+def back_kernel(blocks, block, me_ref, dlr_ref, fac_ref, zn_ref, dgate_ref, normed_ref, rstd_ref, wcat_ref, gains_ref, pair_ref, keep_ref, send_ref, left_scr, right_scr, d_scr, pack_scr):
     groups, parts, count, _ = dlr_ref.shape
     per = parts // 2
     chans = groups * per
@@ -264,47 +267,51 @@
         send_ref[0:chans, :] = pack_scr[pl.ds(other, chans), :]
         keep_ref[chans:chans + 8, :] = pack_scr[2 * chans:2 * chans + 8, :]
         send_ref[chans:chans + 8, :] = pack_scr[2 * chans:2 * chans + 8, :]
-        if parts > 2 * per:
-            done_ref[...] = jnp.sum(dlr_ref[:, 2 * per].astype(F32), axis=0)
-        else:
-            done_ref[...] = jnp.zeros_like(done_ref)
 
 
 def combine_kernel(keep_ref, got_ref, done_ref, out_ref):
     rows = keep_ref.shape[0] - 8
     total = keep_ref[...] + got_ref[...]
-    norm_high, norm_low = split(total[rows:rows + 2])
-    done_high, done_low = split(done_ref[2:6, :] + done_ref[6:10, :])
-    tile = jnp.concatenate([norm_high, norm_low, done_high, done_low, jnp.zeros((4, total.shape[1]), F32)], axis=0)
+    tile = jnp.concatenate([done_ref[0:4, :], *split(total[rows:rows + 2])], axis=0)
     block = jnp.concatenate([total[0:rows], tile], axis=0).astype(BF16)
     for d in range(out_ref.shape[0]):
         out_ref[d] = block
 
 
-def unpack_kernel(scale, share, pack_ref, done_ref, proj_ref, out_ref, norm_ref):
-    n, chans = pack_ref.shape[0], proj_ref.shape[1]
+def total_kernel(pack_ref, mine_ref, norm_ref):
+    chips, length, _ = pack_ref.shape
+    rows = length - 8
+    mine_ref[0:rows, :] = tree_sum([pack_ref[d, 0:rows, :].astype(F32) for d in range(chips)])
+    tiles = [pack_ref[d, rows:, :].astype(F32) for d in range(chips)]
+    for d in range(0, chips, 2):
+        mine_ref[rows + 4 * d:rows + 4 * d + 8, :] = jnp.concatenate([tiles[d][0:4], tiles[d + 1][0:4]], axis=0)
+    norm_ref[...] = tree_sum(tiles)
+
+
+def unpack_kernel(scale, share, me_ref, mine_ref, got_ref, norm_ref, done_ref, proj_ref, out_ref, norms_ref):
+    chans = proj_ref.shape[1]
+    odd = me_ref[0] % 2 == 1
+    mine, got = mine_ref[...] * scale, got_ref[...] * scale
+    even_odd = (jnp.where(odd, got, mine), jnp.where(odd, mine, got))
     for half in range(2):
-        total = tree_sum([pack_ref[d, 0:chans, :].astype(F32) for d in range(half, n, 2)]) * scale
-        proj_ref[2 * half] = total[:, 0:chans]
-        proj_ref[2 * half + 1] = total[:, chans:2 * chans]
-    tiles = [pack_ref[d, chans:chans + 16, :].astype(F32) for d in range(n)]
-    norms = tree_sum(tiles[::2])
-    norms = (norms[0:2] + norms[2:4]) * scale
-    norm_ref[0:2, :] = norms[:, 0:chans]
+        proj_ref[2 * half] = even_odd[half][0:chans, 0:chans]
+        proj_ref[2 * half + 1] = even_odd[half][0:chans, chans:2 * chans]
+    norms_ref[0:2, :] = (norm_ref[4:6, 0:chans] + norm_ref[6:8, 0:chans]) * scale
     if share:
-        norm_ref[2:3, :] = (done_ref[0:1, 0:chans] + done_ref[1:2, 0:chans]) * scale
-        for d in range(n):
-            rows = (tiles[d][4:4 + share] + tiles[d][8:8 + share]) * scale
-            out_ref[0, d * share:(d + 1) * share] = rows[:, 0:chans]
-            out_ref[1, d * share:(d + 1) * share] = rows[:, chans:2 * chans]
+        norms_ref[2:3, :] = (done_ref[share:share + 1, 0:chans] + done_ref[share + 1:share + 2, 0:chans]) * scale
+        for d in range(chans // share):
+            start = chans + d // 2 * 4
+            rows = even_odd[d % 2][start:start + share]
+            for p in range(2):
+                out_ref[p, d * share:(d + 1) * share] = rows[:, p * chans:(p + 1) * chans]
     else:
-        norm_ref[2:3, :] = done_ref[chans:chans + 1, 0:chans] * scale
+        norms_ref[2:3, :] = done_ref[chans:chans + 1, 0:chans] * scale
         for p in range(2):
             out_ref[p] = done_ref[0:chans, p * chans:(p + 1) * chans] * scale
 
 
-def exchange(x):
-    return lax.all_to_all(x, "row", split_axis=0, concat_axis=0, tiled=True)
+def exchange(x, groups=None):
+    return lax.all_to_all(x, "row", split_axis=0, concat_axis=0, axis_index_groups=groups, tiled=True)
 
 
 def per_device(n, pair, cotangent, token_mask, coverage, w_proj, w_out, layer_norm_gains, ln_bias):
@@ -408,30 +415,25 @@
         mixed = mixed.astype(BF16).reshape(slices, n, rows, width).transpose(1, 0, 2, 3)
         mixed_rows = exchange(mixed.reshape(n * slices, rows, width)).reshape(chans, count, width)
 
-    d_mixed, d_gate, out_grads = call(
+    dmix_shape = (n, per * count + 8, width) if direct else (chans, count, width)
+    d_mixed, d_gate, *out_grads = call(
         "middle",
         functools.partial(middle_kernel, n if direct else 0),
         (layer_norm_gains, mixed_rows, d_outn, zn, cg, d_update, w_out),
         [smem, chan_spec, chan_spec, cat_spec, cat_spec, cat_spec, wo_spec],
-        [chan_spec, cat_spec, full((n, 16, 2 * chans) if direct else (chans + 8, 2 * chans))],
-        [
-            jax.ShapeDtypeStruct((chans, count, width), BF16),
-            cat(BF16),
-            array((n, 16, 2 * chans), BF16) if direct else array((chans + 8, 2 * chans), F32),
-        ],
+        [full(dmix_shape) if direct else chan_spec, cat_spec] + [full((chans + 8, 2 * chans))] * (not direct),
+        [jax.ShapeDtypeStruct(dmix_shape, BF16), cat(BF16)] + [array((chans + 8, 2 * chans), F32)] * (not direct),
         [scratch, pltpu.VMEM((chans, LANES), F32), pltpu.VMEM((chans, lanes), BF16)],
     )
 
     if direct:
-        dmix_cols = exchange(d_mixed.reshape(n, per, count, width))
-        d_lr = pl.pallas_call(
-            functools.partial(triangle_back_kernel, rows),
-            out_shape=jax.ShapeDtypeStruct((n, 2 * per + 1, count, width), BF16),
+        d_lr, done = pl.pallas_call(
+            functools.partial(triangle_back_kernel, rows, count),
+            out_shape=[jax.ShapeDtypeStruct((n, 2 * per, count, width), BF16), array((8, width), F32)],
             compiler_params=params,
             name="triangle_back",
-        )(dmix_cols, left_cols, right_cols, out_grads)
+        )(exchange(d_mixed), left_cols, right_cols)
         d_lr = exchange(d_lr)
-        d_lr_spec = whole
     else:
         dmix_cols = exchange(d_mixed.reshape(n * slices, rows, width)).reshape(n, slices, rows, width)
         dmix_cols = dmix_cols.transpose(1, 0, 2, 3).reshape(slices, width, width)
@@ -441,33 +443,41 @@
         d_lr = exchange(d_lr.transpose(2, 1, 0, 3, 4).reshape(n * slices, 2, rows, width))
         d_lr = d_lr.reshape(chans, templ, 2, rows, width).transpose(0, 2, 1, 3, 4)
         d_lr = d_lr.reshape(groups, 2 * per, count, width)
-        d_lr_spec = lr_spec
-
-    pair_grad, keep, send, done = call(
+        done = jnp.zeros((8, 2 * chans), F32)
+
+    pair_grad, keep, send = call(
         "back",
         functools.partial(back_kernel, blocks),
         (me, d_lr, fac, zn, d_gate, normed, rstd, wcat, layer_norm_gains),
-        [smem, d_lr_spec, fac_spec, cat_spec, cat_spec, cat_spec, one_spec, full((chans, 5 * chans)), gains_spec],
-        [rows_spec, full((half_rows, 2 * chans)), full((half_rows, 2 * chans)), full((16, 2 * chans))],
+        [smem, lr_spec, fac_spec, cat_spec, cat_spec, cat_spec, one_spec, full((chans, 5 * chans)), gains_spec],
+        [rows_spec, full((half_rows, 2 * chans)), full((half_rows, 2 * chans))],
         [
             jax.ShapeDtypeStruct((count, chans, width), BF16),
             array((half_rows, 2 * chans), F32),
             jax.ShapeDtypeStruct((half_rows, 2 * chans), F32),
-            array((16, 2 * chans), F32),
         ],
         [scratch, scratch, pltpu.VMEM((5 * chans, lanes), BF16), pltpu.VMEM((2 * chans + 8, 2 * chans), F32)],
     )
 
-    got = lax.ppermute(send, "row", [(d, d ^ 1) for d in range(n)])
+    partner = [(d, d ^ 1) for d in range(n)]
+    got = lax.ppermute(send, "row", partner)
     sums = pl.pallas_call(
         combine_kernel,
-        out_shape=jax.ShapeDtypeStruct((n, chans + 16, 2 * chans), BF16),
+        out_shape=jax.ShapeDtypeStruct((n // 2, half_rows, 2 * chans), BF16),
         compiler_params=params,
         name="combine",
     )(keep, got, done)
-    sums = exchange(sums)
+    sums = exchange(sums, [list(range(core, n, 2)) for core in range(2)])
+    mine, norms = pl.pallas_call(
+        total_kernel,
+        out_shape=[jax.ShapeDtypeStruct((chans + 2 * n, 2 * chans), F32), jax.ShapeDtypeStruct((8, 2 * chans), F32)],
+        compiler_params=params,
+        name="total",
+    )(sums)
+    got = lax.ppermute(mine, "row", partner)
     grad_proj, grad_out, norm_grads = pl.pallas_call(
         functools.partial(unpack_kernel, 1.0 / width, chans // n if direct else 0),
+        in_specs=[smem] + [whole] * 4,
         out_shape=[
             jax.ShapeDtypeStruct(w_proj.shape, F32),
             jax.ShapeDtypeStruct(w_out.shape, F32),
@@ -475,7 +485,7 @@
         ],
         compiler_params=params,
         name="unpack",
-    )(sums, done if direct else lax.psum(out_grads, "row"))
+    )(me, mine, got, norms, done if direct else lax.psum(out_grads[0], "row"))
     return pair_grad.reshape(pair.shape), grad_proj, grad_out, norm_grads
 
 

time: 92.8 us -> 89.6 us (0.966)
  blocking collectives: 82.4 us -> 77.8 us
  waiting for transfers between devices: 1.09 us -> 2.42 us
    all_to_all x5, blocking collectives: 82.4 us -> 77.8 us  [exchange(): lax.all_to_all(x, 'row', split_axis=0, concat_axis=0, axis_index_groups=g...]
    ppermute x1 -> x2, waiting for transfers between devices: 1.09 us -> 2.42 us  [the longest x1 1.22 us: per_device(): got = lax.ppermute(mine, 'row', partner)]
  transfers between devices with their start and end apart: 1 -> 2, of which waited for: 1 -> 2; matrix products, arithmetic and copies ran while one was open for 0% -> 0% of each run, Pallas kernels for 0% -> 0%
where the time goes in v3:
time: 89.6 us; the launch traced here: 89.3 us
  blocking collectives  77.8 us (87%)
  Pallas kernels  8.27 us (9%)
  waiting for transfers between devices  2.42 us (3%)
    all_to_all x5, blocking collectives, exchange(): lax.all_to_all(x, 'row', split_axis=0, concat_axis=0, axis_index_groups=g...  77.8 us
    pallas_call x3, Pallas kernels, call(): pl.pallas_call(kernel, grid=() if blocks == 1 else (blocks,), in_specs=in...  6.82 us
  transfers between devices with their start and end apart: 2, of which 2 were waited for; matrix products, arithmetic and copies ran while one was open for 0% of the time, Pallas kernels for 0%

profile of v3, /device:TPU:0, one launch (start us, length us, event | category | flops | bytes accessed | tf_op | source)
XLA Modules:
  0.0 89.3 jit_solution(17905513207362944380)
XLA Ops:
  0.6 0.0 copy-start.1
  0.6 0.0 copy-start
  0.7 3.5 %front.1 = (bf16[16,8,16,128]{3,2,1,0:T(8,128)(2,1)S(1)}, bf16[1,64,2048]{2,1,0:T(8,128)(2,1)S(1)}, f32[1,256,2048]{2,1,0:T(8,128)S(1)}, f32[1,64,2048]{2,1,0:T(...) custom-call(s32[1]{0:T(128)} %bitcast.me_ref, ...), custom_call_target="tpu_custom_call" | custom-call | tf_op jit(solution)/shard_map/front/pallas_call | solution.py:347
  4.2 21.7 %all_to_all.25.cols_ref = bf16[16,8,16,128]{3,2,1,0:T(8,128)(2,1)S(1)} all-to-all(bf16[16,8,16,128]{3,2,1,0:T(8,128)(2,1)S(1)} %get-tuple-element.28), channel_id=1, replica_groups=mesh['groups'=2,'row'=16] {'row'}, dimensions={0} | all-to-all | bytes 1048576 | tf_op jit(solution)/shard_map/all_to_all | solution.py:314
  25.8 0.3 mixed.1
  26.1 13.9 %all_to_all.26 = bf16[16,4,16,128]{3,2,1,0:T(8,128)(2,1)S(1)} all-to-all(bf16[16,4,16,128]{3,2,1,0:T(8,128)(2,1)S(1)} %get-tuple-element.29), channel_id=1, replica_groups=mesh['groups'=2,'row'=16] {'row'}, dimensions={0} | all-to-all | bytes 524288 | tf_op jit(solution)/shard_map/all_to_all | solution.py:314
  40.1 0.0 copy-done.1
  40.1 0.0 copy-done
  40.1 1.6 %middle.1 = (bf16[16,72,128]{2,1,0:T(8,128)(2,1)S(1)}, bf16[1,64,2048]{2,1,0:T(8,128)(2,1)S(1)}) custom-call(f32[2,64]{1,0:T(2,128)S(1)} %copy-done.1, bf16[64,16,128]{2,1,0:T(8,128)(2,1)S(1)} %bitcast.8, f32[64,16,128]{2,1,0:T(8,128)S(1)} %get-tuple-element.30.dout_ref, bf16[1,64,2048]{2,1,0:T(8,128)(2,1)S(1)} %get-tuple-element.31.zn_ref, ...), custom_call_target="tpu_custom_call" | custom-call | tf_op jit(solution)/shard_map/middle/pallas_call | solution.py:347
  41.7 13.3 %all_to_all.27.dmix_ref = bf16[16,72,128]{2,1,0:T(8,128)(2,1)S(1)} all-to-all(bf16[16,72,128]{2,1,0:T(8,128)(2,1)S(1)} %get-tuple-element.34), channel_id=1, replica_groups=mesh['groups'=2,'row'=16] {'row'}, dimensions={0} | all-to-all | bytes 589824 | tf_op jit(solution)/shard_map/all_to_all | solution.py:314
  55.0 0.3 triangle_back.1
  55.3 17.4 %all_to_all.28.dlr_ref = bf16[16,8,16,128]{3,2,1,0:T(8,128)(2,1)S(1)} all-to-all(bf16[16,8,16,128]{3,2,1,0:T(8,128)(2,1)S(1)} %get-tuple-element.37), channel_id=1, replica_groups=mesh['groups'=2,'row'=16] {'row'}, dimensions={0} | all-to-all | bytes 1048576 | tf_op jit(solution)/shard_map/all_to_all | solution.py:314
  72.7 1.8 %back.1 = (bf16[16,64,128]{2,1,0:T(8,128)(2,1)}, f32[72,128]{1,0:T(8,128)S(1)}, f32[72,128]{1,0:T(8,128)S(1)}) custom-call(s32[1]{0:T(128)} %bitcast.me_ref, bf16[16,8,16,128]{3,2,1,0:T(8,128)(2,1)S(1)} %all_to_all.28.dlr_ref, f32[1,256,2048]{2,1,0:T(8,128)S(1)} %get-tuple-element.38.fac_ref, bf16[1,64,2048]{2,1,0:T(8,128)(2,1)S(1)} %get-tuple-element.31.zn_ref, ...), custom_call_target="tpu_custom_call" | custom-call | tf_op jit(solution)/shard_map/back/pallas_call | solution.py:347
  74.5 0.0 collective-permute-start
  74.5 1.2 %collective-permute-done.got_ref = f32[72,128]{1,0:T(8,128)S(1)} collective-permute-done((f32[72,128]{1,0:T(8,128)S(1)}, f32[72,128]{1,0:T(8,128)S(1)}, u32[]{:S(2)}, u32[]{:S(2)}) %collective-permute-start) | collective-permute-done | bytes 36896 | tf_op jit(solution)/shard_map/ppermute | solution.py:463
  75.7 11.5 %all_to_all.29.pack_ref = bf16[8,72,128]{2,1,0:T(8,128)(2,1)S(1)} all-to-all(bf16[8,72,128]{2,1,0:T(8,128)(2,1)S(1)} %combine.1), channel_id=1, replica_groups={{0,2,4,6,8,10,12,14},{1,3,5,7,9,11,13,15},{16,18,20,22,24,26,28,30},{17..., dimensions={0} | all-to-all | bytes 294912 | tf_op jit(solution)/shard_map/all_to_all | solution.py:314
  87.2 0.1 collective-permute-start.1
  87.3 1.2 %collective-permute-done.1.got_ref = f32[96,128]{1,0:T(8,128)S(1)} collective-permute-done((f32[96,128]{1,0:T(8,128)S(1)}, f32[96,128]{1,0:T(8,128)S(1)}, u32[]{:S(2)}, u32[]{:S(2)}) %collective-permute-start.1) | collective-permute-done | bytes 49184 | tf_op jit(solution)/shard_map/ppermute | solution.py:477
  88.5 0.8 unpack.1
  (2 shorter events, 0.0 us)
Async XLA Ops:
  0.6 39.5 %copy-start.1 = (f32[2,64]{1,0:T(2,128)S(1)}, f32[2,64]{1,0:T(2,128)}, u32[]{:S(2)}) copy-start(f32[2,64]{1,0:T(2,128)} %gains_ref.5) | copy-start | bytes 1540
  0.6 39.4 %copy-start = (bf16[2,64,64]{2,1,0:T(8,128)(2,1)S(1)}, bf16[2,64,64]{2,1,0:T(8,128)(2,1)}, u32[]{:S(2)}) copy-start(bf16[2,64,64]{2,1,0:T(8,128)(2,1)} %wo_ref.3) | copy-start | bytes 49156
  74.5 1.2 %collective-permute-start = (f32[72,128]{1,0:T(8,128)S(1)}, f32[72,128]{1,0:T(8,128)S(1)}, u32[]{:S(2)}, u32[]{:S(2)}) collective-permute-start(f32[72,128]{1,0:T(8,128)S(1)} %get-tuple-element.45), channel_id=1, source_target_pairs={{0,1},{1,0},{2,3},{3,2},{4,5},{5,4},{6,7},{7,6},{8,9},{9,8},{10,11... | collective-permute-start | bytes 110600 | tf_op jit(solution)/shard_map/ppermute | solution.py:463
  87.2 1.3 %collective-permute-start.1 = (f32[96,128]{1,0:T(8,128)S(1)}, f32[96,128]{1,0:T(8,128)S(1)}, u32[]{:S(2)}, u32[]{:S(2)}) collective-permute-start(f32[96,128]{1,0:T(8,128)S(1)} %get-tuple-element.47.mine_ref), channel_id=1, source_target_pairs={{0,1},{1,0},{2,3},{3,2},{4,5},{5,4},{6,7},{7,6},{8,9},{9,8},{10,11... | collective-permute-start | bytes 147464 | tf_op jit(solution)/shard_map/ppermute | solution.py:477

commit v4 on v3

--- a/solution.py
+++ b/solution.py
@@ -72,19 +72,15 @@
     masks = mask_rows(me_ref, tokens_ref, cover_ref, tok_ref, block, rows)
     weights = jnp.concatenate([transposed(w_ref[p]) for p in range(4)] + [transposed(wo_ref[0])], axis=0)
     w_back = wo_ref[1]
-    for pos in range(0, count, 2):
-        span = slice(pos * LANES, (pos + 2) * LANES)
-        zn = []
-        for q in (pos, pos + 1):
-            normed, rstd = layer_norm(pair_ref[q].astype(F32))
-            lanes = slice(q * LANES, (q + 1) * LANES)
-            normed_ref[0, :, lanes] = normed
-            rstd_ref[0, :, lanes] = rstd
-            zn.append((normed * gain + bias).astype(BF16))
-        zn = jnp.concatenate(zn, axis=1)
-        zn_ref[0, :, span] = zn
-        pre = dot(weights, zn)
-        for j in range(2):
+    for q in range(count):
+        normed, rstd = layer_norm(pair_ref[q].astype(F32))
+        lanes = slice(q * LANES, (q + 1) * LANES)
+        normed_ref[0, :, lanes] = normed
+        rstd_ref[0, :, lanes] = rstd
+        zn_ref[0, :, lanes] = (normed * gain + bias).astype(BF16)
+    for pos in range(0, count, 8):
+        pre = dot(weights, zn_ref[0, :, pos * LANES:(pos + 8) * LANES])
+        for j in range(8):
             part = pre[:, j * LANES:(j + 1) * LANES]
             pre_p = [part[p * chans:(p + 1) * chans] for p in range(5)]
             mask = masks[pos + j]
@@ -101,9 +97,9 @@
             d_update = cot_ref[pos + j].astype(F32) * gate
             cg_ref[0, :, lanes] = d_update * (1.0 - gate)
             du_ref[0, :, lanes] = d_update.astype(BF16)
-        d_outn = dot(w_back, du_ref[0, :, span])
-        for j in range(2):
-            dout_scr[pl.ds(pos + j, chans, stride=count), :] = d_outn[:, j * LANES:(j + 1) * LANES]
+    d_outn = dot(w_back, du_ref[0])
+    for pos in range(count):
+        dout_scr[pl.ds(pos, chans, stride=count), :] = d_outn[:, pos * LANES:(pos + 1) * LANES]
     groups, both, _, _ = lr_ref.shape
     per = both // 2
     lr_ref[:, 0:per] = left_scr[...].astype(BF16).reshape(groups, per, count, LANES)
@@ -153,42 +149,35 @@
     return parts[0]
 
 
-def channel_sum(chans, value):
+def channel_sums(chans, values, scale):
     accs = [None] * 4
     for c in range(chans):
-        v = value(c)
-        accs[c % 4] = v if accs[c % 4] is None else accs[c % 4] + v
-    return tree_sum([a for a in accs if a is not None])
+        v = values(c)
+        accs[c % 4] = v if accs[c % 4] is None else [a + b for a, b in zip(accs[c % 4], v)]
+    return [tree_sum(list(parts)) * scale for parts in zip(*accs)]
 
 
 def middle_kernel(n, block, gains_ref, mixed_ref, dout_ref, zn_ref, cg_ref, du_ref, wo_ref, dmix_ref, dgate_ref, *rest_refs):
     *grads_refs, scr, norm_scr, outn_scr = rest_refs
     chans, count, _ = mixed_ref.shape
     inv = 1.0 / chans
-    mean = channel_sum(chans, lambda c: mixed_ref[c].astype(F32)) * inv
-    mean_h = channel_sum(chans, lambda c: dout_ref[c] * gains_ref[1, c]) * inv
-
-    def squares(c):
+    mean, mean_h = channel_sums(chans, lambda c: (mixed_ref[c].astype(F32), dout_ref[c] * gains_ref[1, c]), inv)
+
+    def moments(c):
         centred = mixed_ref[c].astype(F32) - mean
-        return centred * centred
-
-    rstd = lax.rsqrt(channel_sum(chans, squares) * inv + EPS)
-
-    def products(c):
+        return centred * centred, dout_ref[c] * gains_ref[1, c] * centred
+
+    variance, mean_p = channel_sums(chans, moments, inv)
+    rstd = lax.rsqrt(variance + EPS)
+    mean_p = mean_p * rstd
+    per = chans // n if n else 1
+    for c in range(chans):
         gain = gains_ref[1, c]
         xhat = (mixed_ref[c].astype(F32) - mean) * rstd
-        outn = xhat * gain
-        scr[c * count:(c + 1) * count, :] = outn
-        product = dout_ref[c] * xhat
-        norm_scr[c:c + 1, :] = jnp.sum(product, axis=0, keepdims=True)
-        return product * gain
-
-    mean_p = channel_sum(chans, products) * inv
-    for c in range(chans):
-        xhat = (mixed_ref[c].astype(F32) - mean) * rstd
-        d_mixed = (rstd * (dout_ref[c] * gains_ref[1, c] - mean_h - xhat * mean_p)).astype(BF16)
+        scr[c * count:(c + 1) * count, :] = xhat * gain
+        norm_scr[c:c + 1, :] = jnp.sum(dout_ref[c] * xhat, axis=0, keepdims=True)
+        d_mixed = (rstd * (dout_ref[c] * gain - mean_h - xhat * mean_p)).astype(BF16)
         if n:
-            per = chans // n
             dmix_ref[c // per, c % per * count:(c % per + 1) * count] = d_mixed
         else:
             dmix_ref[c] = d_mixed
@@ -206,10 +195,14 @@
         grads = jnp.concatenate([gate_grad, out_grad], axis=1)
         norm = jnp.concatenate([norm, jnp.zeros_like(norm)], axis=1)
         share = chans // n
-        rest = jnp.zeros((6 - share, 2 * chans), F32)
-        for d in range(n):
-            tile = jnp.concatenate([grads[d * share:(d + 1) * share], *split(norm), rest], axis=0)
-            dmix_ref[d, share * count:] = tile.astype(BF16)
+        scr[0:chans, :] = grads
+        tiles = pl.ds(chans, 8 * n)
+        scr[tiles, :] = jnp.zeros((8 * n, 2 * chans), F32)
+        for r in range(share):
+            scr[pl.ds(chans + r, n, stride=8), :] = scr[pl.ds(r, n, stride=share), :]
+        for r, row in enumerate(split(norm)):
+            scr[pl.ds(chans + share + r, n, stride=8), :] = jnp.broadcast_to(row, (n, 2 * chans))
+        dmix_ref[:, share * count:] = scr[tiles, :].reshape(n, 8, 2 * chans).astype(BF16)
         return
     grads_ref, = grads_refs
 
@@ -222,21 +215,38 @@
     grads_ref[chans:chans + 1, 0:chans] += norm
 
 
-def back_kernel(blocks, block, me_ref, dlr_ref, fac_ref, zn_ref, dgate_ref, normed_ref, rstd_ref, wcat_ref, gains_ref, pair_ref, keep_ref, send_ref, left_scr, right_scr, d_scr, pack_scr):
+def gating_back_kernel(blocks, block, me_ref, dlr_ref, fac_ref, zn_ref, d_ref, keep_ref, send_ref, left_scr, right_scr, pack_scr):
     groups, parts, count, _ = dlr_ref.shape
     per = parts // 2
     chans = groups * per
     left_scr[...] = dlr_ref[:, 0:per].astype(F32).reshape(chans * count, LANES)
-    right_scr[...] = dlr_ref[:, per:2 * per].astype(F32).reshape(chans * count, LANES)
-    d_scr[4 * chans:5 * chans, :] = dgate_ref[0]
+    right_scr[...] = dlr_ref[:, per:parts].astype(F32).reshape(chans * count, LANES)
     for pos in range(count):
         span = slice(pos * LANES, (pos + 1) * LANES)
         where = pl.ds(pos, chans, stride=count)
         d_left, d_right = left_scr[where, :], right_scr[where, :]
         for p in range(4):
             d = d_left if p < 2 else d_right
-            d_scr[p * chans:(p + 1) * chans, span] = (d * fac_ref[0, p * chans:(p + 1) * chans, span]).astype(BF16)
-    d_zn = dot(wcat_ref[...], d_scr[...])
+            d_ref[0, p * chans:(p + 1) * chans, span] = (d * fac_ref[0, p * chans:(p + 1) * chans, span]).astype(BF16)
+    grads = dot_nt(zn_ref[0], d_ref[0])
+
+    @pl.when(block() == 0)
+    def _():
+        pack_scr[...] = jnp.zeros_like(pack_scr)
+
+    pack_scr[0:chans, :] += grads[:, 0:2 * chans]
+    pack_scr[chans:2 * chans, :] += grads[:, 2 * chans:4 * chans]
+
+    @pl.when(block() == blocks - 1)
+    def _():
+        half = me_ref[0] % 2
+        keep_ref[...] = pack_scr[pl.ds(pl.multiple_of(half * chans, 8), chans), :]
+        send_ref[...] = pack_scr[pl.ds(pl.multiple_of((1 - half) * chans, 8), chans), :]
+
+
+def pair_grad_kernel(block, d_ref, dgate_ref, normed_ref, rstd_ref, wcat_ref, gains_ref, pair_ref, norm_ref):
+    chans, count = normed_ref.shape[1], normed_ref.shape[2] // LANES
+    d_zn = dot(wcat_ref[:, 0:4 * chans], d_ref[0]) + dot(wcat_ref[:, 4 * chans:5 * chans], dgate_ref[0])
     gain = column(gains_ref[0:1, :])
     for pos in range(count):
         span = slice(pos * LANES, (pos + 1) * LANES)
@@ -245,50 +255,33 @@
         mean_h = jnp.mean(h, axis=0, keepdims=True)
         mean_p = jnp.mean(h * normed, axis=0, keepdims=True)
         pair_ref[pos] = (rstd_ref[0, :, span] * (h - mean_h - normed * mean_p)).astype(BF16)
-    grads = dot_nt(zn_ref[0], d_scr[0:4 * chans, :])
-    bias_grad = as_row(jnp.sum(d_zn, axis=1, keepdims=True))
-    gain_grad = as_row(jnp.sum(d_zn * normed_ref[0], axis=1, keepdims=True))
 
     @pl.when(block() == 0)
     def _():
-        pack_scr[...] = jnp.zeros_like(pack_scr)
-
-    pack_scr[0:chans, :] += grads[:, 0:2 * chans]
-    pack_scr[chans:2 * chans, :] += grads[:, 2 * chans:4 * chans]
-    pack_scr[2 * chans:2 * chans + 1, 0:chans] += gain_grad
-    pack_scr[2 * chans + 1:2 * chans + 2, 0:chans] += bias_grad
-
-    @pl.when(block() == blocks - 1)
-    def _():
-        half = me_ref[0] % 2
-        own = pl.multiple_of(half * chans, 8)
-        other = pl.multiple_of((1 - half) * chans, 8)
-        keep_ref[0:chans, :] = pack_scr[pl.ds(own, chans), :]
-        send_ref[0:chans, :] = pack_scr[pl.ds(other, chans), :]
-        keep_ref[chans:chans + 8, :] = pack_scr[2 * chans:2 * chans + 8, :]
-        send_ref[chans:chans + 8, :] = pack_scr[2 * chans:2 * chans + 8, :]
-
-
-def combine_kernel(keep_ref, got_ref, done_ref, out_ref):
-    rows = keep_ref.shape[0] - 8
-    total = keep_ref[...] + got_ref[...]
-    tile = jnp.concatenate([done_ref[0:4, :], *split(total[rows:rows + 2])], axis=0)
-    block = jnp.concatenate([total[0:rows], tile], axis=0).astype(BF16)
+        norm_ref[...] = jnp.zeros_like(norm_ref)
+
+    norm_ref[0:1, 0:chans] += as_row(jnp.sum(d_zn * normed_ref[0], axis=1, keepdims=True))
+    norm_ref[1:2, 0:chans] += as_row(jnp.sum(d_zn, axis=1, keepdims=True))
+
+
+def combine_kernel(keep_ref, got_ref, done_ref, norm_ref, out_ref):
+    tile = jnp.concatenate([done_ref[0:4, :], *split(norm_ref[0:2, :])], axis=0)
+    block = jnp.concatenate([keep_ref[...] + got_ref[...], tile], axis=0).astype(BF16)
     for d in range(out_ref.shape[0]):
         out_ref[d] = block
 
 
-def total_kernel(pack_ref, mine_ref, norm_ref):
+def total_kernel(pack_ref, mine_ref):
     chips, length, _ = pack_ref.shape
     rows = length - 8
     mine_ref[0:rows, :] = tree_sum([pack_ref[d, 0:rows, :].astype(F32) for d in range(chips)])
     tiles = [pack_ref[d, rows:, :].astype(F32) for d in range(chips)]
     for d in range(0, chips, 2):
         mine_ref[rows + 4 * d:rows + 4 * d + 8, :] = jnp.concatenate([tiles[d][0:4], tiles[d + 1][0:4]], axis=0)
-    norm_ref[...] = tree_sum(tiles)
-
-
-def unpack_kernel(scale, share, me_ref, mine_ref, got_ref, norm_ref, done_ref, proj_ref, out_ref, norms_ref):
+    mine_ref[rows + 4 * chips:, :] = tree_sum(tiles)
+
+
+def unpack_kernel(scale, share, me_ref, mine_ref, got_ref, done_ref, proj_ref, out_ref, norms_ref):
     chans = proj_ref.shape[1]
     odd = me_ref[0] % 2 == 1
     mine, got = mine_ref[...] * scale, got_ref[...] * scale
@@ -296,7 +289,8 @@
     for half in range(2):
         proj_ref[2 * half] = even_odd[half][0:chans, 0:chans]
         proj_ref[2 * half + 1] = even_odd[half][0:chans, chans:2 * chans]
-    norms_ref[0:2, :] = (norm_ref[4:6, 0:chans] + norm_ref[6:8, 0:chans]) * scale
+    norm = (mine + got)[mine.shape[0] - 4:, 0:chans]
+    norms_ref[0:2, :] = norm[0:2] + norm[2:4]
     if share:
         norms_ref[2:3, :] = (done_ref[share:share + 1, 0:chans] + done_ref[share + 1:share + 2, 0:chans]) * scale
         for d in range(chans // share):
@@ -368,7 +362,6 @@
     cot_rows = from_hbm(cotangent.reshape(count, chans, width))
     w_proj_in, w_out_in, gains_in = from_hbm(w_proj), from_hbm(w_out), from_hbm(layer_norm_gains)
     tokens_in, cover_in = from_hbm(tokens_row), from_hbm(coverage.transpose(1, 2, 0))
-    half_rows = chans + 8
 
     def cat(dtype):
         return array((blocks, chans, lanes), dtype)
@@ -445,39 +438,49 @@
         d_lr = d_lr.reshape(groups, 2 * per, count, width)
         done = jnp.zeros((8, 2 * chans), F32)
 
-    pair_grad, keep, send = call(
-        "back",
-        functools.partial(back_kernel, blocks),
-        (me, d_lr, fac, zn, d_gate, normed, rstd, wcat, layer_norm_gains),
-        [smem, lr_spec, fac_spec, cat_spec, cat_spec, cat_spec, one_spec, full((chans, 5 * chans)), gains_spec],
-        [rows_spec, full((half_rows, 2 * chans)), full((half_rows, 2 * chans))],
+    d_spec = block_spec((1, 4 * chans, lanes), lambda b: (b, 0, 0))
+    d_pre, keep, send = call(
+        "gating_back",
+        functools.partial(gating_back_kernel, blocks),
+        (me, d_lr, fac, zn),
+        [smem, lr_spec, fac_spec, cat_spec],
+        [d_spec, full((chans, 2 * chans)), full((chans, 2 * chans))],
         [
-            jax.ShapeDtypeStruct((count, chans, width), BF16),
-            array((half_rows, 2 * chans), F32),
-            jax.ShapeDtypeStruct((half_rows, 2 * chans), F32),
+            array((blocks, 4 * chans, lanes), BF16),
+            array((chans, 2 * chans), F32),
+            jax.ShapeDtypeStruct((chans, 2 * chans), F32),
         ],
-        [scratch, scratch, pltpu.VMEM((5 * chans, lanes), BF16), pltpu.VMEM((2 * chans + 8, 2 * chans), F32)],
+        [scratch, scratch, pltpu.VMEM((2 * chans, 2 * chans), F32)],
+    )
+
+    pair_grad, norm_rows = call(
+        "pair_grad",
+        pair_grad_kernel,
+        (d_pre, d_gate, normed, rstd, wcat, layer_norm_gains),
+        [d_spec, cat_spec, cat_spec, one_spec, full((chans, 5 * chans)), gains_spec],
+        [rows_spec, full((8, 2 * chans))],
+        [jax.ShapeDtypeStruct((count, chans, width), BF16), array((8, 2 * chans), F32)],
     )
 
     partner = [(d, d ^ 1) for d in range(n)]
     got = lax.ppermute(send, "row", partner)
     sums = pl.pallas_call(
         combine_kernel,
-        out_shape=jax.ShapeDtypeStruct((n // 2, half_rows, 2 * chans), BF16),
+        out_shape=jax.ShapeDtypeStruct((n // 2, chans + 8, 2 * chans), BF16),
         compiler_params=params,
         name="combine",
-    )(keep, got, done)
+    )(keep, got, done, norm_rows)
     sums = exchange(sums, [list(range(core, n, 2)) for core in range(2)])
-    mine, norms = pl.pallas_call(
+    mine = pl.pallas_call(
         total_kernel,
-        out_shape=[jax.ShapeDtypeStruct((chans + 2 * n, 2 * chans), F32), jax.ShapeDtypeStruct((8, 2 * chans), F32)],
+        out_shape=jax.ShapeDtypeStruct((chans + 2 * n + 8, 2 * chans), F32),
         compiler_params=params,
         name="total",
     )(sums)
     got = lax.ppermute(mine, "row", partner)
     grad_proj, grad_out, norm_grads = pl.pallas_call(
         functools.partial(unpack_kernel, 1.0 / width, chans // n if direct else 0),
-        in_specs=[smem] + [whole] * 4,
+        in_specs=[smem] + [whole] * 3,
         out_shape=[
             jax.ShapeDtypeStruct(w_proj.shape, F32),
             jax.ShapeDtypeStruct(w_out.shape, F32),
@@ -485,7 +488,7 @@
         ],
         compiler_params=params,
         name="unpack",
-    )(me, mine, got, norms, done if direct else lax.psum(out_grads[0], "row"))
+    )(me, mine, got, done if direct else lax.psum(out_grads[0], "row"))
     return pair_grad.reshape(pair.shape), grad_proj, grad_out, norm_grads
 
 

time: 89.6 us -> 88 us (0.982)
  waiting for transfers between devices: 2.42 us -> 1.23 us
    ppermute x1, waiting for transfers between devices: 1.2 us -> 0.01 us  [per_device(): got = lax.ppermute(send, 'row', partner)]
    pallas_call x3 -> x4, Pallas kernels: 6.82 us -> 6.14 us  [call(): pl.pallas_call(kernel, grid=() if blocks == 1 else (blocks,), in_specs=in...]
  transfers between devices with their start and end apart: 2 -> 2, of which waited for: 2 -> 1; matrix products, arithmetic and copies ran while one was open for 0% -> 0% of each run, Pallas kernels for 0% -> 1%
where the time goes in v4:
time: 88 us; the launch traced here: 87.7 us
  blocking collectives  78 us (89%)
  Pallas kernels  7.59 us (9%)
  waiting for transfers between devices  1.23 us (1%)
    all_to_all x5, blocking collectives, exchange(): lax.all_to_all(x, 'row', split_axis=0, concat_axis=0, axis_index_groups=g...  78 us
    pallas_call x4, Pallas kernels, call(): pl.pallas_call(kernel, grid=() if blocks == 1 else (blocks,), in_specs=in...  6.14 us
  transfers between devices with their start and end apart: 2, of which 1 were waited for; matrix products, arithmetic and copies ran while one was open for 0% of the time, Pallas kernels for 1%

profile of v4, /device:TPU:0, one launch (start us, length us, event | category | flops | bytes accessed | tf_op | source)
XLA Modules:
  0.0 87.7 jit_solution(13924138261702596729)
XLA Ops:
  0.6 0.0 copy-start.1
  0.6 0.0 copy-start
  0.7 2.4 %front.1 = (bf16[16,8,16,128]{3,2,1,0:T(8,128)(2,1)S(1)}, bf16[1,64,2048]{2,1,0:T(8,128)(2,1)S(1)}, f32[1,256,2048]{2,1,0:T(8,128)S(1)}, f32[1,64,2048]{2,1,0:T(...) custom-call(s32[1]{0:T(128)} %bitcast.me_ref, ...), custom_call_target="tpu_custom_call" | custom-call | tf_op jit(solution)/shard_map/front/pallas_call | solution.py:341
  3.1 21.7 %all_to_all.25.cols_ref = bf16[16,8,16,128]{3,2,1,0:T(8,128)(2,1)S(1)} all-to-all(bf16[16,8,16,128]{3,2,1,0:T(8,128)(2,1)S(1)} %get-tuple-element.28), channel_id=1, replica_groups=mesh['groups'=2,'row'=16] {'row'}, dimensions={0} | all-to-all | bytes 1048576 | tf_op jit(solution)/shard_map/all_to_all | solution.py:308
  24.7 0.3 mixed.1
  25.0 13.9 %all_to_all.26 = bf16[16,4,16,128]{3,2,1,0:T(8,128)(2,1)S(1)} all-to-all(bf16[16,4,16,128]{3,2,1,0:T(8,128)(2,1)S(1)} %get-tuple-element.29), channel_id=1, replica_groups=mesh['groups'=2,'row'=16] {'row'}, dimensions={0} | all-to-all | bytes 524288 | tf_op jit(solution)/shard_map/all_to_all | solution.py:308
  39.0 0.0 copy-done.1
  39.0 0.0 copy-done
  39.0 1.6 %middle.1 = (bf16[16,72,128]{2,1,0:T(8,128)(2,1)S(1)}, bf16[1,64,2048]{2,1,0:T(8,128)(2,1)S(1)}) custom-call(f32[2,64]{1,0:T(2,128)S(1)} %copy-done.1, bf16[64,16,128]{2,1,0:T(8,128)(2,1)S(1)} %bitcast.8, f32[64,16,128]{2,1,0:T(8,128)S(1)} %get-tuple-element.30.dout_ref, bf16[1,64,2048]{2,1,0:T(8,128)(2,1)S(1)} %get-tuple-element.31.zn_ref, ...), custom_call_target="tpu_custom_call" | custom-call | tf_op jit(solution)/shard_map/middle/pallas_call | solution.py:341
  40.6 13.3 %all_to_all.27.dmix_ref = bf16[16,72,128]{2,1,0:T(8,128)(2,1)S(1)} all-to-all(bf16[16,72,128]{2,1,0:T(8,128)(2,1)S(1)} %get-tuple-element.34), channel_id=1, replica_groups=mesh['groups'=2,'row'=16] {'row'}, dimensions={0} | all-to-all | bytes 589824 | tf_op jit(solution)/shard_map/all_to_all | solution.py:308
  53.9 0.3 triangle_back.1
  54.3 17.4 %all_to_all.28.dlr_ref = bf16[16,8,16,128]{3,2,1,0:T(8,128)(2,1)S(1)} all-to-all(bf16[16,8,16,128]{3,2,1,0:T(8,128)(2,1)S(1)} %get-tuple-element.37), channel_id=1, replica_groups=mesh['groups'=2,'row'=16] {'row'}, dimensions={0} | all-to-all | bytes 1048576 | tf_op jit(solution)/shard_map/all_to_all | solution.py:308
  71.6 1.0 %gating_back.1 = (bf16[1,256,2048]{2,1,0:T(8,128)(2,1)S(1)}, f32[64,128]{1,0:T(8,128)S(1)}, f32[64,128]{1,0:T(8,128)S(1)}) custom-call(s32[1]{0:T(128)} %bitcast.me_ref, bf16[16,8,16,128]{3,2,1,0:T(8,128)(2,1)S(1)} %all_to_all.28.dlr_ref, f32[1,256,2048]{2,1,0:T(8,128)S(1)} %get-tuple-element.38.fac_ref, bf16[1,64,2048]{2,1,0:T(8,128)(2,1)S(1)} %get-tuple-element.31.zn_ref), custom_call_target="tpu_custom_call" | custom-call | tf_op jit(solution)/shard_map/gating_back/pallas_call | solution.py:341
  72.6 0.1 collective-permute-start
  72.7 1.2 %pair_grad.1 = (bf16[16,64,128]{2,1,0:T(8,128)(2,1)}, f32[8,128]{1,0:T(8,128)S(1)}) custom-call(bf16[1,256,2048]{2,1,0:T(8,128)(2,1)S(1)} %get-tuple-element.39.d_ref, bf16[1,64,2048]{2,1,0:T(8,128)(2,1)S(1)} %get-tuple-element.40.dgate_ref, f32[1,64,2048]{2,1,0:T(8,128)S(1)} %get-tuple-element.41.normed_ref, f32[1,1,2048]{2,1,0:T(1,128)S(1)} %get-tuple-element.42.rstd_ref, ...), custom_call_target="tpu_custom_call" | custom-call | tf_op jit(solution)/shard_map/pair_grad/pallas_call | solution.py:341
  73.9 0.0 collective-permute-done.got_ref
  73.9 11.7 %all_to_all.29.pack_ref = bf16[8,72,128]{2,1,0:T(8,128)(2,1)S(1)} all-to-all(bf16[8,72,128]{2,1,0:T(8,128)(2,1)S(1)} %combine.1), channel_id=1, replica_groups={{0,2,4,6,8,10,12,14},{1,3,5,7,9,11,13,15},{16,18,20,22,24,26,28,30},{17..., dimensions={0} | all-to-all | bytes 294912 | tf_op jit(solution)/shard_map/all_to_all | solution.py:308
  85.6 0.1 collective-permute-start.1
  85.7 1.2 %collective-permute-done.1.got_ref = f32[104,128]{1,0:T(8,128)S(1)} collective-permute-done((f32[104,128]{1,0:T(8,128)S(1)}, f32[104,128]{1,0:T(8,128)S(1)}, u32[]{:S(2)}, u32[]{:S(2)}) %collective-permute-start.1) | collective-permute-done | bytes 53280 | tf_op jit(solution)/shard_map/ppermute | solution.py:480
  86.9 0.8 unpack.1
  (2 shorter events, 0.0 us)
Async XLA Ops:
  0.6 38.4 %copy-start.1 = (f32[2,64]{1,0:T(2,128)S(1)}, f32[2,64]{1,0:T(2,128)}, u32[]{:S(2)}) copy-start(f32[2,64]{1,0:T(2,128)} %gains_ref.5) | copy-start | bytes 1540
  0.6 38.4 %copy-start = (bf16[2,64,64]{2,1,0:T(8,128)(2,1)S(1)}, bf16[2,64,64]{2,1,0:T(8,128)(2,1)}, u32[]{:S(2)}) copy-start(bf16[2,64,64]{2,1,0:T(8,128)(2,1)} %wo_ref.3) | copy-start | bytes 49156
  72.6 1.3 %collective-permute-start = (f32[64,128]{1,0:T(8,128)S(1)}, f32[64,128]{1,0:T(8,128)S(1)}, u32[]{:S(2)}, u32[]{:S(2)}) collective-permute-start(f32[64,128]{1,0:T(8,128)S(1)} %get-tuple-element.46), channel_id=1, source_target_pairs={{0,1},{1,0},{2,3},{3,2},{4,5},{5,4},{6,7},{7,6},{8,9},{9,8},{10,11... | collective-permute-start | bytes 98312 | tf_op jit(solution)/shard_map/ppermute | solution.py:466
  85.6 1.3 %collective-permute-start.1 = (f32[104,128]{1,0:T(8,128)S(1)}, f32[104,128]{1,0:T(8,128)S(1)}, u32[]{:S(2)}, u32[]{:S(2)}) collective-permute-start(f32[104,128]{1,0:T(8,128)S(1)} %total.1.mine_ref), channel_id=1, source_target_pairs={{0,1},{1,0},{2,3},{3,2},{4,5},{5,4},{6,7},{7,6},{8,9},{9,8},{10,11... | collective-permute-start | bytes 159752 | tf_op jit(solution)/shard_map/ppermute | solution.py:480

commit v5 on v4

v5 whole, which is shorter than its diff:
```python
import functools

import jax
import jax.numpy as jnp
from jax import lax
from jax.experimental import pallas as pl
from jax.experimental.pallas import tpu as pltpu
from jax.sharding import PartitionSpec as P

EPS = 1e-05
LANES = 128
F32 = jnp.float32
BF16 = jnp.bfloat16


def dot(a, b):
    return jnp.dot(a, b, preferred_element_type=F32)


def dot_nt(a, b):
    return lax.dot_general(a, b, (((1,), (1,)), ((), ())), preferred_element_type=F32)


def dot_tn(a, b):
    return lax.dot_general(a, b, (((0,), (0,)), ((), ())), preferred_element_type=F32)


def transposed(weight):
    return weight.astype(F32).T.astype(BF16)


def column(row):
    n = row.shape[1]
    eye = lax.broadcasted_iota(jnp.int32, (n, n), 0) == lax.broadcasted_iota(jnp.int32, (n, n), 1)
    return jnp.sum(jnp.where(eye, row, 0.0), axis=1, keepdims=True)


def as_row(col):
    n = col.shape[0]
    eye = lax.broadcasted_iota(jnp.int32, (n, n), 0) == lax.broadcasted_iota(jnp.int32, (n, n), 1)
    return jnp.sum(jnp.where(eye, col, 0.0), axis=0, keepdims=True)


def layer_norm(x):
    mean = jnp.mean(x, axis=0, keepdims=True)
    centred = x - mean
    rstd = lax.rsqrt(jnp.mean(centred * centred, axis=0, keepdims=True) + EPS)
    return centred * rstd, rstd


def mask_rows(me_ref, tokens_ref, cover_ref, tok_ref, block, rows):
    width, (tiles, _, templ) = tokens_ref.shape[1], cover_ref.shape
    tile = width // tiles
    first = me_ref[0] * rows
    here = lax.broadcasted_iota(jnp.int32, (rows, width), 0) + first == lax.broadcasted_iota(jnp.int32, (rows, width), 1)
    row_mask = jnp.sum(jnp.where(here, tokens_ref[...].astype(F32), 0.0), axis=1, keepdims=True)
    column_mask = tok_ref[...].astype(F32)
    cover = cover_ref[first // tile].astype(F32)
    here = lax.broadcasted_iota(jnp.int32, (tiles, templ), 0) == block() * LANES // tile
    cover = jnp.sum(jnp.where(here, cover, 0.0), axis=0, keepdims=True)
    out = []
    for t in range(templ):
        masked = column_mask * cover[:, t:t + 1]
        out += [masked * row_mask[r:r + 1, :] for r in range(rows)]
    return out


def project_kernel(rows, chips, block, me_ref, tokens_ref, cover_ref, pair_ref, tok_ref, w_ref, gains_ref, bias_ref, *refs):
    *out_refs, zn_ref, fac_ref, normed_ref, rstd_ref, left_scr, right_scr = refs
    count, chans, _ = pair_ref.shape
    gain, bias = column(gains_ref[0:1, :]), column(bias_ref[...])
    masks = mask_rows(me_ref, tokens_ref, cover_ref, tok_ref, block, rows)
    weights = jnp.concatenate([transposed(w_ref[p]) for p in range(4)], axis=0)
    for q in range(count):
        normed, rstd = layer_norm(pair_ref[q].astype(F32))
        lanes = slice(q * LANES, (q + 1) * LANES)
        normed_ref[0, :, lanes] = normed
        rstd_ref[0, :, lanes] = rstd
        zn_ref[0, :, lanes] = (normed * gain + bias).astype(BF16)
    step = 8
    for pos in range(0, count, step):
        pre = dot(weights, zn_ref[0, :, pos * LANES:(pos + step) * LANES])
        for j in range(step):
            part = pre[:, j * LANES:(j + 1) * LANES]
            pre_p = [part[p * chans:(p + 1) * chans] for p in range(4)]
            mask = masks[pos + j]
            where = pl.ds(pos + j, chans, stride=count)
            lanes = slice((pos + j) * LANES, (pos + j + 1) * LANES)
            for p, scr in ((0, left_scr), (2, right_scr)):
                sig = jax.nn.sigmoid(pre_p[p])
                sig_mask = sig * mask
                both = sig_mask * pre_p[p + 1]
                scr[where, :] = both
                fac_ref[0, p * chans:(p + 1) * chans, lanes] = both * (1.0 - sig)
                fac_ref[0, (p + 1) * chans:(p + 2) * chans, lanes] = sig_mask
    if chips:
        per = chans // chips
        for k in range(chips):
            here = pl.ds(partner_chip(me_ref, k) * (per * count), per * count)
            out_refs[k][0:per] = left_scr[here, :].astype(BF16).reshape(per, count, LANES)
            out_refs[k][per:2 * per] = right_scr[here, :].astype(BF16).reshape(per, count, LANES)
        return
    lr_ref, = out_refs
    lr_ref[:, 0] = left_scr[...].astype(BF16).reshape(chans, count, LANES)
    lr_ref[:, 1] = right_scr[...].astype(BF16).reshape(chans, count, LANES)


def prepare_kernel(block, cot_ref, zn_ref, w_ref, wo_ref, cg_ref, du_ref, dout_ref, wcat_ref, scr):
    count, chans, _ = cot_ref.shape
    wcat_ref[...] = jnp.concatenate([w_ref[0], w_ref[1], w_ref[2], w_ref[3], wo_ref[0]], axis=1)
    gates = jax.nn.sigmoid(dot(transposed(wo_ref[0]), zn_ref[0]))
    for pos in range(count):
        lanes = slice(pos * LANES, (pos + 1) * LANES)
        gate = gates[:, lanes]
        d_update = cot_ref[pos].astype(F32) * gate
        cg_ref[0, :, lanes] = d_update * (1.0 - gate)
        du_ref[0, :, lanes] = d_update.astype(BF16)
    d_outn = dot(wo_ref[1], du_ref[0])
    for pos in range(count):
        scr[pl.ds(pos, chans, stride=count), :] = d_outn[:, pos * LANES:(pos + 1) * LANES]
    dout_ref[...] = scr[...].reshape(chans, count, LANES)


def partner_chip(me_ref, k):
    return jnp.bitwise_xor(me_ref[0] // 2, k)


def collect_kernel(after_ref, *refs):
    *in_refs, out_ref = refs
    per = out_ref.shape[1]
    for k, ref in enumerate(in_refs):
        out_ref[k] = ref[per:2 * per]


def slice_rows(values, t, rows):
    chips, _, width = values.shape
    return values[:, t * rows:(t + 1) * rows].reshape(chips * rows, width).astype(BF16)


def mixed_kernel(rows, chips, me_ref, *refs):
    cols_refs, (own_ref, got_ref, out_ref, left_ref, right_ref, scr) = refs[:chips], refs[chips:]
    per, count, width = own_ref.shape[1:]
    templ, core = count // rows, me_ref[0] % 2
    for c in range(per):
        left_all = jnp.stack([ref[c].astype(F32) for ref in cols_refs])
        own, got = own_ref[:, c].astype(F32), got_ref[:, c].astype(F32)
        parts = []
        for t in range(templ):
            s = c * templ + t
            left = slice_rows(left_all, t, rows)
            left_ref[s] = left
            for k in range(chips):
                chip = partner_chip(me_ref, k)
                for values, half in ((own, core), (got, 1 - core)):
                    start = pl.multiple_of((chip * 2 + half) * rows, rows)
                    scr[s, pl.ds(start, rows), :] = values[k, t * rows:(t + 1) * rows]
            right = scr[s].astype(BF16)
            right_ref[s] = right
            parts.append(dot_nt(left, right).reshape(chips, rows, width))
        mixed = jnp.concatenate(parts, axis=1).astype(BF16)
        for k in range(chips):
            out_ref[partner_chip(me_ref, k), c] = mixed[k]


def triangle_back_kernel(rows, me_ref, dmix_ref, left_ref, right_ref, d_left_ref, keep_ref, send_ref, scr):
    chips, per, count, width = d_left_ref.shape
    templ, core = count // rows, me_ref[0] % 2
    for c in range(per):
        dmix_all = jnp.stack([dmix_ref[partner_chip(me_ref, k), c].astype(F32) for k in range(chips)])
        parts = []
        for t in range(templ):
            s = c * templ + t
            dmix = slice_rows(dmix_all, t, rows)
            parts.append(dot(dmix, right_ref[s]).reshape(chips, rows, width))
            scr[s] = dot_tn(dmix, left_ref[s])
        d_left_ref[:, c] = jnp.concatenate(parts, axis=1).astype(BF16)
    for k in range(chips):
        chip = partner_chip(me_ref, k)
        for ref, half in ((keep_ref, core), (send_ref, 1 - core)):
            here = pl.ds(pl.multiple_of((chip * 2 + half) * rows, rows), rows)
            for c in range(per):
                both = jnp.concatenate([scr[c * templ + t, here, :] for t in range(templ)], axis=0)
                ref[k, c] = both.astype(ref.dtype)


def join_kernel(d_left_ref, keep_ref, got_ref, *out_refs):
    chips, per, _, _ = d_left_ref.shape
    for k in range(chips):
        out_refs[k][0:per] = d_left_ref[k]
        out_refs[k][per:2 * per] = (keep_ref[k] + got_ref[k].astype(F32)).astype(BF16)


def split(x):
    high = x.astype(BF16).astype(F32)
    return high, x - high


def tree_sum(parts):
    while len(parts) > 1:
        parts = [a + b for a, b in zip(parts[::2], parts[1::2])] + parts[len(parts) // 2 * 2:]
    return parts[0]


def channel_sums(chans, values, scale):
    accs = [None] * 4
    for c in range(chans):
        v = values(c)
        accs[c % 4] = v if accs[c % 4] is None else [a + b for a, b in zip(accs[c % 4], v)]
    return [tree_sum(list(parts)) * scale for parts in zip(*accs)]


def middle_kernel(block, gains_ref, dout_ref, mixed_ref, dmix_ref, outn_ref, norm_ref):
    chans = dout_ref.shape[0]
    inv = 1.0 / chans

    def mixed(c):
        return mixed_ref[c].astype(F32)

    def scaled(c):
        return dout_ref[c] * gains_ref[1, c]

    mean, mean_h = channel_sums(chans, lambda c: (mixed(c), scaled(c)), inv)

    def moments(c):
        centred = mixed(c) - mean
        return centred * centred, scaled(c) * centred

    variance, mean_p = channel_sums(chans, moments, inv)
    rstd = lax.rsqrt(variance + EPS)
    mean_p = mean_p * rstd

    @pl.when(block() == 0)
    def _():
        norm_ref[...] = jnp.zeros_like(norm_ref)

    for c in range(chans):
        xhat = (mixed(c) - mean) * rstd
        outn_ref[c] = xhat * gains_ref[1, c]
        norm_ref[c:c + 1, :] += jnp.sum(dout_ref[c] * xhat, axis=0, keepdims=True)
        dmix_ref[c] = (rstd * (scaled(c) - mean_h - xhat * mean_p)).astype(BF16)


def update_kernel(block, outn_ref, norm_ref, zn_ref, cg_ref, du_ref, wo_ref, dgate_ref, grads_ref, scr, outn_scr):
    chans, count, _ = outn_ref.shape
    scr[...] = outn_ref[...].reshape(chans * count, LANES)
    for pos in range(count):
        span = slice(pos * LANES, (pos + 1) * LANES)
        outn_scr[:, span] = scr[pl.ds(pos, chans, stride=count), :].astype(BF16)
    update = dot(transposed(wo_ref[1]), outn_scr[...])
    d_gate = (cg_ref[0] * update).astype(BF16)
    dgate_ref[0] = d_gate
    gate_grad = dot_nt(zn_ref[0], d_gate)
    out_grad = dot_nt(outn_scr[...], du_ref[0])

    @pl.when(block() == 0)
    def _():
        grads_ref[...] = jnp.zeros_like(grads_ref)

    grads_ref[0:chans, 0:chans] += gate_grad
    grads_ref[0:chans, chans:2 * chans] += out_grad
    grads_ref[chans:chans + 1, 0:chans] = as_row(jnp.sum(norm_ref[...], axis=1, keepdims=True))


def gating_back_kernel(blocks, chips, block, me_ref, fac_ref, zn_ref, grads_ref, *refs):
    *in_refs, d_ref, keep_ref, send_ref, left_scr, right_scr, pack_scr = refs
    chans = zn_ref.shape[1]
    count = left_scr.shape[0] // chans
    if chips:
        per = chans // chips
        for k in range(chips):
            here = pl.ds(partner_chip(me_ref, k) * (per * count), per * count)
            left_scr[here, :] = in_refs[k][0:per].astype(F32).reshape(per * count, LANES)
            right_scr[here, :] = in_refs[k][per:2 * per].astype(F32).reshape(per * count, LANES)
    else:
        left_scr[...] = in_refs[0][:, 0].astype(F32).reshape(chans * count, LANES)
        right_scr[...] = in_refs[0][:, 1].astype(F32).reshape(chans * count, LANES)
    for pos in range(count):
        span = slice(pos * LANES, (pos + 1) * LANES)
        where = pl.ds(pos, chans, stride=count)
        d_left, d_right = left_scr[where, :], right_scr[where, :]
        for p in range(4):
            d = d_left if p < 2 else d_right
            d_ref[0, p * chans:(p + 1) * chans, span] = (d * fac_ref[0, p * chans:(p + 1) * chans, span]).astype(BF16)
    grads = dot_nt(zn_ref[0], d_ref[0])

    @pl.when(block() == 0)
    def _():
        pack_scr[...] = jnp.zeros_like(pack_scr)

    pack_scr[0:chans, :] += grads[:, 0:2 * chans]
    pack_scr[chans:2 * chans, :] += grads[:, 2 * chans:4 * chans]

    @pl.when(block() == blocks - 1)
    def _():
        for ref, half in ((keep_ref, me_ref[0] % 2), (send_ref, 1 - me_ref[0] % 2)):
            ref[0:chans, :] = pack_scr[pl.ds(pl.multiple_of(half * chans, 8), chans), :]
            ref[chans:, :] = grads_ref[pl.ds(pl.multiple_of(half * (chans // 2), 8), chans // 2), :]


def input_grad_kernel(block, d_ref, dgate_ref, normed_ref, wcat_ref, dzn_ref, norm_ref):
    chans = normed_ref.shape[1]
    d_zn = dot(wcat_ref[:, 0:4 * chans], d_ref[0]) + dot(wcat_ref[:, 4 * chans:5 * chans], dgate_ref[0])
    dzn_ref[0] = d_zn

    @pl.when(block() == 0)
    def _():
        norm_ref[...] = jnp.zeros_like(norm_ref)

    norm_ref[0:1, 0:chans] += as_row(jnp.sum(d_zn * normed_ref[0], axis=1, keepdims=True))
    norm_ref[1:2, 0:chans] += as_row(jnp.sum(d_zn, axis=1, keepdims=True))


def pair_grad_kernel(block, after_ref, dzn_ref, normed_ref, rstd_ref, gains_ref, pair_ref):
    gain = column(gains_ref[0:1, :])
    for pos in range(pair_ref.shape[0]):
        span = slice(pos * LANES, (pos + 1) * LANES)
        h = dzn_ref[0, :, span] * gain
        normed = normed_ref[0, :, span]
        mean_h = jnp.mean(h, axis=0, keepdims=True)
        mean_p = jnp.mean(h * normed, axis=0, keepdims=True)
        pair_ref[pos] = (rstd_ref[0, :, span] * (h - mean_h - normed * mean_p)).astype(BF16)


def combine_kernel(keep_ref, got_ref, norm_ref, grads_ref, out_ref):
    chans = grads_ref.shape[0] - 8
    high, low = split(jnp.concatenate([norm_ref[0:2, :], grads_ref[chans:chans + 1, :]], axis=0))
    rest = jnp.zeros((2, norm_ref.shape[1]), F32)
    block = jnp.concatenate([keep_ref[...] + got_ref[...], high, low, rest], axis=0).astype(BF16)
    for d in range(out_ref.shape[0]):
        out_ref[d] = block


def total_kernel(pack_ref, mine_ref):
    mine_ref[...] = tree_sum([pack_ref[d].astype(F32) for d in range(pack_ref.shape[0])])


def unpack_kernel(scale, me_ref, mine_ref, got_ref, proj_ref, out_ref, norms_ref):
    chans = proj_ref.shape[1]
    rows = chans + chans // 2
    odd = me_ref[0] % 2 == 1
    mine, got = mine_ref[...] * scale, got_ref[...] * scale
    for half, total in enumerate((jnp.where(odd, got, mine), jnp.where(odd, mine, got))):
        for p in range(2):
            lanes = slice(p * chans, (p + 1) * chans)
            proj_ref[2 * half + p] = total[0:chans, lanes]
            out_ref[p, half * (chans // 2):(half + 1) * (chans // 2)] = total[chans:rows, lanes]
    norm = (mine + got)[rows:rows + 6, 0:chans]
    norms_ref[...] = norm[0:3] + norm[3:6]


def exchange(x, groups=None):
    return lax.all_to_all(x, "row", split_axis=0, concat_axis=0, axis_index_groups=groups, tiled=True)


def per_device(n, pair, cotangent, token_mask, coverage, w_proj, w_out, layer_norm_gains, ln_bias):
    templ, rows, chans, width = pair.shape
    count = templ * rows
    blocks = width // LANES
    chips = n // 2
    direct = blocks == 1 and n % 2 == 0 and chips & (chips - 1) == 0 and chans % chips == 0
    per = chans // chips if direct else 1
    lanes = count * LANES
    me = lax.axis_index("row").astype(jnp.int32).reshape(1)
    tokens_row = token_mask.reshape(1, width)

    params = pltpu.CompilerParams(vmem_limit_bytes=(16 if blocks == 1 else 40) * 1024 * 1024)
    smem = pl.BlockSpec(memory_space=pltpu.SMEM)
    whole = pl.BlockSpec(memory_space=pltpu.VMEM)

    def block_spec(shape, index):
        return whole if blocks == 1 else pl.BlockSpec(shape, index)

    def full(shape):
        return block_spec(shape, lambda b: (0,) * len(shape))

    def array(shape, dtype):
        return pltpu.VMEM(shape, dtype) if blocks == 1 else jax.ShapeDtypeStruct(shape, dtype)

    def from_hbm(x):
        return pltpu.with_memory_space_constraint(x, pltpu.HBM)

    def call(name, kernel, args, in_specs, out_specs, out_shape, scratch_shapes=()):
        block = (lambda: 0) if blocks == 1 else (lambda: pl.program_id(0))
        kernel = functools.partial(kernel, block)
        return pl.pallas_call(
            kernel,
            grid=() if blocks == 1 else (blocks,),
            in_specs=in_specs,
            out_specs=out_specs,
            out_shape=out_shape,
            scratch_shapes=scratch_shapes,
            compiler_params=params,
            name=name,
        )(*args)

    rows_spec = block_spec((count, chans, LANES), lambda b: (0, 0, b))
    tok_spec = block_spec((1, LANES), lambda b: (0, b))
    lr_spec = block_spec((chans, 2, count, LANES), lambda b: (0, 0, 0, b))
    cat_spec = block_spec((1, chans, lanes), lambda b: (b, 0, 0))
    fac_spec = block_spec((1, 4 * chans, lanes), lambda b: (b, 0, 0))
    one_spec = block_spec((1, 1, lanes), lambda b: (b, 0, 0))
    chan_spec = block_spec((chans, count, LANES), lambda b: (0, 0, b))
    w_spec, wo_spec, gains_spec = full(w_proj.shape), full(w_out.shape), full(layer_norm_gains.shape)
    scratch = pltpu.VMEM((chans * count, LANES), F32)
    pair_rows = from_hbm(pair.reshape(count, chans, width))
    cot_rows = from_hbm(cotangent.reshape(count, chans, width))
    w_proj_in, w_out_in, gains_in = from_hbm(w_proj), from_hbm(w_out), from_hbm(layer_norm_gains)
    tokens_in, cover_in = from_hbm(tokens_row), from_hbm(coverage.transpose(1, 2, 0))

    def cat(dtype):
        return array((blocks, chans, lanes), dtype)

    def chunks(depth):
        return [jax.ShapeDtypeStruct((depth, count, width), BF16)] * chips

    def send_chunks(parts):
        got = [parts[0]] + [None] * (chips - 1)
        for k in reversed(range(1, chips)):
            got[k] = lax.ppermute(parts[k], "row", [(d, d ^ (2 * k)) for d in range(n)])
        return got

    *projected, zn, fac, normed, rstd = call(
        "project",
        functools.partial(project_kernel, rows, chips if direct else 0),
        (me, tokens_in, cover_in, pair_rows, tokens_in, w_proj_in, gains_in, from_hbm(ln_bias.reshape(1, chans))),
        [smem, full((1, width)), full(cover_in.shape), rows_spec, tok_spec, w_spec, gains_spec, full((1, chans))],
        ([whole] * chips if direct else [lr_spec]) + [cat_spec, fac_spec, cat_spec, one_spec],
        (chunks(2 * per) if direct else [jax.ShapeDtypeStruct((chans, 2, count, width), BF16)])
        + [cat(BF16), array((blocks, 4 * chans, lanes), F32), cat(F32), array((blocks, 1, lanes), F32)],
        [scratch, scratch],
    )
    if direct:
        cols = send_chunks(projected)

    cg, d_update, d_outn, wcat = call(
        "prepare",
        prepare_kernel,
        (cot_rows, zn, w_proj_in, w_out_in),
        [rows_spec, cat_spec, w_spec, wo_spec],
        [cat_spec, cat_spec, chan_spec, full((chans, 5 * chans))],
        [cat(F32), cat(BF16), array((chans, count, width), F32), array((chans, 5 * chans), BF16)],
        [scratch],
    )

    partner = [(d, d ^ 1) for d in range(n)]
    same_core = [list(range(core, n, 2)) for core in range(2)]
    if direct:
        slices = per * templ
        split_shape = (chips, per, count, width)
        square = pltpu.VMEM((slices, width, width), F32)
        own = pl.pallas_call(
            collect_kernel,
            in_specs=[pl.BlockSpec(memory_space=pl.ANY)] + [whole] * chips,
            out_shape=jax.ShapeDtypeStruct(split_shape, BF16),
            compiler_params=params,
            name="collect",
        )(wcat, *cols)
        got = lax.ppermute(own, "row", partner)
        mixed, left_cols, right_cols = pl.pallas_call(
            functools.partial(mixed_kernel, rows, chips),
            in_specs=[smem] + [whole] * (chips + 2),
            out_shape=[
                jax.ShapeDtypeStruct(split_shape, BF16),
                array((slices, chips * rows, width), BF16),
                array((slices, width, width), BF16),
            ],
            scratch_shapes=[square],
            compiler_params=params,
            name="mixed",
        )(me, *cols, own, got)
        mixed_rows = exchange(mixed, same_core).reshape(chans, count, width)
    else:
        slices = chans * templ // n
        cols = projected[0].reshape(chans, 2, templ, rows, width).transpose(0, 2, 1, 3, 4)
        cols = exchange(cols.reshape(n * slices, 2, rows, width)).reshape(n, slices, 2, rows, width)
        left_cols, right_cols = cols.transpose(2, 1, 0, 3, 4).reshape(2, slices, width, width)
        mixed = jnp.einsum("sik,sjk->sij", left_cols, right_cols, preferred_element_type=F32)
        mixed = mixed.astype(BF16).reshape(slices, n, rows, width).transpose(1, 0, 2, 3)
        mixed_rows = exchange(mixed.reshape(n * slices, rows, width)).reshape(chans, count, width)

    d_mixed, outn, norm_sums = call(
        "middle",
        middle_kernel,
        (layer_norm_gains, d_outn, mixed_rows),
        [smem, chan_spec, chan_spec],
        [chan_spec, chan_spec, full((chans, LANES))],
        [
            jax.ShapeDtypeStruct((chans, count, width), BF16),
            array((chans, count, width), F32),
            array((chans, LANES), F32),
        ],
    )
    if direct:
        dmix_cols = exchange(d_mixed.reshape(split_shape), same_core)

    d_gate, out_grads = call(
        "update",
        update_kernel,
        (outn, norm_sums, zn, cg, d_update, w_out),
        [chan_spec, full((chans, LANES)), cat_spec, cat_spec, cat_spec, wo_spec],
        [cat_spec, full((chans + 8, 2 * chans))],
        [cat(BF16), array((chans + 8, 2 * chans), F32)],
        [scratch, pltpu.VMEM((chans, lanes), BF16)],
    )

    if direct:
        d_left, keep, send = pl.pallas_call(
            functools.partial(triangle_back_kernel, rows),
            in_specs=[smem] + [whole] * 3,
            out_shape=[array(split_shape, BF16), array(split_shape, F32), jax.ShapeDtypeStruct(split_shape, BF16)],
            scratch_shapes=[square],
            compiler_params=params,
            name="triangle_back",
        )(me, dmix_cols, left_cols, right_cols)
        got = lax.ppermute(send, "row", partner)
        d_lr = pl.pallas_call(
            join_kernel,
            out_shape=chunks(2 * per),
            compiler_params=params,
            name="join",
        )(d_left, keep, got)
        d_lr = send_chunks(d_lr)
    else:
        dmix_cols = exchange(d_mixed.reshape(n * slices, rows, width)).reshape(n, slices, rows, width)
        dmix_cols = dmix_cols.transpose(1, 0, 2, 3).reshape(slices, width, width)
        d_left = jnp.einsum("sij,sjk->sik", dmix_cols, right_cols, preferred_element_type=F32)
        d_right = jnp.einsum("sij,sik->sjk", dmix_cols, left_cols, preferred_element_type=F32)
        d_lr = jnp.stack([d_left.astype(BF16), d_right.astype(BF16)]).reshape(2, slices, n, rows, width)
        d_lr = exchange(d_lr.transpose(2, 1, 0, 3, 4).reshape(n * slices, 2, rows, width))
        d_lr = d_lr.reshape(chans, templ, 2, rows, width).transpose(0, 2, 1, 3, 4)
        d_lr = [d_lr.reshape(chans, 2, count, width)]

    half_rows = chans + chans // 2
    d_spec = block_spec((1, 4 * chans, lanes), lambda b: (b, 0, 0))
    d_pre, keep, send = call(
        "gating_back",
        functools.partial(gating_back_kernel, blocks, chips if direct else 0),
        (me, fac, zn, out_grads, *d_lr),
        [smem, fac_spec, cat_spec, full((chans + 8, 2 * chans))] + ([whole] * chips if direct else [lr_spec]),
        [d_spec, full((half_rows, 2 * chans)), full((half_rows, 2 * chans))],
        [
            array((blocks, 4 * chans, lanes), BF16),
            array((half_rows, 2 * chans), F32),
            jax.ShapeDtypeStruct((half_rows, 2 * chans), F32),
        ],
        [scratch, scratch, pltpu.VMEM((2 * chans, 2 * chans), F32)],
    )
    got = lax.ppermute(send, "row", partner)
    d_zn, norm_rows = call(
        "input_grad",
        input_grad_kernel,
        (d_pre, d_gate, normed, wcat),
        [d_spec, cat_spec, cat_spec, full((chans, 5 * chans))],
        [cat_spec, full((8, 2 * chans))],
        [cat(F32), array((8, 2 * chans), F32)],
    )
    sums = pl.pallas_call(
        combine_kernel,
        out_shape=jax.ShapeDtypeStruct((chips, half_rows + 8, 2 * chans), BF16),
        compiler_params=params,
        name="combine",
    )(keep, got, norm_rows, out_grads)
    sums = exchange(sums, same_core)
    mine = pl.pallas_call(
        total_kernel,
        out_shape=jax.ShapeDtypeStruct((half_rows + 8, 2 * chans), F32),
        compiler_params=params,
        name="total",
    )(sums)
    got = lax.ppermute(mine, "row", partner)
    pair_grad = call(
        "pair_grad",
        pair_grad_kernel,
        (mine, d_zn, normed, rstd, layer_norm_gains),
        [pl.BlockSpec(memory_space=pl.ANY), cat_spec, cat_spec, one_spec, gains_spec],
        rows_spec,
        jax.ShapeDtypeStruct((count, chans, width), BF16),
    )
    grad_proj, grad_out, norm_grads = pl.pallas_call(
        functools.partial(unpack_kernel, 1.0 / width),
        in_specs=[smem] + [whole] * 2,
        out_shape=[
            jax.ShapeDtypeStruct(w_proj.shape, F32),
            jax.ShapeDtypeStruct(w_out.shape, F32),
            jax.ShapeDtypeStruct((3, chans), F32),
        ],
        compiler_params=params,
        name="unpack",
    )(me, mine, got)
    return pair_grad.reshape(pair.shape), grad_proj, grad_out, norm_grads


def solution(mesh):
    return jax.shard_map(
        functools.partial(per_device, mesh.shape["row"]),
        mesh=mesh,
        in_specs=(
            P("groups", "row", None, None),
            P("groups", "row", None, None),
            P("groups"),
            P("groups", None, None),
            P(),
            P(),
            P(),
            P(),
        ),
        out_specs=(
            P("groups", "row", None, None),
            P("groups", None, None),
            P("groups", None, None),
            P("groups", None),
        ),
        check_vma=False,
    )
```

time: 88 us -> 86 us (0.977)
  blocking collectives: 78 us -> 37.8 us
  starting transfers between devices: 0.15 us -> 24 us
  waiting for transfers between devices: 1.23 us -> 13.7 us
  Pallas kernels: 7.59 us -> 9.4 us
    all_to_all x5 -> x3, blocking collectives: 78 us -> 37.8 us  [exchange(): lax.all_to_all(x, 'row', split_axis=0, concat_axis=0, axis_index_groups=g...]
    ppermute x0 -> x15, starting transfers between devices: none -> 23.8 us  [the longest x14 23.7 us: send_chunks(): got[k] = lax.ppermute(parts[k], 'row', [(d, d ^ 2 * k) for d in range(n)])]
    ppermute x0 -> x15, waiting for transfers between devices: none -> 11.2 us  [the longest x14 9.68 us: send_chunks(): got[k] = lax.ppermute(parts[k], 'row', [(d, d ^ 2 * k) for d in range(n)])]
    ppermute x1 -> x2, waiting for transfers between devices: 0.01 us -> 2.25 us  [per_device(): got = lax.ppermute(send, 'row', partner)]
    pallas_call x4 -> x7, Pallas kernels: 6.14 us -> 7.52 us  [call(): pl.pallas_call(kernel, grid=() if blocks == 1 else (blocks,), in_specs=in...]
    ppermute x1, waiting for transfers between devices: 1.22 us -> 0.25 us  [per_device(): got = lax.ppermute(mine, 'row', partner)]
    pallas_call x5 -> x7, Pallas kernels: 1.45 us -> 1.88 us  [the longest x1 0.76 us: per_device(): pl.pallas_call(functools.partial(unpack_kernel, 1.0 / width), in_specs=[s...]
  transfers between devices with their start and end apart: 2 -> 18, of which waited for: 1 -> 8; matrix products, arithmetic and copies ran while one was open for 0% -> 0% of each run, Pallas kernels for 1% -> 4%
where the time goes in v5:
time: 86 us; the launch traced here: 85.7 us
  blocking collectives  37.8 us (44%)
  starting transfers between devices  24 us (28%)
  waiting for transfers between devices  13.7 us (16%)
  Pallas kernels  9.4 us (11%)
    all_to_all x3, blocking collectives, exchange(): lax.all_to_all(x, 'row', split_axis=0, concat_axis=0, axis_index_groups=g...  37.8 us
    ppermute x14, starting transfers between devices, send_chunks(): got[k] = lax.ppermute(parts[k], 'row', [(d, d ^ 2 * k) for d in range(n)])  23.7 us
    ppermute x14, waiting for transfers between devices, send_chunks(): got[k] = lax.ppermute(parts[k], 'row', [(d, d ^ 2 * k) for d in range(n)])  9.68 us
    pallas_call x7, Pallas kernels, call(): pl.pallas_call(kernel, grid=() if blocks == 1 else (blocks,), in_specs=in...  7.52 us
    ppermute x2, waiting for transfers between devices, per_device(): got = lax.ppermute(send, 'row', partner)  2.25 us
  transfers between devices with their start and end apart: 18, of which 8 were waited for; matrix products, arithmetic and copies ran while one was open for 0% of the time, Pallas kernels for 4%

profile of v5, /device:TPU:0, one launch (start us, length us, event | category | flops | bytes accessed | tf_op | source)
XLA Modules:
  0.0 85.7 jit_solution(11091389175163983365)
XLA Ops:
  0.6 1.9 %project.1 = (bf16[16,16,128]{2,1,0:T(8,128)(2,1)S(1)}, bf16[16,16,128]{2,1,0:T(8,128)(2,1)S(1)}, bf16[16,16,128]{2,1,0:T(8,128)(2,1)S(1)}, bf16[16,16,128]{2,1,...) custom-call(s32[1]{0:T(128)} %bitcast.me_ref, ...), custom_call_target="tpu_custom_call" | custom-call | tf_op jit(solution)/shard_map/project/pallas_call | solution.py:385
  2.5 3.0 %collective-permute-start = (bf16[16,16,128]{2,1,0:T(8,128)(2,1)S(1)}, bf16[16,16,128]{2,1,0:T(8,128)(2,1)S(1)}, u32[]{:S(2)}, u32[]{:S(2)}) collective-permute-start(bf16[16,16,128]{2,1,0:T(8,128)(2,1)S(1)} %get-tuple-element.51), channel_id=1, source_target_pairs={{0,2},{1,3},{2,0},{3,1},{4,6},{5,7},{6,4},{7,5},{8,10},{9,11},{10,... | collective-permute-start | bytes 196616 | tf_op jit(solution)/shard_map/ppermute | solution.py:419
  5.6 1.6 %collective-permute-start.1 = (bf16[16,16,128]{2,1,0:T(8,128)(2,1)S(1)}, bf16[16,16,128]{2,1,0:T(8,128)(2,1)S(1)}, u32[]{:S(2)}, u32[]{:S(2)}) collective-permute-start(bf16[16,16,128]{2,1,0:T(8,128)(2,1)S(1)} %get-tuple-element.52), channel_id=1, source_target_pairs={{0,4},{1,5},{2,6},{3,7},{4,0},{5,1},{6,2},{7,3},{8,12},{9,13},{10,... | collective-permute-start | bytes 196616 | tf_op jit(solution)/shard_map/ppermute | solution.py:419
  7.2 3.0 %collective-permute-start.3 = (bf16[16,16,128]{2,1,0:T(8,128)(2,1)S(1)}, bf16[16,16,128]{2,1,0:T(8,128)(2,1)S(1)}, u32[]{:S(2)}, u32[]{:S(2)}) collective-permute-start(bf16[16,16,128]{2,1,0:T(8,128)(2,1)S(1)} %get-tuple-element.54), channel_id=1, source_target_pairs={{0,8},{1,9},{2,10},{3,11},{4,12},{5,13},{6,14},{7,15},{8,0},{9,1},... | collective-permute-start | bytes 196616 | tf_op jit(solution)/shard_map/ppermute | solution.py:419
  10.1 1.3 %collective-permute-start.4 = (bf16[16,16,128]{2,1,0:T(8,128)(2,1)S(1)}, bf16[16,16,128]{2,1,0:T(8,128)(2,1)S(1)}, u32[]{:S(2)}, u32[]{:S(2)}) collective-permute-start(bf16[16,16,128]{2,1,0:T(8,128)(2,1)S(1)} %get-tuple-element.55), channel_id=1, source_target_pairs={{0,10},{1,11},{2,8},{3,9},{4,14},{5,15},{6,12},{7,13},{8,2},{9,3},... | collective-permute-start | bytes 196616 | tf_op jit(solution)/shard_map/ppermute | solution.py:419
  11.4 3.6 %collective-permute-start.5 = (bf16[16,16,128]{2,1,0:T(8,128)(2,1)S(1)}, bf16[16,16,128]{2,1,0:T(8,128)(2,1)S(1)}, u32[]{:S(2)}, u32[]{:S(2)}) collective-permute-start(bf16[16,16,128]{2,1,0:T(8,128)(2,1)S(1)} %get-tuple-element.56), channel_id=1, source_target_pairs={{0,12},{1,13},{2,14},{3,15},{4,8},{5,9},{6,10},{7,11},{8,4},{9,5},... | collective-permute-start | bytes 196616 | tf_op jit(solution)/shard_map/ppermute | solution.py:419
  15.1 1.6 %prepare.1 = (f32[1,64,2048]{2,1,0:T(8,128)S(1)}, bf16[1,64,2048]{2,1,0:T(8,128)(2,1)S(1)}, f32[64,16,128]{2,1,0:T(8,128)S(1)}, bf16[64,320]{1,0:T(8,128)(2,1)S(1)}) custom-call(bf16[16,64,128]{2,1,0:T(8,128)(2,1)} %bitcast.12, bf16[1,64,2048]{2,1,0:T(8,128)(2,1)S(1)} %get-tuple-element.48.zn_ref, bf16[4,64,64]{2,1,0:T(8,128)(2,1)} %w_ref.3, ...), custom_call_target="tpu_custom_call" | custom-call | tf_op jit(solution)/shard_map/prepare/pallas_call | solution.py:385
  16.7 3.7 %collective-permute-done.4.refs_5_ = bf16[16,16,128]{2,1,0:T(8,128)(2,1)S(1)} collective-permute-done((bf16[16,16,128]{2,1,0:T(8,128)(2,1)S(1)}, bf16[16,16,128]{2,1,0:T(8,128)(2,1)S(1)}, u32[]{:S(2)}, u32[]{:S(2)}) %collective-permute-start.4) | collective-permute-done | bytes 65568 | tf_op jit(solution)/shard_map/ppermute | solution.py:419
  20.4 1.8 %collective-permute-done.6.refs_7_ = bf16[16,16,128]{2,1,0:T(8,128)(2,1)S(1)} collective-permute-done((bf16[16,16,128]{2,1,0:T(8,128)(2,1)S(1)}, bf16[16,16,128]{2,1,0:T(8,128)(2,1)S(1)}, u32[]{:S(2)}, u32[]{:S(2)}) %collective-permute-start.6) | collective-permute-done | bytes 65568 | tf_op jit(solution)/shard_map/ppermute | solution.py:419
  22.2 1.5 %collective-permute-done.7.refs_9_ = bf16[8,8,16,128]{3,2,1,0:T(8,128)(2,1)S(1)} collective-permute-done((bf16[8,8,16,128]{3,2,1,0:T(8,128)(2,1)S(1)}, bf16[8,8,16,128]{3,2,1,0:T(8,128)(2,1)S(1)}, u32[]{:S(2)}, u32[]{:S(2)}) %collective-permute-start.7) | collective-permute-done | bytes 262176 | tf_op jit(solution)/shard_map/ppermute | solution.py:458
  23.7 0.4 mixed.1
  24.2 13.2 %all_to_all.15 = bf16[8,8,16,128]{3,2,1,0:T(8,128)(2,1)S(1)} all-to-all(bf16[8,8,16,128]{3,2,1,0:T(8,128)(2,1)S(1)} %get-tuple-element.59), channel_id=1, replica_groups={{0,2,4,6,8,10,12,14},{1,3,5,7,9,11,13,15},{16,18,20,22,24,26,28,30},{17..., dimensions={0} | all-to-all | bytes 524288 | tf_op jit(solution)/shard_map/all_to_all | solution.py:352
  37.4 1.0 %middle.1 = (bf16[64,16,128]{2,1,0:T(8,128)(2,1)S(1)}, f32[64,16,128]{2,1,0:T(8,128)S(1)}, f32[64,128]{1,0:T(8,128)S(1)}) custom-call(f32[2,64]{1,0:T(2,128)S(1)} %copy-done.1, f32[64,16,128]{2,1,0:T(8,128)S(1)} %get-tuple-element.49.dout_ref, bf16[64,16,128]{2,1,0:T(8,128)(2,1)S(1)} %bitcast.9), custom_call_target="tpu_custom_call" | custom-call | tf_op jit(solution)/shard_map/middle/pallas_call | solution.py:385
  38.4 12.0 %all_to_all.16.dmix_ref = bf16[8,8,16,128]{3,2,1,0:T(8,128)(2,1)S(1)} all-to-all(bf16[8,8,16,128]{3,2,1,0:T(8,128)(2,1)S(1)} %bitcast.10), channel_id=1, replica_groups={{0,2,4,6,8,10,12,14},{1,3,5,7,9,11,13,15},{16,18,20,22,24,26,28,30},{17..., dimensions={0} | all-to-all | bytes 524288 | tf_op jit(solution)/shard_map/all_to_all | solution.py:352
  50.3 0.6 triangle_back.1
  51.0 1.5 %collective-permute-done.8.got_ref = bf16[8,8,16,128]{3,2,1,0:T(8,128)(2,1)S(1)} collective-permute-done((bf16[8,8,16,128]{3,2,1,0:T(8,128)(2,1)S(1)}, bf16[8,8,16,128]{3,2,1,0:T(8,128)(2,1)S(1)}, u32[]{:S(2)}, u32[]{:S(2)}) %collective-permute-start.8) | collective-permute-done | bytes 262176 | tf_op jit(solution)/shard_map/ppermute | solution.py:515
  52.6 1.5 %collective-permute-start.9 = (bf16[16,16,128]{2,1,0:T(8,128)(2,1)S(1)}, bf16[16,16,128]{2,1,0:T(8,128)(2,1)S(1)}, u32[]{:S(2)}, u32[]{:S(2)}) collective-permute-start(bf16[16,16,128]{2,1,0:T(8,128)(2,1)S(1)} %get-tuple-element.72), channel_id=1, source_target_pairs={{0,2},{1,3},{2,0},{3,1},{4,6},{5,7},{6,4},{7,5},{8,10},{9,11},{10,... | collective-permute-start | bytes 196616 | tf_op jit(solution)/shard_map/ppermute | solution.py:419
  54.1 2.0 %collective-permute-start.11 = (bf16[16,16,128]{2,1,0:T(8,128)(2,1)S(1)}, bf16[16,16,128]{2,1,0:T(8,128)(2,1)S(1)}, u32[]{:S(2)}, u32[]{:S(2)}) collective-permute-start(bf16[16,16,128]{2,1,0:T(8,128)(2,1)S(1)} %get-tuple-element.74), channel_id=1, source_target_pairs={{0,6},{1,7},{2,4},{3,5},{4,2},{5,3},{6,0},{7,1},{8,14},{9,15},{10,... | collective-permute-start | bytes 196616 | tf_op jit(solution)/shard_map/ppermute | solution.py:419
  56.1 1.1 %collective-permute-start.12 = (bf16[16,16,128]{2,1,0:T(8,128)(2,1)S(1)}, bf16[16,16,128]{2,1,0:T(8,128)(2,1)S(1)}, u32[]{:S(2)}, u32[]{:S(2)}) collective-permute-start(bf16[16,16,128]{2,1,0:T(8,128)(2,1)S(1)} %get-tuple-element.75), channel_id=1, source_target_pairs={{0,8},{1,9},{2,10},{3,11},{4,12},{5,13},{6,14},{7,15},{8,0},{9,1},... | collective-permute-start | bytes 196616 | tf_op jit(solution)/shard_map/ppermute | solution.py:419
  57.2 2.8 %collective-permute-start.13 = (bf16[16,16,128]{2,1,0:T(8,128)(2,1)S(1)}, bf16[16,16,128]{2,1,0:T(8,128)(2,1)S(1)}, u32[]{:S(2)}, u32[]{:S(2)}) collective-permute-start(bf16[16,16,128]{2,1,0:T(8,128)(2,1)S(1)} %get-tuple-element.76), channel_id=1, source_target_pairs={{0,10},{1,11},{2,8},{3,9},{4,14},{5,15},{6,12},{7,13},{8,2},{9,3},... | collective-permute-start | bytes 196616 | tf_op jit(solution)/shard_map/ppermute | solution.py:419
  59.9 1.4 %collective-permute-start.14 = (bf16[16,16,128]{2,1,0:T(8,128)(2,1)S(1)}, bf16[16,16,128]{2,1,0:T(8,128)(2,1)S(1)}, u32[]{:S(2)}, u32[]{:S(2)}) collective-permute-start(bf16[16,16,128]{2,1,0:T(8,128)(2,1)S(1)} %get-tuple-element.77), channel_id=1, source_target_pairs={{0,12},{1,13},{2,14},{3,15},{4,8},{5,9},{6,10},{7,11},{8,4},{9,5},... | collective-permute-start | bytes 196616 | tf_op jit(solution)/shard_map/ppermute | solution.py:419
  61.4 2.4 %collective-permute-start.15 = (bf16[16,16,128]{2,1,0:T(8,128)(2,1)S(1)}, bf16[16,16,128]{2,1,0:T(8,128)(2,1)S(1)}, u32[]{:S(2)}, u32[]{:S(2)}) collective-permute-start(bf16[16,16,128]{2,1,0:T(8,128)(2,1)S(1)} %get-tuple-element.78), channel_id=1, source_target_pairs={{0,14},{1,15},{2,12},{3,13},{4,10},{5,11},{6,8},{7,9},{8,6},{9,7},... | collective-permute-start | bytes 196616 | tf_op jit(solution)/shard_map/ppermute | solution.py:419
  63.8 0.7 update.1
  64.5 1.7 %collective-permute-done.12.refs_4_ = bf16[16,16,128]{2,1,0:T(8,128)(2,1)S(1)} collective-permute-done((bf16[16,16,128]{2,1,0:T(8,128)(2,1)S(1)}, bf16[16,16,128]{2,1,0:T(8,128)(2,1)S(1)}, u32[]{:S(2)}, u32[]{:S(2)}) %collective-permute-start.12) | collective-permute-done | bytes 65568 | tf_op jit(solution)/shard_map/ppermute | solution.py:419
  66.3 2.5 %collective-permute-done.13.refs_5_ = bf16[16,16,128]{2,1,0:T(8,128)(2,1)S(1)} collective-permute-done((bf16[16,16,128]{2,1,0:T(8,128)(2,1)S(1)}, bf16[16,16,128]{2,1,0:T(8,128)(2,1)S(1)}, u32[]{:S(2)}, u32[]{:S(2)}) %collective-permute-start.13) | collective-permute-done | bytes 65568 | tf_op jit(solution)/shard_map/ppermute | solution.py:419
  68.8 0.8 gating_back.1
  69.7 0.5 input_grad.1
  70.2 0.7 collective-permute-done.16.got_ref
  70.9 12.7 %all_to_all.17.pack_ref = bf16[8,104,128]{2,1,0:T(8,128)(2,1)S(1)} all-to-all(bf16[8,104,128]{2,1,0:T(8,128)(2,1)S(1)} %combine.1), channel_id=1, replica_groups={{0,2,4,6,8,10,12,14},{1,3,5,7,9,11,13,15},{16,18,20,22,24,26,28,30},{17..., dimensions={0} | all-to-all | bytes 425984 | tf_op jit(solution)/shard_map/all_to_all | solution.py:352
  83.7 1.0 %pair_grad.1 = bf16[16,64,128]{2,1,0:T(8,128)(2,1)} custom-call(f32[104,128]{1,0:T(8,128)S(1)} %total.1.after_ref.mine_ref, f32[1,64,2048]{2,1,0:T(8,128)S(1)} %get-tuple-element.85.dzn_ref, f32[1,64,2048]{2,1,0:T(8,128)S(1)} %get-tuple-element.83.normed_ref, f32[1,1,2048]{2,1,0:T(1,128)S(1)} %get-tuple-element.86.rstd_ref, f32[2,64]{1,0:T(2,128)S(1)} %copy-done.1), custom_call_target="tpu_custom_call" | custom-call | tf_op jit(solution)/shard_map/pair_grad/pallas_call | solution.py:385
  84.7 0.2 collective-permute-done.17.got_ref
  84.9 0.8 unpack.1
  (25 shorter events, 0.5 us)
Async XLA Ops:
  0.6 36.7 %copy-start.1 = (f32[2,64]{1,0:T(2,128)S(1)}, f32[2,64]{1,0:T(2,128)}, u32[]{:S(2)}) copy-start(f32[2,64]{1,0:T(2,128)} %gains_ref.5) | copy-start | bytes 1540
  2.5 8.9 %collective-permute-start = (bf16[16,16,128]{2,1,0:T(8,128)(2,1)S(1)}, bf16[16,16,128]{2,1,0:T(8,128)(2,1)S(1)}, u32[]{:S(2)}, u32[]{:S(2)}) collective-permute-start(bf16[16,16,128]{2,1,0:T(8,128)(2,1)S(1)} %get-tuple-element.51), channel_id=1, source_target_pairs={{0,2},{1,3},{2,0},{3,1},{4,6},{5,7},{6,4},{7,5},{8,10},{9,11},{10,... | collective-permute-start | bytes 196616 | tf_op jit(solution)/shard_map/ppermute | solution.py:419
  5.6 9.5 %collective-permute-start.1 = (bf16[16,16,128]{2,1,0:T(8,128)(2,1)S(1)}, bf16[16,16,128]{2,1,0:T(8,128)(2,1)S(1)}, u32[]{:S(2)}, u32[]{:S(2)}) collective-permute-start(bf16[16,16,128]{2,1,0:T(8,128)(2,1)S(1)} %get-tuple-element.52), channel_id=1, source_target_pairs={{0,4},{1,5},{2,6},{3,7},{4,0},{5,1},{6,2},{7,3},{8,12},{9,13},{10,... | collective-permute-start | bytes 196616 | tf_op jit(solution)/shard_map/ppermute | solution.py:419
  7.2 9.5 %collective-permute-start.2 = (bf16[16,16,128]{2,1,0:T(8,128)(2,1)S(1)}, bf16[16,16,128]{2,1,0:T(8,128)(2,1)S(1)}, u32[]{:S(2)}, u32[]{:S(2)}) collective-permute-start(bf16[16,16,128]{2,1,0:T(8,128)(2,1)S(1)} %get-tuple-element.53), channel_id=1, source_target_pairs={{0,6},{1,7},{2,4},{3,5},{4,2},{5,3},{6,0},{7,1},{8,14},{9,15},{10,... | collective-permute-start | bytes 196616 | tf_op jit(solution)/shard_map/ppermute | solution.py:419
  7.2 9.5 %collective-permute-start.3 = (bf16[16,16,128]{2,1,0:T(8,128)(2,1)S(1)}, bf16[16,16,128]{2,1,0:T(8,128)(2,1)S(1)}, u32[]{:S(2)}, u32[]{:S(2)}) collective-permute-start(bf16[16,16,128]{2,1,0:T(8,128)(2,1)S(1)} %get-tuple-element.54), channel_id=1, source_target_pairs={{0,8},{1,9},{2,10},{3,11},{4,12},{5,13},{6,14},{7,15},{8,0},{9,1},... | collective-permute-start | bytes 196616 | tf_op jit(solution)/shard_map/ppermute | solution.py:419
  10.1 10.2 %collective-permute-start.4 = (bf16[16,16,128]{2,1,0:T(8,128)(2,1)S(1)}, bf16[16,16,128]{2,1,0:T(8,128)(2,1)S(1)}, u32[]{:S(2)}, u32[]{:S(2)}) collective-permute-start(bf16[16,16,128]{2,1,0:T(8,128)(2,1)S(1)} %get-tuple-element.55), channel_id=1, source_target_pairs={{0,10},{1,11},{2,8},{3,9},{4,14},{5,15},{6,12},{7,13},{8,2},{9,3},... | collective-permute-start | bytes 196616 | tf_op jit(solution)/shard_map/ppermute | solution.py:419
  11.4 8.9 %collective-permute-start.5 = (bf16[16,16,128]{2,1,0:T(8,128)(2,1)S(1)}, bf16[16,16,128]{2,1,0:T(8,128)(2,1)S(1)}, u32[]{:S(2)}, u32[]{:S(2)}) collective-permute-start(bf16[16,16,128]{2,1,0:T(8,128)(2,1)S(1)} %get-tuple-element.56), channel_id=1, source_target_pairs={{0,12},{1,13},{2,14},{3,15},{4,8},{5,9},{6,10},{7,11},{8,4},{9,5},... | collective-permute-start | bytes 196616 | tf_op jit(solution)/shard_map/ppermute | solution.py:419
  15.0 7.1 %collective-permute-start.6 = (bf16[16,16,128]{2,1,0:T(8,128)(2,1)S(1)}, bf16[16,16,128]{2,1,0:T(8,128)(2,1)S(1)}, u32[]{:S(2)}, u32[]{:S(2)}) collective-permute-start(bf16[16,16,128]{2,1,0:T(8,128)(2,1)S(1)} %get-tuple-element.57), channel_id=1, source_target_pairs={{0,14},{1,15},{2,12},{3,13},{4,10},{5,11},{6,8},{7,9},{8,6},{9,7},... | collective-permute-start | bytes 196616 | tf_op jit(solution)/shard_map/ppermute | solution.py:419
  22.1 1.6 %collective-permute-start.7 = (bf16[8,8,16,128]{3,2,1,0:T(8,128)(2,1)S(1)}, bf16[8,8,16,128]{3,2,1,0:T(8,128)(2,1)S(1)}, u32[]{:S(2)}, u32[]{:S(2)}) collective-permute-start(bf16[8,8,16,128]{3,2,1,0:T(8,128)(2,1)S(1)} %collect.1.refs_8_), channel_id=1, source_target_pairs={{0,1},{1,0},{2,3},{3,2},{4,5},{5,4},{6,7},{7,6},{8,9},{9,8},{10,11... | collective-permute-start | bytes 786440 | tf_op jit(solution)/shard_map/ppermute | solution.py:458
  24.2 39.6 %copy-start = (bf16[2,64,64]{2,1,0:T(8,128)(2,1)S(1)}, bf16[2,64,64]{2,1,0:T(8,128)(2,1)}, u32[]{:S(2)}) copy-start(bf16[2,64,64]{2,1,0:T(8,128)(2,1)} %wo_ref.3) | copy-start | bytes 49156
  50.9 1.6 %collective-permute-start.8 = (bf16[8,8,16,128]{3,2,1,0:T(8,128)(2,1)S(1)}, bf16[8,8,16,128]{3,2,1,0:T(8,128)(2,1)S(1)}, u32[]{:S(2)}, u32[]{:S(2)}) collective-permute-start(bf16[8,8,16,128]{3,2,1,0:T(8,128)(2,1)S(1)} %get-tuple-element.70), channel_id=1, source_target_pairs={{0,1},{1,0},{2,3},{3,2},{4,5},{5,4},{6,7},{7,6},{8,9},{9,8},{10,11... | collective-permute-start | bytes 786440 | tf_op jit(solution)/shard_map/ppermute | solution.py:515
  52.6 7.4 %collective-permute-start.9 = (bf16[16,16,128]{2,1,0:T(8,128)(2,1)S(1)}, bf16[16,16,128]{2,1,0:T(8,128)(2,1)S(1)}, u32[]{:S(2)}, u32[]{:S(2)}) collective-permute-start(bf16[16,16,128]{2,1,0:T(8,128)(2,1)S(1)} %get-tuple-element.72), channel_id=1, source_target_pairs={{0,2},{1,3},{2,0},{3,1},{4,6},{5,7},{6,4},{7,5},{8,10},{9,11},{10,... | collective-permute-start | bytes 196616 | tf_op jit(solution)/shard_map/ppermute | solution.py:419
  54.1 7.3 %collective-permute-start.10 = (bf16[16,16,128]{2,1,0:T(8,128)(2,1)S(1)}, bf16[16,16,128]{2,1,0:T(8,128)(2,1)S(1)}, u32[]{:S(2)}, u32[]{:S(2)}) collective-permute-start(bf16[16,16,128]{2,1,0:T(8,128)(2,1)S(1)} %get-tuple-element.73), channel_id=1, source_target_pairs={{0,4},{1,5},{2,6},{3,7},{4,0},{5,1},{6,2},{7,3},{8,12},{9,13},{10,... | collective-permute-start | bytes 196616 | tf_op jit(solution)/shard_map/ppermute | solution.py:419
  54.1 10.4 %collective-permute-start.11 = (bf16[16,16,128]{2,1,0:T(8,128)(2,1)S(1)}, bf16[16,16,128]{2,1,0:T(8,128)(2,1)S(1)}, u32[]{:S(2)}, u32[]{:S(2)}) collective-permute-start(bf16[16,16,128]{2,1,0:T(8,128)(2,1)S(1)} %get-tuple-element.74), channel_id=1, source_target_pairs={{0,6},{1,7},{2,4},{3,5},{4,2},{5,3},{6,0},{7,1},{8,14},{9,15},{10,... | collective-permute-start | bytes 196616 | tf_op jit(solution)/shard_map/ppermute | solution.py:419
  56.1 10.1 %collective-permute-start.12 = (bf16[16,16,128]{2,1,0:T(8,128)(2,1)S(1)}, bf16[16,16,128]{2,1,0:T(8,128)(2,1)S(1)}, u32[]{:S(2)}, u32[]{:S(2)}) collective-permute-start(bf16[16,16,128]{2,1,0:T(8,128)(2,1)S(1)} %get-tuple-element.75), channel_id=1, source_target_pairs={{0,8},{1,9},{2,10},{3,11},{4,12},{5,13},{6,14},{7,15},{8,0},{9,1},... | collective-permute-start | bytes 196616 | tf_op jit(solution)/shard_map/ppermute | solution.py:419
  57.2 11.6 %collective-permute-start.13 = (bf16[16,16,128]{2,1,0:T(8,128)(2,1)S(1)}, bf16[16,16,128]{2,1,0:T(8,128)(2,1)S(1)}, u32[]{:S(2)}, u32[]{:S(2)}) collective-permute-start(bf16[16,16,128]{2,1,0:T(8,128)(2,1)S(1)} %get-tuple-element.76), channel_id=1, source_target_pairs={{0,10},{1,11},{2,8},{3,9},{4,14},{5,15},{6,12},{7,13},{8,2},{9,3},... | collective-permute-start | bytes 196616 | tf_op jit(solution)/shard_map/ppermute | solution.py:419
  59.9 8.8 %collective-permute-start.14 = (bf16[16,16,128]{2,1,0:T(8,128)(2,1)S(1)}, bf16[16,16,128]{2,1,0:T(8,128)(2,1)S(1)}, u32[]{:S(2)}, u32[]{:S(2)}) collective-permute-start(bf16[16,16,128]{2,1,0:T(8,128)(2,1)S(1)} %get-tuple-element.77), channel_id=1, source_target_pairs={{0,12},{1,13},{2,14},{3,15},{4,8},{5,9},{6,10},{7,11},{8,4},{9,5},... | collective-permute-start | bytes 196616 | tf_op jit(solution)/shard_map/ppermute | solution.py:419
  61.4 7.4 %collective-permute-start.15 = (bf16[16,16,128]{2,1,0:T(8,128)(2,1)S(1)}, bf16[16,16,128]{2,1,0:T(8,128)(2,1)S(1)}, u32[]{:S(2)}, u32[]{:S(2)}) collective-permute-start(bf16[16,16,128]{2,1,0:T(8,128)(2,1)S(1)} %get-tuple-element.78), channel_id=1, source_target_pairs={{0,14},{1,15},{2,12},{3,13},{4,10},{5,11},{6,8},{7,9},{8,6},{9,7},... | collective-permute-start | bytes 196616 | tf_op jit(solution)/shard_map/ppermute | solution.py:419
  69.6 1.3 %collective-permute-start.16 = (f32[96,128]{1,0:T(8,128)S(1)}, f32[96,128]{1,0:T(8,128)S(1)}, u32[]{:S(2)}, u32[]{:S(2)}) collective-permute-start(f32[96,128]{1,0:T(8,128)S(1)} %get-tuple-element.80), channel_id=1, source_target_pairs={{0,1},{1,0},{2,3},{3,2},{4,5},{5,4},{6,7},{7,6},{8,9},{9,8},{10,11... | collective-permute-start | bytes 147464 | tf_op jit(solution)/shard_map/ppermute | solution.py:548
  83.6 1.3 %collective-permute-start.17 = (f32[104,128]{1,0:T(8,128)S(1)}, f32[104,128]{1,0:T(8,128)S(1)}, u32[]{:S(2)}, u32[]{:S(2)}) collective-permute-start(f32[104,128]{1,0:T(8,128)S(1)} %total.1.after_ref.mine_ref), channel_id=1, source_target_pairs={{0,1},{1,0},{2,3},{3,2},{4,5},{5,4},{6,7},{7,6},{8,9},{9,8},{10,11... | collective-permute-start | bytes 159752 | tf_op jit(solution)/shard_map/ppermute | solution.py:570

commit v6 on v5

--- a/solution.py
+++ b/solution.py
@@ -96,7 +96,7 @@
     if chips:
         per = chans // chips
         for k in range(chips):
-            here = pl.ds(partner_chip(me_ref, k) * (per * count), per * count)
+            here = pl.ds(chunk_chip(me_ref, k, chips) * (per * count), per * count)
             out_refs[k][0:per] = left_scr[here, :].astype(BF16).reshape(per, count, LANES)
             out_refs[k][per:2 * per] = right_scr[here, :].astype(BF16).reshape(per, count, LANES)
         return
@@ -121,8 +121,15 @@
     dout_ref[...] = scr[...].reshape(chans, count, LANES)
 
 
-def partner_chip(me_ref, k):
-    return jnp.bitwise_xor(me_ref[0] // 2, k)
+def chunk_order(chips):
+    half = chips // 2
+    far = [half + (j ^ (half // 2)) for j in range(half)]
+    near = list(range(1, half))
+    return [step for pair in zip(far, near) for step in pair] + far[len(near):] + [0]
+
+
+def chunk_chip(me_ref, k, chips):
+    return jnp.bitwise_xor(me_ref[0] // 2, chunk_order(chips)[k])
 
 
 def collect_kernel(after_ref, *refs):
@@ -150,7 +157,7 @@
             left = slice_rows(left_all, t, rows)
             left_ref[s] = left
             for k in range(chips):
-                chip = partner_chip(me_ref, k)
+                chip = chunk_chip(me_ref, k, chips)
                 for values, half in ((own, core), (got, 1 - core)):
                     start = pl.multiple_of((chip * 2 + half) * rows, rows)
                     scr[s, pl.ds(start, rows), :] = values[k, t * rows:(t + 1) * rows]
@@ -159,14 +166,14 @@
             parts.append(dot_nt(left, right).reshape(chips, rows, width))
         mixed = jnp.concatenate(parts, axis=1).astype(BF16)
         for k in range(chips):
-            out_ref[partner_chip(me_ref, k), c] = mixed[k]
+            out_ref[chunk_chip(me_ref, k, chips), c] = mixed[k]
 
 
 def triangle_back_kernel(rows, me_ref, dmix_ref, left_ref, right_ref, d_left_ref, keep_ref, send_ref, scr):
     chips, per, count, width = d_left_ref.shape
     templ, core = count // rows, me_ref[0] % 2
     for c in range(per):
-        dmix_all = jnp.stack([dmix_ref[partner_chip(me_ref, k), c].astype(F32) for k in range(chips)])
+        dmix_all = jnp.stack([dmix_ref[chunk_chip(me_ref, k, chips), c].astype(F32) for k in range(chips)])
         parts = []
         for t in range(templ):
             s = c * templ + t
@@ -175,7 +182,7 @@
             scr[s] = dot_tn(dmix, left_ref[s])
         d_left_ref[:, c] = jnp.concatenate(parts, axis=1).astype(BF16)
     for k in range(chips):
-        chip = partner_chip(me_ref, k)
+        chip = chunk_chip(me_ref, k, chips)
         for ref, half in ((keep_ref, core), (send_ref, 1 - core)):
             here = pl.ds(pl.multiple_of((chip * 2 + half) * rows, rows), rows)
             for c in range(per):
@@ -268,7 +275,7 @@
     if chips:
         per = chans // chips
         for k in range(chips):
-            here = pl.ds(partner_chip(me_ref, k) * (per * count), per * count)
+            here = pl.ds(chunk_chip(me_ref, k, chips) * (per * count), per * count)
             left_scr[here, :] = in_refs[k][0:per].astype(F32).reshape(per * count, LANES)
             right_scr[here, :] = in_refs[k][per:2 * per].astype(F32).reshape(per * count, LANES)
     else:
@@ -414,10 +421,10 @@
         return [jax.ShapeDtypeStruct((depth, count, width), BF16)] * chips
 
     def send_chunks(parts):
-        got = [parts[0]] + [None] * (chips - 1)
-        for k in reversed(range(1, chips)):
-            got[k] = lax.ppermute(parts[k], "row", [(d, d ^ (2 * k)) for d in range(n)])
-        return got
+        return [
+            lax.ppermute(part, "row", [(d, d ^ (2 * step)) for d in range(n)]) if step else part
+            for part, step in zip(parts, chunk_order(chips))
+        ]
 
     *projected, zn, fac, normed, rstd = call(
         "project",

time: 86 us -> 81.7 us (0.950)
  waiting for transfers between devices: 13.7 us -> 10.1 us
  blocking collectives: 37.8 us -> 36.4 us
    ppermute x14, waiting for transfers between devices: 9.68 us -> 6.08 us  [send_chunks(): lax.ppermute(part, 'row', [(d, d ^ 2 * step) for d in range(n)])]
    all_to_all x3, blocking collectives: 37.8 us -> 36.4 us  [exchange(): lax.all_to_all(x, 'row', split_axis=0, concat_axis=0, axis_index_groups=g...]
  transfers between devices with their start and end apart: 18 -> 18, of which waited for: 8 -> 8; matrix products, arithmetic and copies ran while one was open for 0% -> 0% of each run, Pallas kernels for 4% -> 5%
where the time goes in v6:
time: 81.7 us; the launch traced here: 81.4 us
  blocking collectives  36.4 us (45%)
  starting transfers between devices  24.7 us (30%)
  waiting for transfers between devices  10.1 us (12%)
  Pallas kernels  9.44 us (12%)
    all_to_all x3, blocking collectives, exchange(): lax.all_to_all(x, 'row', split_axis=0, concat_axis=0, axis_index_groups=g...  36.4 us
    ppermute x14, starting transfers between devices, send_chunks(): lax.ppermute(part, 'row', [(d, d ^ 2 * step) for d in range(n)])  24.4 us
    pallas_call x7, Pallas kernels, call(): pl.pallas_call(kernel, grid=() if blocks == 1 else (blocks,), in_specs=in...  7.53 us
    ppermute x14, waiting for transfers between devices, send_chunks(): lax.ppermute(part, 'row', [(d, d ^ 2 * step) for d in range(n)])  6.08 us
    ppermute x2, waiting for transfers between devices, per_device(): got = lax.ppermute(send, 'row', partner)  2.25 us
  transfers between devices with their start and end apart: 18, of which 8 were waited for; matrix products, arithmetic and copies ran while one was open for 0% of the time, Pallas kernels for 5%

profile of v6, /device:TPU:0, one launch (start us, length us, event | category | flops | bytes accessed | tf_op | source)
XLA Modules:
  0.0 81.4 jit_solution(1887702351073677182)
XLA Ops:
  0.6 1.9 %project.1 = (bf16[16,16,128]{2,1,0:T(8,128)(2,1)S(1)}, bf16[16,16,128]{2,1,0:T(8,128)(2,1)S(1)}, bf16[16,16,128]{2,1,0:T(8,128)(2,1)S(1)}, bf16[16,16,128]{2,1,...) custom-call(s32[1]{0:T(128)} %bitcast.me_ref, ...), custom_call_target="tpu_custom_call" | custom-call | tf_op jit(solution)/shard_map/project/pallas_call | solution.py:392
  2.5 5.1 %collective-permute-start = (bf16[16,16,128]{2,1,0:T(8,128)(2,1)S(1)}, bf16[16,16,128]{2,1,0:T(8,128)(2,1)S(1)}, u32[]{:S(2)}, u32[]{:S(2)}) collective-permute-start(bf16[16,16,128]{2,1,0:T(8,128)(2,1)S(1)} %get-tuple-element.50), channel_id=1, source_target_pairs={{0,12},{1,13},{2,14},{3,15},{4,8},{5,9},{6,10},{7,11},{8,4},{9,5},... | collective-permute-start | bytes 196616 | tf_op jit(solution)/shard_map/ppermute | solution.py:425
  7.7 1.5 %collective-permute-start.1 = (bf16[16,16,128]{2,1,0:T(8,128)(2,1)S(1)}, bf16[16,16,128]{2,1,0:T(8,128)(2,1)S(1)}, u32[]{:S(2)}, u32[]{:S(2)}) collective-permute-start(bf16[16,16,128]{2,1,0:T(8,128)(2,1)S(1)} %get-tuple-element.51), channel_id=1, source_target_pairs={{0,2},{1,3},{2,0},{3,1},{4,6},{5,7},{6,4},{7,5},{8,10},{9,11},{10,... | collective-permute-start | bytes 196616 | tf_op jit(solution)/shard_map/ppermute | solution.py:425
  9.2 4.3 %collective-permute-start.4 = (bf16[16,16,128]{2,1,0:T(8,128)(2,1)S(1)}, bf16[16,16,128]{2,1,0:T(8,128)(2,1)S(1)}, u32[]{:S(2)}, u32[]{:S(2)}) collective-permute-start(bf16[16,16,128]{2,1,0:T(8,128)(2,1)S(1)} %get-tuple-element.54), channel_id=1, source_target_pairs={{0,8},{1,9},{2,10},{3,11},{4,12},{5,13},{6,14},{7,15},{8,0},{9,1},... | collective-permute-start | bytes 196616 | tf_op jit(solution)/shard_map/ppermute | solution.py:425
  13.5 1.0 %collective-permute-start.5 = (bf16[16,16,128]{2,1,0:T(8,128)(2,1)S(1)}, bf16[16,16,128]{2,1,0:T(8,128)(2,1)S(1)}, u32[]{:S(2)}, u32[]{:S(2)}) collective-permute-start(bf16[16,16,128]{2,1,0:T(8,128)(2,1)S(1)} %get-tuple-element.55), channel_id=1, source_target_pairs={{0,6},{1,7},{2,4},{3,5},{4,2},{5,3},{6,0},{7,1},{8,14},{9,15},{10,... | collective-permute-start | bytes 196616 | tf_op jit(solution)/shard_map/ppermute | solution.py:425
  14.5 1.3 %collective-permute-start.6 = (bf16[16,16,128]{2,1,0:T(8,128)(2,1)S(1)}, bf16[16,16,128]{2,1,0:T(8,128)(2,1)S(1)}, u32[]{:S(2)}, u32[]{:S(2)}) collective-permute-start(bf16[16,16,128]{2,1,0:T(8,128)(2,1)S(1)} %get-tuple-element.56), channel_id=1, source_target_pairs={{0,10},{1,11},{2,8},{3,9},{4,14},{5,15},{6,12},{7,13},{8,2},{9,3},... | collective-permute-start | bytes 196616 | tf_op jit(solution)/shard_map/ppermute | solution.py:425
  15.8 1.6 %prepare.1 = (f32[1,64,2048]{2,1,0:T(8,128)S(1)}, bf16[1,64,2048]{2,1,0:T(8,128)(2,1)S(1)}, f32[64,16,128]{2,1,0:T(8,128)S(1)}, bf16[64,320]{1,0:T(8,128)(2,1)S(1)}) custom-call(bf16[16,64,128]{2,1,0:T(8,128)(2,1)} %bitcast.12, bf16[1,64,2048]{2,1,0:T(8,128)(2,1)S(1)} %get-tuple-element.48.zn_ref, bf16[4,64,64]{2,1,0:T(8,128)(2,1)} %w_ref.3, ...), custom_call_target="tpu_custom_call" | custom-call | tf_op jit(solution)/shard_map/prepare/pallas_call | solution.py:392
  17.4 2.0 %collective-permute-done.5.refs_5_ = bf16[16,16,128]{2,1,0:T(8,128)(2,1)S(1)} collective-permute-done((bf16[16,16,128]{2,1,0:T(8,128)(2,1)S(1)}, bf16[16,16,128]{2,1,0:T(8,128)(2,1)S(1)}, u32[]{:S(2)}, u32[]{:S(2)}) %collective-permute-start.5) | collective-permute-done | bytes 65568 | tf_op jit(solution)/shard_map/ppermute | solution.py:425
  19.4 1.2 %collective-permute-done.6.refs_6_ = bf16[16,16,128]{2,1,0:T(8,128)(2,1)S(1)} collective-permute-done((bf16[16,16,128]{2,1,0:T(8,128)(2,1)S(1)}, bf16[16,16,128]{2,1,0:T(8,128)(2,1)S(1)}, u32[]{:S(2)}, u32[]{:S(2)}) %collective-permute-start.6) | collective-permute-done | bytes 65568 | tf_op jit(solution)/shard_map/ppermute | solution.py:425
  20.7 1.5 %collective-permute-done.7.refs_9_ = bf16[8,8,16,128]{3,2,1,0:T(8,128)(2,1)S(1)} collective-permute-done((bf16[8,8,16,128]{3,2,1,0:T(8,128)(2,1)S(1)}, bf16[8,8,16,128]{3,2,1,0:T(8,128)(2,1)S(1)}, u32[]{:S(2)}, u32[]{:S(2)}) %collective-permute-start.7) | collective-permute-done | bytes 262176 | tf_op jit(solution)/shard_map/ppermute | solution.py:465
  22.2 0.5 mixed.1
  22.7 12.4 %all_to_all.15 = bf16[8,8,16,128]{3,2,1,0:T(8,128)(2,1)S(1)} all-to-all(bf16[8,8,16,128]{3,2,1,0:T(8,128)(2,1)S(1)} %get-tuple-element.59), channel_id=1, replica_groups={{0,2,4,6,8,10,12,14},{1,3,5,7,9,11,13,15},{16,18,20,22,24,26,28,30},{17..., dimensions={0} | all-to-all | bytes 524288 | tf_op jit(solution)/shard_map/all_to_all | solution.py:359
  35.1 1.0 %middle.1 = (bf16[64,16,128]{2,1,0:T(8,128)(2,1)S(1)}, f32[64,16,128]{2,1,0:T(8,128)S(1)}, f32[64,128]{1,0:T(8,128)S(1)}) custom-call(f32[2,64]{1,0:T(2,128)S(1)} %copy-done.1, f32[64,16,128]{2,1,0:T(8,128)S(1)} %get-tuple-element.49.dout_ref, bf16[64,16,128]{2,1,0:T(8,128)(2,1)S(1)} %bitcast.9), custom_call_target="tpu_custom_call" | custom-call | tf_op jit(solution)/shard_map/middle/pallas_call | solution.py:392
  36.1 12.0 %all_to_all.16.dmix_ref = bf16[8,8,16,128]{3,2,1,0:T(8,128)(2,1)S(1)} all-to-all(bf16[8,8,16,128]{3,2,1,0:T(8,128)(2,1)S(1)} %bitcast.10), channel_id=1, replica_groups={{0,2,4,6,8,10,12,14},{1,3,5,7,9,11,13,15},{16,18,20,22,24,26,28,30},{17..., dimensions={0} | all-to-all | bytes 524288 | tf_op jit(solution)/shard_map/all_to_all | solution.py:359
  48.1 0.6 triangle_back.1
  48.7 1.5 %collective-permute-done.8.got_ref = bf16[8,8,16,128]{3,2,1,0:T(8,128)(2,1)S(1)} collective-permute-done((bf16[8,8,16,128]{3,2,1,0:T(8,128)(2,1)S(1)}, bf16[8,8,16,128]{3,2,1,0:T(8,128)(2,1)S(1)}, u32[]{:S(2)}, u32[]{:S(2)}) %collective-permute-start.8) | collective-permute-done | bytes 262176 | tf_op jit(solution)/shard_map/ppermute | solution.py:522
  50.3 1.2 %collective-permute-start.9 = (bf16[16,16,128]{2,1,0:T(8,128)(2,1)S(1)}, bf16[16,16,128]{2,1,0:T(8,128)(2,1)S(1)}, u32[]{:S(2)}, u32[]{:S(2)}) collective-permute-start(bf16[16,16,128]{2,1,0:T(8,128)(2,1)S(1)} %get-tuple-element.71), channel_id=1, source_target_pairs={{0,12},{1,13},{2,14},{3,15},{4,8},{5,9},{6,10},{7,11},{8,4},{9,5},... | collective-permute-start | bytes 196616 | tf_op jit(solution)/shard_map/ppermute | solution.py:425
  51.5 1.7 %collective-permute-start.10 = (bf16[16,16,128]{2,1,0:T(8,128)(2,1)S(1)}, bf16[16,16,128]{2,1,0:T(8,128)(2,1)S(1)}, u32[]{:S(2)}, u32[]{:S(2)}) collective-permute-start(bf16[16,16,128]{2,1,0:T(8,128)(2,1)S(1)} %get-tuple-element.72), channel_id=1, source_target_pairs={{0,2},{1,3},{2,0},{3,1},{4,6},{5,7},{6,4},{7,5},{8,10},{9,11},{10,... | collective-permute-start | bytes 196616 | tf_op jit(solution)/shard_map/ppermute | solution.py:425
  53.2 2.4 %collective-permute-start.11 = (bf16[16,16,128]{2,1,0:T(8,128)(2,1)S(1)}, bf16[16,16,128]{2,1,0:T(8,128)(2,1)S(1)}, u32[]{:S(2)}, u32[]{:S(2)}) collective-permute-start(bf16[16,16,128]{2,1,0:T(8,128)(2,1)S(1)} %get-tuple-element.73), channel_id=1, source_target_pairs={{0,14},{1,15},{2,12},{3,13},{4,10},{5,11},{6,8},{7,9},{8,6},{9,7},... | collective-permute-start | bytes 196616 | tf_op jit(solution)/shard_map/ppermute | solution.py:425
  55.6 1.7 %collective-permute-start.13 = (bf16[16,16,128]{2,1,0:T(8,128)(2,1)S(1)}, bf16[16,16,128]{2,1,0:T(8,128)(2,1)S(1)}, u32[]{:S(2)}, u32[]{:S(2)}) collective-permute-start(bf16[16,16,128]{2,1,0:T(8,128)(2,1)S(1)} %get-tuple-element.75), channel_id=1, source_target_pairs={{0,8},{1,9},{2,10},{3,11},{4,12},{5,13},{6,14},{7,15},{8,0},{9,1},... | collective-permute-start | bytes 196616 | tf_op jit(solution)/shard_map/ppermute | solution.py:425
  57.3 1.2 %collective-permute-start.14 = (bf16[16,16,128]{2,1,0:T(8,128)(2,1)S(1)}, bf16[16,16,128]{2,1,0:T(8,128)(2,1)S(1)}, u32[]{:S(2)}, u32[]{:S(2)}) collective-permute-start(bf16[16,16,128]{2,1,0:T(8,128)(2,1)S(1)} %get-tuple-element.76), channel_id=1, source_target_pairs={{0,6},{1,7},{2,4},{3,5},{4,2},{5,3},{6,0},{7,1},{8,14},{9,15},{10,... | collective-permute-start | bytes 196616 | tf_op jit(solution)/shard_map/ppermute | solution.py:425
  58.6 2.9 %collective-permute-start.15 = (bf16[16,16,128]{2,1,0:T(8,128)(2,1)S(1)}, bf16[16,16,128]{2,1,0:T(8,128)(2,1)S(1)}, u32[]{:S(2)}, u32[]{:S(2)}) collective-permute-start(bf16[16,16,128]{2,1,0:T(8,128)(2,1)S(1)} %get-tuple-element.77), channel_id=1, source_target_pairs={{0,10},{1,11},{2,8},{3,9},{4,14},{5,15},{6,12},{7,13},{8,2},{9,3},... | collective-permute-start | bytes 196616 | tf_op jit(solution)/shard_map/ppermute | solution.py:425
  61.5 0.7 update.1
  62.3 1.2 %collective-permute-done.13.refs_4_ = bf16[16,16,128]{2,1,0:T(8,128)(2,1)S(1)} collective-permute-done((bf16[16,16,128]{2,1,0:T(8,128)(2,1)S(1)}, bf16[16,16,128]{2,1,0:T(8,128)(2,1)S(1)}, u32[]{:S(2)}, u32[]{:S(2)}) %collective-permute-start.13) | collective-permute-done | bytes 65568 | tf_op jit(solution)/shard_map/ppermute | solution.py:425
  63.4 1.7 %collective-permute-done.14.refs_5_ = bf16[16,16,128]{2,1,0:T(8,128)(2,1)S(1)} collective-permute-done((bf16[16,16,128]{2,1,0:T(8,128)(2,1)S(1)}, bf16[16,16,128]{2,1,0:T(8,128)(2,1)S(1)}, u32[]{:S(2)}, u32[]{:S(2)}) %collective-permute-start.14) | collective-permute-done | bytes 65568 | tf_op jit(solution)/shard_map/ppermute | solution.py:425
  65.1 0.8 %gating_back.1 = (bf16[1,256,2048]{2,1,0:T(8,128)(2,1)S(1)}, f32[96,128]{1,0:T(8,128)S(1)}, f32[96,128]{1,0:T(8,128)S(1)}) custom-call(s32[1]{0:T(128)} %bitcast.me_ref, f32[1,256,2048]{2,1,0:T(8,128)S(1)} %get-tuple-element.47.fac_ref, bf16[1,64,2048]{2,1,0:T(8,128)(2,1)S(1)} %get-tuple-element.48.zn_ref, f32[72,128]{1,0:T(8,128)S(1)} %get-tuple-element.64.grads_ref, ...), custom_call_target="tpu_custom_call" | custom-call | tf_op jit(solution)/shard_map/gating_back/pallas_call | solution.py:392
  66.0 0.5 input_grad.1
  66.5 0.7 collective-permute-done.16.got_ref
  67.3 12.0 %all_to_all.17.pack_ref = bf16[8,104,128]{2,1,0:T(8,128)(2,1)S(1)} all-to-all(bf16[8,104,128]{2,1,0:T(8,128)(2,1)S(1)} %combine.1), channel_id=1, replica_groups={{0,2,4,6,8,10,12,14},{1,3,5,7,9,11,13,15},{16,18,20,22,24,26,28,30},{17..., dimensions={0} | all-to-all | bytes 425984 | tf_op jit(solution)/shard_map/all_to_all | solution.py:359
  79.4 1.0 %pair_grad.1 = bf16[16,64,128]{2,1,0:T(8,128)(2,1)} custom-call(f32[104,128]{1,0:T(8,128)S(1)} %total.1.after_ref.mine_ref, f32[1,64,2048]{2,1,0:T(8,128)S(1)} %get-tuple-element.85.dzn_ref, f32[1,64,2048]{2,1,0:T(8,128)S(1)} %get-tuple-element.83.normed_ref, f32[1,1,2048]{2,1,0:T(1,128)S(1)} %get-tuple-element.86.rstd_ref, f32[2,64]{1,0:T(2,128)S(1)} %copy-done.1), custom_call_target="tpu_custom_call" | custom-call | tf_op jit(solution)/shard_map/pair_grad/pallas_call | solution.py:392
  80.4 0.2 collective-permute-done.17.got_ref
  80.7 0.8 unpack.1
  (25 shorter events, 0.5 us)
Async XLA Ops:
  0.6 34.5 %copy-start.1 = (f32[2,64]{1,0:T(2,128)S(1)}, f32[2,64]{1,0:T(2,128)}, u32[]{:S(2)}) copy-start(f32[2,64]{1,0:T(2,128)} %gains_ref.5) | copy-start | bytes 1540
  2.5 11.0 %collective-permute-start = (bf16[16,16,128]{2,1,0:T(8,128)(2,1)S(1)}, bf16[16,16,128]{2,1,0:T(8,128)(2,1)S(1)}, u32[]{:S(2)}, u32[]{:S(2)}) collective-permute-start(bf16[16,16,128]{2,1,0:T(8,128)(2,1)S(1)} %get-tuple-element.50), channel_id=1, source_target_pairs={{0,12},{1,13},{2,14},{3,15},{4,8},{5,9},{6,10},{7,11},{8,4},{9,5},... | collective-permute-start | bytes 196616 | tf_op jit(solution)/shard_map/ppermute | solution.py:425
  7.7 6.8 %collective-permute-start.1 = (bf16[16,16,128]{2,1,0:T(8,128)(2,1)S(1)}, bf16[16,16,128]{2,1,0:T(8,128)(2,1)S(1)}, u32[]{:S(2)}, u32[]{:S(2)}) collective-permute-start(bf16[16,16,128]{2,1,0:T(8,128)(2,1)S(1)} %get-tuple-element.51), channel_id=1, source_target_pairs={{0,2},{1,3},{2,0},{3,1},{4,6},{5,7},{6,4},{7,5},{8,10},{9,11},{10,... | collective-permute-start | bytes 196616 | tf_op jit(solution)/shard_map/ppermute | solution.py:425
  9.2 8.2 %collective-permute-start.2 = (bf16[16,16,128]{2,1,0:T(8,128)(2,1)S(1)}, bf16[16,16,128]{2,1,0:T(8,128)(2,1)S(1)}, u32[]{:S(2)}, u32[]{:S(2)}) collective-permute-start(bf16[16,16,128]{2,1,0:T(8,128)(2,1)S(1)} %get-tuple-element.52), channel_id=1, source_target_pairs={{0,14},{1,15},{2,12},{3,13},{4,10},{5,11},{6,8},{7,9},{8,6},{9,7},... | collective-permute-start | bytes 196616 | tf_op jit(solution)/shard_map/ppermute | solution.py:425
  9.2 8.2 %collective-permute-start.3 = (bf16[16,16,128]{2,1,0:T(8,128)(2,1)S(1)}, bf16[16,16,128]{2,1,0:T(8,128)(2,1)S(1)}, u32[]{:S(2)}, u32[]{:S(2)}) collective-permute-start(bf16[16,16,128]{2,1,0:T(8,128)(2,1)S(1)} %get-tuple-element.53), channel_id=1, source_target_pairs={{0,4},{1,5},{2,6},{3,7},{4,0},{5,1},{6,2},{7,3},{8,12},{9,13},{10,... | collective-permute-start | bytes 196616 | tf_op jit(solution)/shard_map/ppermute | solution.py:425
  9.2 8.2 %collective-permute-start.4 = (bf16[16,16,128]{2,1,0:T(8,128)(2,1)S(1)}, bf16[16,16,128]{2,1,0:T(8,128)(2,1)S(1)}, u32[]{:S(2)}, u32[]{:S(2)}) collective-permute-start(bf16[16,16,128]{2,1,0:T(8,128)(2,1)S(1)} %get-tuple-element.54), channel_id=1, source_target_pairs={{0,8},{1,9},{2,10},{3,11},{4,12},{5,13},{6,14},{7,15},{8,0},{9,1},... | collective-permute-start | bytes 196616 | tf_op jit(solution)/shard_map/ppermute | solution.py:425
  13.5 5.8 %collective-permute-start.5 = (bf16[16,16,128]{2,1,0:T(8,128)(2,1)S(1)}, bf16[16,16,128]{2,1,0:T(8,128)(2,1)S(1)}, u32[]{:S(2)}, u32[]{:S(2)}) collective-permute-start(bf16[16,16,128]{2,1,0:T(8,128)(2,1)S(1)} %get-tuple-element.55), channel_id=1, source_target_pairs={{0,6},{1,7},{2,4},{3,5},{4,2},{5,3},{6,0},{7,1},{8,14},{9,15},{10,... | collective-permute-start | bytes 196616 | tf_op jit(solution)/shard_map/ppermute | solution.py:425
  14.5 6.1 %collective-permute-start.6 = (bf16[16,16,128]{2,1,0:T(8,128)(2,1)S(1)}, bf16[16,16,128]{2,1,0:T(8,128)(2,1)S(1)}, u32[]{:S(2)}, u32[]{:S(2)}) collective-permute-start(bf16[16,16,128]{2,1,0:T(8,128)(2,1)S(1)} %get-tuple-element.56), channel_id=1, source_target_pairs={{0,10},{1,11},{2,8},{3,9},{4,14},{5,15},{6,12},{7,13},{8,2},{9,3},... | collective-permute-start | bytes 196616 | tf_op jit(solution)/shard_map/ppermute | solution.py:425
  20.6 1.6 %collective-permute-start.7 = (bf16[8,8,16,128]{3,2,1,0:T(8,128)(2,1)S(1)}, bf16[8,8,16,128]{3,2,1,0:T(8,128)(2,1)S(1)}, u32[]{:S(2)}, u32[]{:S(2)}) collective-permute-start(bf16[8,8,16,128]{3,2,1,0:T(8,128)(2,1)S(1)} %collect.1.refs_8_), channel_id=1, source_target_pairs={{0,1},{1,0},{2,3},{3,2},{4,5},{5,4},{6,7},{7,6},{8,9},{9,8},{10,11... | collective-permute-start | bytes 786440 | tf_op jit(solution)/shard_map/ppermute | solution.py:465
  22.7 38.8 %copy-start = (bf16[2,64,64]{2,1,0:T(8,128)(2,1)S(1)}, bf16[2,64,64]{2,1,0:T(8,128)(2,1)}, u32[]{:S(2)}) copy-start(bf16[2,64,64]{2,1,0:T(8,128)(2,1)} %wo_ref.3) | copy-start | bytes 49156
  48.6 1.6 %collective-permute-start.8 = (bf16[8,8,16,128]{3,2,1,0:T(8,128)(2,1)S(1)}, bf16[8,8,16,128]{3,2,1,0:T(8,128)(2,1)S(1)}, u32[]{:S(2)}, u32[]{:S(2)}) collective-permute-start(bf16[8,8,16,128]{3,2,1,0:T(8,128)(2,1)S(1)} %get-tuple-element.70), channel_id=1, source_target_pairs={{0,1},{1,0},{2,3},{3,2},{4,5},{5,4},{6,7},{7,6},{8,9},{9,8},{10,11... | collective-permute-start | bytes 786440 | tf_op jit(solution)/shard_map/ppermute | solution.py:522
  50.3 7.1 %collective-permute-start.9 = (bf16[16,16,128]{2,1,0:T(8,128)(2,1)S(1)}, bf16[16,16,128]{2,1,0:T(8,128)(2,1)S(1)}, u32[]{:S(2)}, u32[]{:S(2)}) collective-permute-start(bf16[16,16,128]{2,1,0:T(8,128)(2,1)S(1)} %get-tuple-element.71), channel_id=1, source_target_pairs={{0,12},{1,13},{2,14},{3,15},{4,8},{5,9},{6,10},{7,11},{8,4},{9,5},... | collective-permute-start | bytes 196616 | tf_op jit(solution)/shard_map/ppermute | solution.py:425
  51.5 7.1 %collective-permute-start.10 = (bf16[16,16,128]{2,1,0:T(8,128)(2,1)S(1)}, bf16[16,16,128]{2,1,0:T(8,128)(2,1)S(1)}, u32[]{:S(2)}, u32[]{:S(2)}) collective-permute-start(bf16[16,16,128]{2,1,0:T(8,128)(2,1)S(1)} %get-tuple-element.72), channel_id=1, source_target_pairs={{0,2},{1,3},{2,0},{3,1},{4,6},{5,7},{6,4},{7,5},{8,10},{9,11},{10,... | collective-permute-start | bytes 196616 | tf_op jit(solution)/shard_map/ppermute | solution.py:425
  53.2 9.0 %collective-permute-start.11 = (bf16[16,16,128]{2,1,0:T(8,128)(2,1)S(1)}, bf16[16,16,128]{2,1,0:T(8,128)(2,1)S(1)}, u32[]{:S(2)}, u32[]{:S(2)}) collective-permute-start(bf16[16,16,128]{2,1,0:T(8,128)(2,1)S(1)} %get-tuple-element.73), channel_id=1, source_target_pairs={{0,14},{1,15},{2,12},{3,13},{4,10},{5,11},{6,8},{7,9},{8,6},{9,7},... | collective-permute-start | bytes 196616 | tf_op jit(solution)/shard_map/ppermute | solution.py:425
  55.6 6.6 %collective-permute-start.12 = (bf16[16,16,128]{2,1,0:T(8,128)(2,1)S(1)}, bf16[16,16,128]{2,1,0:T(8,128)(2,1)S(1)}, u32[]{:S(2)}, u32[]{:S(2)}) collective-permute-start(bf16[16,16,128]{2,1,0:T(8,128)(2,1)S(1)} %get-tuple-element.74), channel_id=1, source_target_pairs={{0,4},{1,5},{2,6},{3,7},{4,0},{5,1},{6,2},{7,3},{8,12},{9,13},{10,... | collective-permute-start | bytes 196616 | tf_op jit(solution)/shard_map/ppermute | solution.py:425
  55.6 7.8 %collective-permute-start.13 = (bf16[16,16,128]{2,1,0:T(8,128)(2,1)S(1)}, bf16[16,16,128]{2,1,0:T(8,128)(2,1)S(1)}, u32[]{:S(2)}, u32[]{:S(2)}) collective-permute-start(bf16[16,16,128]{2,1,0:T(8,128)(2,1)S(1)} %get-tuple-element.75), channel_id=1, source_target_pairs={{0,8},{1,9},{2,10},{3,11},{4,12},{5,13},{6,14},{7,15},{8,0},{9,1},... | collective-permute-start | bytes 196616 | tf_op jit(solution)/shard_map/ppermute | solution.py:425
  57.3 7.8 %collective-permute-start.14 = (bf16[16,16,128]{2,1,0:T(8,128)(2,1)S(1)}, bf16[16,16,128]{2,1,0:T(8,128)(2,1)S(1)}, u32[]{:S(2)}, u32[]{:S(2)}) collective-permute-start(bf16[16,16,128]{2,1,0:T(8,128)(2,1)S(1)} %get-tuple-element.76), channel_id=1, source_target_pairs={{0,6},{1,7},{2,4},{3,5},{4,2},{5,3},{6,0},{7,1},{8,14},{9,15},{10,... | collective-permute-start | bytes 196616 | tf_op jit(solution)/shard_map/ppermute | solution.py:425
  58.6 6.5 %collective-permute-start.15 = (bf16[16,16,128]{2,1,0:T(8,128)(2,1)S(1)}, bf16[16,16,128]{2,1,0:T(8,128)(2,1)S(1)}, u32[]{:S(2)}, u32[]{:S(2)}) collective-permute-start(bf16[16,16,128]{2,1,0:T(8,128)(2,1)S(1)} %get-tuple-element.77), channel_id=1, source_target_pairs={{0,10},{1,11},{2,8},{3,9},{4,14},{5,15},{6,12},{7,13},{8,2},{9,3},... | collective-permute-start | bytes 196616 | tf_op jit(solution)/shard_map/ppermute | solution.py:425
  66.0 1.3 %collective-permute-start.16 = (f32[96,128]{1,0:T(8,128)S(1)}, f32[96,128]{1,0:T(8,128)S(1)}, u32[]{:S(2)}, u32[]{:S(2)}) collective-permute-start(f32[96,128]{1,0:T(8,128)S(1)} %get-tuple-element.80), channel_id=1, source_target_pairs={{0,1},{1,0},{2,3},{3,2},{4,5},{5,4},{6,7},{7,6},{8,9},{9,8},{10,11... | collective-permute-start | bytes 147464 | tf_op jit(solution)/shard_map/ppermute | solution.py:555
  79.3 1.3 %collective-permute-start.17 = (f32[104,128]{1,0:T(8,128)S(1)}, f32[104,128]{1,0:T(8,128)S(1)}, u32[]{:S(2)}, u32[]{:S(2)}) collective-permute-start(f32[104,128]{1,0:T(8,128)S(1)} %total.1.after_ref.mine_ref), channel_id=1, source_target_pairs={{0,1},{1,0},{2,3},{3,2},{4,5},{5,4},{6,7},{7,6},{8,9},{9,8},{10,11... | collective-permute-start | bytes 159752 | tf_op jit(solution)/shard_map/ppermute | solution.py:577

commit v7 on v6

--- a/solution.py
+++ b/solution.py
@@ -216,7 +216,7 @@
     return [tree_sum(list(parts)) * scale for parts in zip(*accs)]
 
 
-def middle_kernel(block, gains_ref, dout_ref, mixed_ref, dmix_ref, outn_ref, norm_ref):
+def middle_kernel(block, gains_ref, dout_ref, mixed_ref, dmix_ref, stats_ref):
     chans = dout_ref.shape[0]
     inv = 1.0 / chans
 
@@ -236,20 +236,20 @@
     rstd = lax.rsqrt(variance + EPS)
     mean_p = mean_p * rstd
 
-    @pl.when(block() == 0)
-    def _():
-        norm_ref[...] = jnp.zeros_like(norm_ref)
-
+    stats_ref[0] = mean
+    stats_ref[1] = rstd
     for c in range(chans):
         xhat = (mixed(c) - mean) * rstd
-        outn_ref[c] = xhat * gains_ref[1, c]
-        norm_ref[c:c + 1, :] += jnp.sum(dout_ref[c] * xhat, axis=0, keepdims=True)
         dmix_ref[c] = (rstd * (scaled(c) - mean_h - xhat * mean_p)).astype(BF16)
 
 
-def update_kernel(block, outn_ref, norm_ref, zn_ref, cg_ref, du_ref, wo_ref, dgate_ref, grads_ref, scr, outn_scr):
-    chans, count, _ = outn_ref.shape
-    scr[...] = outn_ref[...].reshape(chans * count, LANES)
+def update_kernel(block, gains_ref, mixed_ref, dout_ref, stats_ref, zn_ref, cg_ref, du_ref, wo_ref, dgate_ref, grads_ref, scr, norm_scr, outn_scr):
+    chans, count, _ = mixed_ref.shape
+    mean, rstd = stats_ref[0], stats_ref[1]
+    for c in range(chans):
+        xhat = (mixed_ref[c].astype(F32) - mean) * rstd
+        scr[c * count:(c + 1) * count, :] = xhat * gains_ref[1, c]
+        norm_scr[c:c + 1, :] = jnp.sum(dout_ref[c] * xhat, axis=0, keepdims=True)
     for pos in range(count):
         span = slice(pos * LANES, (pos + 1) * LANES)
         outn_scr[:, span] = scr[pl.ds(pos, chans, stride=count), :].astype(BF16)
@@ -265,7 +265,7 @@
 
     grads_ref[0:chans, 0:chans] += gate_grad
     grads_ref[0:chans, chans:2 * chans] += out_grad
-    grads_ref[chans:chans + 1, 0:chans] = as_row(jnp.sum(norm_ref[...], axis=1, keepdims=True))
+    grads_ref[chans:chans + 1, 0:chans] += as_row(jnp.sum(norm_scr[...], axis=1, keepdims=True))
 
 
 def gating_back_kernel(blocks, chips, block, me_ref, fac_ref, zn_ref, grads_ref, *refs):
@@ -485,16 +485,16 @@
         mixed = mixed.astype(BF16).reshape(slices, n, rows, width).transpose(1, 0, 2, 3)
         mixed_rows = exchange(mixed.reshape(n * slices, rows, width)).reshape(chans, count, width)
 
-    d_mixed, outn, norm_sums = call(
+    stats_spec = block_spec((2, count, LANES), lambda b: (0, 0, b))
+    d_mixed, stats = call(
         "middle",
         middle_kernel,
         (layer_norm_gains, d_outn, mixed_rows),
         [smem, chan_spec, chan_spec],
-        [chan_spec, chan_spec, full((chans, LANES))],
+        [chan_spec, stats_spec],
         [
             jax.ShapeDtypeStruct((chans, count, width), BF16),
-            array((chans, count, width), F32),
-            array((chans, LANES), F32),
+            array((2, count, width), F32),
         ],
     )
     if direct:
@@ -503,11 +503,11 @@
     d_gate, out_grads = call(
         "update",
         update_kernel,
-        (outn, norm_sums, zn, cg, d_update, w_out),
-        [chan_spec, full((chans, LANES)), cat_spec, cat_spec, cat_spec, wo_spec],
+        (layer_norm_gains, mixed_rows, d_outn, stats, zn, cg, d_update, w_out),
+        [smem, chan_spec, chan_spec, stats_spec, cat_spec, cat_spec, cat_spec, wo_spec],
         [cat_spec, full((chans + 8, 2 * chans))],
         [cat(BF16), array((chans + 8, 2 * chans), F32)],
-        [scratch, pltpu.VMEM((chans, lanes), BF16)],
+        [scratch, pltpu.VMEM((chans, LANES), F32), pltpu.VMEM((chans, lanes), BF16)],
     )
 
     if direct:

time: 81.7 us -> 81.6 us (level)
  no operation moved by 1% of the time
where the time goes in v7:
time: 81.6 us; the launch traced here: 81.3 us
  blocking collectives  36.4 us (45%)
  starting transfers between devices  24.7 us (30%)
  Pallas kernels  9.95 us (12%)
  waiting for transfers between devices  9.48 us (12%)
    all_to_all x3, blocking collectives, exchange(): lax.all_to_all(x, 'row', split_axis=0, concat_axis=0, axis_index_groups=g...  36.4 us
    ppermute x14, starting transfers between devices, send_chunks(): lax.ppermute(part, 'row', [(d, d ^ 2 * step) for d in range(n)])  24.4 us
    pallas_call x7, Pallas kernels, call(): pl.pallas_call(kernel, grid=() if blocks == 1 else (blocks,), in_specs=in...  8.03 us
    ppermute x14, waiting for transfers between devices, send_chunks(): lax.ppermute(part, 'row', [(d, d ^ 2 * step) for d in range(n)])  5.47 us
    ppermute x2, waiting for transfers between devices, per_device(): got = lax.ppermute(send, 'row', partner)  2.25 us
  transfers between devices with their start and end apart: 18, of which 8 were waited for; matrix products, arithmetic and copies ran while one was open for 0% of the time, Pallas kernels for 5%

profile of v7, /device:TPU:0, one launch (start us, length us, event | category | flops | bytes accessed | tf_op | source)
XLA Modules:
  0.0 81.3 jit_solution(3492599302944179461)
XLA Ops:
  0.6 1.9 %project.1 = (bf16[16,16,128]{2,1,0:T(8,128)(2,1)S(1)}, bf16[16,16,128]{2,1,0:T(8,128)(2,1)S(1)}, bf16[16,16,128]{2,1,0:T(8,128)(2,1)S(1)}, bf16[16,16,128]{2,1,...) custom-call(s32[1]{0:T(128)} %bitcast.me_ref, ...), custom_call_target="tpu_custom_call" | custom-call | tf_op jit(solution)/shard_map/project/pallas_call | solution.py:392
  2.5 5.1 %collective-permute-start = (bf16[16,16,128]{2,1,0:T(8,128)(2,1)S(1)}, bf16[16,16,128]{2,1,0:T(8,128)(2,1)S(1)}, u32[]{:S(2)}, u32[]{:S(2)}) collective-permute-start(bf16[16,16,128]{2,1,0:T(8,128)(2,1)S(1)} %get-tuple-element.48), channel_id=1, source_target_pairs={{0,12},{1,13},{2,14},{3,15},{4,8},{5,9},{6,10},{7,11},{8,4},{9,5},... | collective-permute-start | bytes 196616 | tf_op jit(solution)/shard_map/ppermute | solution.py:425
  7.7 1.5 %collective-permute-start.1 = (bf16[16,16,128]{2,1,0:T(8,128)(2,1)S(1)}, bf16[16,16,128]{2,1,0:T(8,128)(2,1)S(1)}, u32[]{:S(2)}, u32[]{:S(2)}) collective-permute-start(bf16[16,16,128]{2,1,0:T(8,128)(2,1)S(1)} %get-tuple-element.49), channel_id=1, source_target_pairs={{0,2},{1,3},{2,0},{3,1},{4,6},{5,7},{6,4},{7,5},{8,10},{9,11},{10,... | collective-permute-start | bytes 196616 | tf_op jit(solution)/shard_map/ppermute | solution.py:425
  9.2 4.3 %collective-permute-start.4 = (bf16[16,16,128]{2,1,0:T(8,128)(2,1)S(1)}, bf16[16,16,128]{2,1,0:T(8,128)(2,1)S(1)}, u32[]{:S(2)}, u32[]{:S(2)}) collective-permute-start(bf16[16,16,128]{2,1,0:T(8,128)(2,1)S(1)} %get-tuple-element.52), channel_id=1, source_target_pairs={{0,8},{1,9},{2,10},{3,11},{4,12},{5,13},{6,14},{7,15},{8,0},{9,1},... | collective-permute-start | bytes 196616 | tf_op jit(solution)/shard_map/ppermute | solution.py:425
  13.5 1.0 %collective-permute-start.5 = (bf16[16,16,128]{2,1,0:T(8,128)(2,1)S(1)}, bf16[16,16,128]{2,1,0:T(8,128)(2,1)S(1)}, u32[]{:S(2)}, u32[]{:S(2)}) collective-permute-start(bf16[16,16,128]{2,1,0:T(8,128)(2,1)S(1)} %get-tuple-element.53), channel_id=1, source_target_pairs={{0,6},{1,7},{2,4},{3,5},{4,2},{5,3},{6,0},{7,1},{8,14},{9,15},{10,... | collective-permute-start | bytes 196616 | tf_op jit(solution)/shard_map/ppermute | solution.py:425
  14.5 1.3 %collective-permute-start.6 = (bf16[16,16,128]{2,1,0:T(8,128)(2,1)S(1)}, bf16[16,16,128]{2,1,0:T(8,128)(2,1)S(1)}, u32[]{:S(2)}, u32[]{:S(2)}) collective-permute-start(bf16[16,16,128]{2,1,0:T(8,128)(2,1)S(1)} %get-tuple-element.54), channel_id=1, source_target_pairs={{0,10},{1,11},{2,8},{3,9},{4,14},{5,15},{6,12},{7,13},{8,2},{9,3},... | collective-permute-start | bytes 196616 | tf_op jit(solution)/shard_map/ppermute | solution.py:425
  15.8 1.6 %prepare.1 = (f32[1,64,2048]{2,1,0:T(8,128)S(1)}, bf16[1,64,2048]{2,1,0:T(8,128)(2,1)S(1)}, f32[64,16,128]{2,1,0:T(8,128)S(1)}, bf16[64,320]{1,0:T(8,128)(2,1)S(1)}) custom-call(bf16[16,64,128]{2,1,0:T(8,128)(2,1)} %bitcast.13, bf16[1,64,2048]{2,1,0:T(8,128)(2,1)S(1)} %get-tuple-element.47.zn_ref, bf16[4,64,64]{2,1,0:T(8,128)(2,1)} %w_ref.3, ...), custom_call_target="tpu_custom_call" | custom-call | tf_op jit(solution)/shard_map/prepare/pallas_call | solution.py:392
  17.4 1.9 %collective-permute-done.5.refs_5_ = bf16[16,16,128]{2,1,0:T(8,128)(2,1)S(1)} collective-permute-done((bf16[16,16,128]{2,1,0:T(8,128)(2,1)S(1)}, bf16[16,16,128]{2,1,0:T(8,128)(2,1)S(1)}, u32[]{:S(2)}, u32[]{:S(2)}) %collective-permute-start.5) | collective-permute-done | bytes 65568 | tf_op jit(solution)/shard_map/ppermute | solution.py:425
  19.4 1.2 %collective-permute-done.6.refs_6_ = bf16[16,16,128]{2,1,0:T(8,128)(2,1)S(1)} collective-permute-done((bf16[16,16,128]{2,1,0:T(8,128)(2,1)S(1)}, bf16[16,16,128]{2,1,0:T(8,128)(2,1)S(1)}, u32[]{:S(2)}, u32[]{:S(2)}) %collective-permute-start.6) | collective-permute-done | bytes 65568 | tf_op jit(solution)/shard_map/ppermute | solution.py:425
  20.7 1.5 %collective-permute-done.7.refs_9_ = bf16[8,8,16,128]{3,2,1,0:T(8,128)(2,1)S(1)} collective-permute-done((bf16[8,8,16,128]{3,2,1,0:T(8,128)(2,1)S(1)}, bf16[8,8,16,128]{3,2,1,0:T(8,128)(2,1)S(1)}, u32[]{:S(2)}, u32[]{:S(2)}) %collective-permute-start.7) | collective-permute-done | bytes 262176 | tf_op jit(solution)/shard_map/ppermute | solution.py:465
  22.2 0.5 mixed.1
  22.7 12.4 %all_to_all.15 = bf16[8,8,16,128]{3,2,1,0:T(8,128)(2,1)S(1)} all-to-all(bf16[8,8,16,128]{3,2,1,0:T(8,128)(2,1)S(1)} %get-tuple-element.57), channel_id=1, replica_groups={{0,2,4,6,8,10,12,14},{1,3,5,7,9,11,13,15},{16,18,20,22,24,26,28,30},{17..., dimensions={0} | all-to-all | bytes 524288 | tf_op jit(solution)/shard_map/all_to_all | solution.py:359
  35.1 0.9 %middle.1 = (bf16[64,16,128]{2,1,0:T(8,128)(2,1)S(1)}, f32[2,16,128]{2,1,0:T(8,128)S(1)}) custom-call(f32[2,64]{1,0:T(2,128)S(1)} %copy-done.1, f32[64,16,128]{2,1,0:T(8,128)S(1)} %get-tuple-element.58.dout_ref, bf16[64,16,128]{2,1,0:T(8,128)(2,1)S(1)} %bitcast.9), custom_call_target="tpu_custom_call" | custom-call | tf_op jit(solution)/shard_map/middle/pallas_call | solution.py:392
  36.0 12.0 %all_to_all.16.dmix_ref = bf16[8,8,16,128]{3,2,1,0:T(8,128)(2,1)S(1)} all-to-all(bf16[8,8,16,128]{3,2,1,0:T(8,128)(2,1)S(1)} %bitcast.11), channel_id=1, replica_groups={{0,2,4,6,8,10,12,14},{1,3,5,7,9,11,13,15},{16,18,20,22,24,26,28,30},{17..., dimensions={0} | all-to-all | bytes 524288 | tf_op jit(solution)/shard_map/all_to_all | solution.py:359
  48.0 0.6 triangle_back.1
  48.6 1.5 %collective-permute-done.8.got_ref = bf16[8,8,16,128]{3,2,1,0:T(8,128)(2,1)S(1)} collective-permute-done((bf16[8,8,16,128]{3,2,1,0:T(8,128)(2,1)S(1)}, bf16[8,8,16,128]{3,2,1,0:T(8,128)(2,1)S(1)}, u32[]{:S(2)}, u32[]{:S(2)}) %collective-permute-start.8) | collective-permute-done | bytes 262176 | tf_op jit(solution)/shard_map/ppermute | solution.py:522
  50.2 1.2 %collective-permute-start.9 = (bf16[16,16,128]{2,1,0:T(8,128)(2,1)S(1)}, bf16[16,16,128]{2,1,0:T(8,128)(2,1)S(1)}, u32[]{:S(2)}, u32[]{:S(2)}) collective-permute-start(bf16[16,16,128]{2,1,0:T(8,128)(2,1)S(1)} %get-tuple-element.69), channel_id=1, source_target_pairs={{0,12},{1,13},{2,14},{3,15},{4,8},{5,9},{6,10},{7,11},{8,4},{9,5},... | collective-permute-start | bytes 196616 | tf_op jit(solution)/shard_map/ppermute | solution.py:425
  51.4 1.7 %collective-permute-start.10 = (bf16[16,16,128]{2,1,0:T(8,128)(2,1)S(1)}, bf16[16,16,128]{2,1,0:T(8,128)(2,1)S(1)}, u32[]{:S(2)}, u32[]{:S(2)}) collective-permute-start(bf16[16,16,128]{2,1,0:T(8,128)(2,1)S(1)} %get-tuple-element.70), channel_id=1, source_target_pairs={{0,2},{1,3},{2,0},{3,1},{4,6},{5,7},{6,4},{7,5},{8,10},{9,11},{10,... | collective-permute-start | bytes 196616 | tf_op jit(solution)/shard_map/ppermute | solution.py:425
  53.1 2.4 %collective-permute-start.11 = (bf16[16,16,128]{2,1,0:T(8,128)(2,1)S(1)}, bf16[16,16,128]{2,1,0:T(8,128)(2,1)S(1)}, u32[]{:S(2)}, u32[]{:S(2)}) collective-permute-start(bf16[16,16,128]{2,1,0:T(8,128)(2,1)S(1)} %get-tuple-element.71), channel_id=1, source_target_pairs={{0,14},{1,15},{2,12},{3,13},{4,10},{5,11},{6,8},{7,9},{8,6},{9,7},... | collective-permute-start | bytes 196616 | tf_op jit(solution)/shard_map/ppermute | solution.py:425
  55.5 1.7 %collective-permute-start.13 = (bf16[16,16,128]{2,1,0:T(8,128)(2,1)S(1)}, bf16[16,16,128]{2,1,0:T(8,128)(2,1)S(1)}, u32[]{:S(2)}, u32[]{:S(2)}) collective-permute-start(bf16[16,16,128]{2,1,0:T(8,128)(2,1)S(1)} %get-tuple-element.73), channel_id=1, source_target_pairs={{0,8},{1,9},{2,10},{3,11},{4,12},{5,13},{6,14},{7,15},{8,0},{9,1},... | collective-permute-start | bytes 196616 | tf_op jit(solution)/shard_map/ppermute | solution.py:425
  57.2 1.2 %collective-permute-start.14 = (bf16[16,16,128]{2,1,0:T(8,128)(2,1)S(1)}, bf16[16,16,128]{2,1,0:T(8,128)(2,1)S(1)}, u32[]{:S(2)}, u32[]{:S(2)}) collective-permute-start(bf16[16,16,128]{2,1,0:T(8,128)(2,1)S(1)} %get-tuple-element.74), channel_id=1, source_target_pairs={{0,6},{1,7},{2,4},{3,5},{4,2},{5,3},{6,0},{7,1},{8,14},{9,15},{10,... | collective-permute-start | bytes 196616 | tf_op jit(solution)/shard_map/ppermute | solution.py:425
  58.5 2.9 %collective-permute-start.15 = (bf16[16,16,128]{2,1,0:T(8,128)(2,1)S(1)}, bf16[16,16,128]{2,1,0:T(8,128)(2,1)S(1)}, u32[]{:S(2)}, u32[]{:S(2)}) collective-permute-start(bf16[16,16,128]{2,1,0:T(8,128)(2,1)S(1)} %get-tuple-element.75), channel_id=1, source_target_pairs={{0,10},{1,11},{2,8},{3,9},{4,14},{5,15},{6,12},{7,13},{8,2},{9,3},... | collective-permute-start | bytes 196616 | tf_op jit(solution)/shard_map/ppermute | solution.py:425
  61.4 1.3 %update.1 = (bf16[1,64,2048]{2,1,0:T(8,128)(2,1)S(1)}, f32[72,128]{1,0:T(8,128)S(1)}) custom-call(f32[2,64]{1,0:T(2,128)S(1)} %copy-done.1, bf16[64,16,128]{2,1,0:T(8,128)(2,1)S(1)} %bitcast.10, f32[64,16,128]{2,1,0:T(8,128)S(1)} %get-tuple-element.58.dout_ref, f32[2,16,128]{2,1,0:T(8,128)S(1)} %get-tuple-element.59.stats_ref, ...), custom_call_target="tpu_custom_call" | custom-call | tf_op jit(solution)/shard_map/update/pallas_call | solution.py:392
  62.8 0.6 collective-permute-done.13.refs_4_
  63.3 1.7 %collective-permute-done.14.refs_5_ = bf16[16,16,128]{2,1,0:T(8,128)(2,1)S(1)} collective-permute-done((bf16[16,16,128]{2,1,0:T(8,128)(2,1)S(1)}, bf16[16,16,128]{2,1,0:T(8,128)(2,1)S(1)}, u32[]{:S(2)}, u32[]{:S(2)}) %collective-permute-start.14) | collective-permute-done | bytes 65568 | tf_op jit(solution)/shard_map/ppermute | solution.py:425
  65.0 0.8 %gating_back.1 = (bf16[1,256,2048]{2,1,0:T(8,128)(2,1)S(1)}, f32[96,128]{1,0:T(8,128)S(1)}, f32[96,128]{1,0:T(8,128)S(1)}) custom-call(s32[1]{0:T(128)} %bitcast.me_ref, f32[1,256,2048]{2,1,0:T(8,128)S(1)} %get-tuple-element.46.fac_ref, bf16[1,64,2048]{2,1,0:T(8,128)(2,1)S(1)} %get-tuple-element.47.zn_ref, f32[72,128]{1,0:T(8,128)S(1)} %get-tuple-element.62.grads_ref, ...), custom_call_target="tpu_custom_call" | custom-call | tf_op jit(solution)/shard_map/gating_back/pallas_call | solution.py:392
  65.9 0.5 input_grad.1
  66.4 0.7 collective-permute-done.16.got_ref
  67.2 12.0 %all_to_all.17.pack_ref = bf16[8,104,128]{2,1,0:T(8,128)(2,1)S(1)} all-to-all(bf16[8,104,128]{2,1,0:T(8,128)(2,1)S(1)} %combine.1), channel_id=1, replica_groups={{0,2,4,6,8,10,12,14},{1,3,5,7,9,11,13,15},{16,18,20,22,24,26,28,30},{17..., dimensions={0} | all-to-all | bytes 425984 | tf_op jit(solution)/shard_map/all_to_all | solution.py:359
  79.3 1.0 %pair_grad.1 = bf16[16,64,128]{2,1,0:T(8,128)(2,1)} custom-call(f32[104,128]{1,0:T(8,128)S(1)} %total.1.after_ref.mine_ref, f32[1,64,2048]{2,1,0:T(8,128)S(1)} %get-tuple-element.83.dzn_ref, f32[1,64,2048]{2,1,0:T(8,128)S(1)} %get-tuple-element.81.normed_ref, f32[1,1,2048]{2,1,0:T(1,128)S(1)} %get-tuple-element.84.rstd_ref, f32[2,64]{1,0:T(2,128)S(1)} %copy-done.1), custom_call_target="tpu_custom_call" | custom-call | tf_op jit(solution)/shard_map/pair_grad/pallas_call | solution.py:392
  80.3 0.2 collective-permute-done.17.got_ref
  80.6 0.8 unpack.1
  (25 shorter events, 0.5 us)
Async XLA Ops:
  0.6 34.5 %copy-start.1 = (f32[2,64]{1,0:T(2,128)S(1)}, f32[2,64]{1,0:T(2,128)}, u32[]{:S(2)}) copy-start(f32[2,64]{1,0:T(2,128)} %gains_ref.7) | copy-start | bytes 1540
  2.5 11.0 %collective-permute-start = (bf16[16,16,128]{2,1,0:T(8,128)(2,1)S(1)}, bf16[16,16,128]{2,1,0:T(8,128)(2,1)S(1)}, u32[]{:S(2)}, u32[]{:S(2)}) collective-permute-start(bf16[16,16,128]{2,1,0:T(8,128)(2,1)S(1)} %get-tuple-element.48), channel_id=1, source_target_pairs={{0,12},{1,13},{2,14},{3,15},{4,8},{5,9},{6,10},{7,11},{8,4},{9,5},... | collective-permute-start | bytes 196616 | tf_op jit(solution)/shard_map/ppermute | solution.py:425
  7.7 6.8 %collective-permute-start.1 = (bf16[16,16,128]{2,1,0:T(8,128)(2,1)S(1)}, bf16[16,16,128]{2,1,0:T(8,128)(2,1)S(1)}, u32[]{:S(2)}, u32[]{:S(2)}) collective-permute-start(bf16[16,16,128]{2,1,0:T(8,128)(2,1)S(1)} %get-tuple-element.49), channel_id=1, source_target_pairs={{0,2},{1,3},{2,0},{3,1},{4,6},{5,7},{6,4},{7,5},{8,10},{9,11},{10,... | collective-permute-start | bytes 196616 | tf_op jit(solution)/shard_map/ppermute | solution.py:425
  9.2 8.2 %collective-permute-start.2 = (bf16[16,16,128]{2,1,0:T(8,128)(2,1)S(1)}, bf16[16,16,128]{2,1,0:T(8,128)(2,1)S(1)}, u32[]{:S(2)}, u32[]{:S(2)}) collective-permute-start(bf16[16,16,128]{2,1,0:T(8,128)(2,1)S(1)} %get-tuple-element.50), channel_id=1, source_target_pairs={{0,14},{1,15},{2,12},{3,13},{4,10},{5,11},{6,8},{7,9},{8,6},{9,7},... | collective-permute-start | bytes 196616 | tf_op jit(solution)/shard_map/ppermute | solution.py:425
  9.2 8.2 %collective-permute-start.3 = (bf16[16,16,128]{2,1,0:T(8,128)(2,1)S(1)}, bf16[16,16,128]{2,1,0:T(8,128)(2,1)S(1)}, u32[]{:S(2)}, u32[]{:S(2)}) collective-permute-start(bf16[16,16,128]{2,1,0:T(8,128)(2,1)S(1)} %get-tuple-element.51), channel_id=1, source_target_pairs={{0,4},{1,5},{2,6},{3,7},{4,0},{5,1},{6,2},{7,3},{8,12},{9,13},{10,... | collective-permute-start | bytes 196616 | tf_op jit(solution)/shard_map/ppermute | solution.py:425
  9.2 8.2 %collective-permute-start.4 = (bf16[16,16,128]{2,1,0:T(8,128)(2,1)S(1)}, bf16[16,16,128]{2,1,0:T(8,128)(2,1)S(1)}, u32[]{:S(2)}, u32[]{:S(2)}) collective-permute-start(bf16[16,16,128]{2,1,0:T(8,128)(2,1)S(1)} %get-tuple-element.52), channel_id=1, source_target_pairs={{0,8},{1,9},{2,10},{3,11},{4,12},{5,13},{6,14},{7,15},{8,0},{9,1},... | collective-permute-start | bytes 196616 | tf_op jit(solution)/shard_map/ppermute | solution.py:425
  13.5 5.8 %collective-permute-start.5 = (bf16[16,16,128]{2,1,0:T(8,128)(2,1)S(1)}, bf16[16,16,128]{2,1,0:T(8,128)(2,1)S(1)}, u32[]{:S(2)}, u32[]{:S(2)}) collective-permute-start(bf16[16,16,128]{2,1,0:T(8,128)(2,1)S(1)} %get-tuple-element.53), channel_id=1, source_target_pairs={{0,6},{1,7},{2,4},{3,5},{4,2},{5,3},{6,0},{7,1},{8,14},{9,15},{10,... | collective-permute-start | bytes 196616 | tf_op jit(solution)/shard_map/ppermute | solution.py:425
  14.5 6.1 %collective-permute-start.6 = (bf16[16,16,128]{2,1,0:T(8,128)(2,1)S(1)}, bf16[16,16,128]{2,1,0:T(8,128)(2,1)S(1)}, u32[]{:S(2)}, u32[]{:S(2)}) collective-permute-start(bf16[16,16,128]{2,1,0:T(8,128)(2,1)S(1)} %get-tuple-element.54), channel_id=1, source_target_pairs={{0,10},{1,11},{2,8},{3,9},{4,14},{5,15},{6,12},{7,13},{8,2},{9,3},... | collective-permute-start | bytes 196616 | tf_op jit(solution)/shard_map/ppermute | solution.py:425
  20.6 1.6 %collective-permute-start.7 = (bf16[8,8,16,128]{3,2,1,0:T(8,128)(2,1)S(1)}, bf16[8,8,16,128]{3,2,1,0:T(8,128)(2,1)S(1)}, u32[]{:S(2)}, u32[]{:S(2)}) collective-permute-start(bf16[8,8,16,128]{3,2,1,0:T(8,128)(2,1)S(1)} %collect.1.refs_8_), channel_id=1, source_target_pairs={{0,1},{1,0},{2,3},{3,2},{4,5},{5,4},{6,7},{7,6},{8,9},{9,8},{10,11... | collective-permute-start | bytes 786440 | tf_op jit(solution)/shard_map/ppermute | solution.py:465
  22.7 38.7 %copy-start = (bf16[2,64,64]{2,1,0:T(8,128)(2,1)S(1)}, bf16[2,64,64]{2,1,0:T(8,128)(2,1)}, u32[]{:S(2)}) copy-start(bf16[2,64,64]{2,1,0:T(8,128)(2,1)} %wo_ref.3) | copy-start | bytes 49156
  48.5 1.6 %collective-permute-start.8 = (bf16[8,8,16,128]{3,2,1,0:T(8,128)(2,1)S(1)}, bf16[8,8,16,128]{3,2,1,0:T(8,128)(2,1)S(1)}, u32[]{:S(2)}, u32[]{:S(2)}) collective-permute-start(bf16[8,8,16,128]{3,2,1,0:T(8,128)(2,1)S(1)} %get-tuple-element.68), channel_id=1, source_target_pairs={{0,1},{1,0},{2,3},{3,2},{4,5},{5,4},{6,7},{7,6},{8,9},{9,8},{10,11... | collective-permute-start | bytes 786440 | tf_op jit(solution)/shard_map/ppermute | solution.py:522
  50.2 7.1 %collective-permute-start.9 = (bf16[16,16,128]{2,1,0:T(8,128)(2,1)S(1)}, bf16[16,16,128]{2,1,0:T(8,128)(2,1)S(1)}, u32[]{:S(2)}, u32[]{:S(2)}) collective-permute-start(bf16[16,16,128]{2,1,0:T(8,128)(2,1)S(1)} %get-tuple-element.69), channel_id=1, source_target_pairs={{0,12},{1,13},{2,14},{3,15},{4,8},{5,9},{6,10},{7,11},{8,4},{9,5},... | collective-permute-start | bytes 196616 | tf_op jit(solution)/shard_map/ppermute | solution.py:425
  51.4 7.1 %collective-permute-start.10 = (bf16[16,16,128]{2,1,0:T(8,128)(2,1)S(1)}, bf16[16,16,128]{2,1,0:T(8,128)(2,1)S(1)}, u32[]{:S(2)}, u32[]{:S(2)}) collective-permute-start(bf16[16,16,128]{2,1,0:T(8,128)(2,1)S(1)} %get-tuple-element.70), channel_id=1, source_target_pairs={{0,2},{1,3},{2,0},{3,1},{4,6},{5,7},{6,4},{7,5},{8,10},{9,11},{10,... | collective-permute-start | bytes 196616 | tf_op jit(solution)/shard_map/ppermute | solution.py:425
  53.1 9.6 %collective-permute-start.11 = (bf16[16,16,128]{2,1,0:T(8,128)(2,1)S(1)}, bf16[16,16,128]{2,1,0:T(8,128)(2,1)S(1)}, u32[]{:S(2)}, u32[]{:S(2)}) collective-permute-start(bf16[16,16,128]{2,1,0:T(8,128)(2,1)S(1)} %get-tuple-element.71), channel_id=1, source_target_pairs={{0,14},{1,15},{2,12},{3,13},{4,10},{5,11},{6,8},{7,9},{8,6},{9,7},... | collective-permute-start | bytes 196616 | tf_op jit(solution)/shard_map/ppermute | solution.py:425
  55.5 7.2 %collective-permute-start.12 = (bf16[16,16,128]{2,1,0:T(8,128)(2,1)S(1)}, bf16[16,16,128]{2,1,0:T(8,128)(2,1)S(1)}, u32[]{:S(2)}, u32[]{:S(2)}) collective-permute-start(bf16[16,16,128]{2,1,0:T(8,128)(2,1)S(1)} %get-tuple-element.72), channel_id=1, source_target_pairs={{0,4},{1,5},{2,6},{3,7},{4,0},{5,1},{6,2},{7,3},{8,12},{9,13},{10,... | collective-permute-start | bytes 196616 | tf_op jit(solution)/shard_map/ppermute | solution.py:425
  55.5 7.8 %collective-permute-start.13 = (bf16[16,16,128]{2,1,0:T(8,128)(2,1)S(1)}, bf16[16,16,128]{2,1,0:T(8,128)(2,1)S(1)}, u32[]{:S(2)}, u32[]{:S(2)}) collective-permute-start(bf16[16,16,128]{2,1,0:T(8,128)(2,1)S(1)} %get-tuple-element.73), channel_id=1, source_target_pairs={{0,8},{1,9},{2,10},{3,11},{4,12},{5,13},{6,14},{7,15},{8,0},{9,1},... | collective-permute-start | bytes 196616 | tf_op jit(solution)/shard_map/ppermute | solution.py:425
  57.2 7.8 %collective-permute-start.14 = (bf16[16,16,128]{2,1,0:T(8,128)(2,1)S(1)}, bf16[16,16,128]{2,1,0:T(8,128)(2,1)S(1)}, u32[]{:S(2)}, u32[]{:S(2)}) collective-permute-start(bf16[16,16,128]{2,1,0:T(8,128)(2,1)S(1)} %get-tuple-element.74), channel_id=1, source_target_pairs={{0,6},{1,7},{2,4},{3,5},{4,2},{5,3},{6,0},{7,1},{8,14},{9,15},{10,... | collective-permute-start | bytes 196616 | tf_op jit(solution)/shard_map/ppermute | solution.py:425
  58.5 6.5 %collective-permute-start.15 = (bf16[16,16,128]{2,1,0:T(8,128)(2,1)S(1)}, bf16[16,16,128]{2,1,0:T(8,128)(2,1)S(1)}, u32[]{:S(2)}, u32[]{:S(2)}) collective-permute-start(bf16[16,16,128]{2,1,0:T(8,128)(2,1)S(1)} %get-tuple-element.75), channel_id=1, source_target_pairs={{0,10},{1,11},{2,8},{3,9},{4,14},{5,15},{6,12},{7,13},{8,2},{9,3},... | collective-permute-start | bytes 196616 | tf_op jit(solution)/shard_map/ppermute | solution.py:425
  65.9 1.3 %collective-permute-start.16 = (f32[96,128]{1,0:T(8,128)S(1)}, f32[96,128]{1,0:T(8,128)S(1)}, u32[]{:S(2)}, u32[]{:S(2)}) collective-permute-start(f32[96,128]{1,0:T(8,128)S(1)} %get-tuple-element.78), channel_id=1, source_target_pairs={{0,1},{1,0},{2,3},{3,2},{4,5},{5,4},{6,7},{7,6},{8,9},{9,8},{10,11... | collective-permute-start | bytes 147464 | tf_op jit(solution)/shard_map/ppermute | solution.py:555
  79.3 1.3 %collective-permute-start.17 = (f32[104,128]{1,0:T(8,128)S(1)}, f32[104,128]{1,0:T(8,128)S(1)}, u32[]{:S(2)}, u32[]{:S(2)}) collective-permute-start(f32[104,128]{1,0:T(8,128)S(1)} %total.1.after_ref.mine_ref), channel_id=1, source_target_pairs={{0,1},{1,0},{2,3},{3,2},{4,5},{5,4},{6,7},{7,6},{8,9},{9,8},{10,11... | collective-permute-start | bytes 159752 | tf_op jit(solution)/shard_map/ppermute | solution.py:577
